TPU v7x, 32 devices: a whole 2x2x4 slice. The times are simulated.
32 devices in a mesh: fields: 2 (over y), rows: 4 (over z), cols: 2 (over x), sub: 2 (over core).
Axes of the slice: x: 2, y: 2, z: 4, core: 2. Of those that a mesh axis runs over, the one named last changes fastest.
Arguments:
- convergence: bfloat16 [32, 32, 16, 512], P(('fields', 'rows'), 'cols'), parts along dimension 0, may hold values from -6 to 6
- block_level: int32 [32, 32], P(('fields', 'rows'), 'cols'), parts along dimension 0, may hold values from 0 to 1
- near_codes: int32 [32, 32, 8], P(('fields', 'rows'), 'cols', 'sub'), parts along dimension 0, may hold values from 0 to 24, as said below
- far_rows: int32 [32, 32, 4], P(('fields', 'rows'), 'cols', 'sub'), parts along dimension 0, may hold values from 0 to 15, as said below
- near_factor: bfloat16 [512, 4096], P(None, 'sub'), may hold values from -0.09375 to 0.09375
- far_factor: bfloat16 [512, 2048], P(None, 'sub'), may hold values from -0.125 to 0.125
Outputs:
- whitened: bfloat16 [32, 32, 16, 512], P(('fields', 'rows'), 'cols', 'sub'), parts along dimension 0
There are 2 independent parts, one for each index of `fields`. A program takes and returns all parts, laid end to end along the dimension named above; an argument that names none is the same for every part. Nothing has to cross between parts.
Inputs may be any that keep to these rules, and one draw needn't show every extreme that they name: `near_codes`: the 8 codes of a block are different from one another and never 12 (the block itself). `far_rows`: an entry never names a block row held by the same index of rows as the block. Among the 128 entries that one index of rows, cols and sub holds (slots 0 to 1 or 2 to 3), each other index of rows is named at most 64 times through its block rows, and one is named exactly 64 times.
All inputs are finite; a program needn't handle non-finite values.
Results may differ from a plain program's by a relative error of at most 0.001.
Values may be sent and summed in bfloat16 or wider, within the bound.
No kernel may reach another device: no remote copies, remote signals or barrier semaphores. Data moves between devices by JAX's collectives and lax.ppermute only.
A program may use at most 64 MiB of HBM per device.

v0:
```python
import jax
import jax.numpy as jnp
from jax import lax
from jax.sharding import PartitionSpec as P


def padded(array, sides, width):
    for axis, dim in sides:
        count, length = (lax.axis_size(axis), array.shape[dim])
        up = [(i, (i + 1) % count) for i in range(count - 1)]
        down = [(j, i) for i, j in up]
        last = lax.slice_in_dim(array, length - width, length, axis=dim)
        first = lax.slice_in_dim(array, 0, width, axis=dim)
        before = lax.ppermute(last, axis, up)
        after = lax.ppermute(first, axis, down)
        array = jnp.concatenate([before, array, after], axis=dim)
    return array


def on_device(convergence, block_level, near_codes, far_rows, near_factor, far_factor):
    tile_rows, tile_cols, samples, pixels = convergence.shape
    block_count = tile_rows * tile_cols
    sub_index = lax.axis_index("sub")
    half_count = samples // 2
    extended = padded(convergence, (("rows", 0), ("cols", 1)), 2)
    flat_ext = extended.reshape((tile_rows + 4) * (tile_cols + 4), samples, pixels)
    row_pos = jnp.arange(tile_rows, dtype=jnp.int32)[:, None, None]
    col_pos = jnp.arange(tile_cols, dtype=jnp.int32)[None, :, None]
    near_index = (row_pos + near_codes // 5) * (tile_cols + 4) + col_pos + near_codes % 5
    near_slots = near_codes.shape[2]
    near_blocks = jnp.take(flat_ext, near_index.reshape(-1), axis=0).reshape(
        block_count, near_slots, samples, pixels
    )
    near_terms = lax.dot_general(
        near_blocks,
        near_factor.reshape(pixels, near_slots, pixels),
        (((1, 3), (1, 2)), ((), ())),
        preferred_element_type=jnp.float32,
    )
    requests = far_rows.reshape(-1)
    far_slots = far_rows.shape[2]
    flat_tile = convergence.reshape(block_count, samples, pixels)
    request_cols = jnp.arange(requests.shape[0], dtype=jnp.int32) // far_slots % tile_cols
    empty = jnp.zeros((requests.shape[0], samples, pixels), jnp.bfloat16)
    piece = lax.all_gather(convergence, "rows", axis=0, tiled=True)
    start = jnp.int32(0)
    piece_rows = piece.shape[0]
    flat_piece = piece.reshape(piece_rows * tile_cols, samples, pixels)
    inside = (requests >= start) & (requests < start + piece_rows)
    local = jnp.clip(requests * tile_cols + request_cols, 0, piece_rows * tile_cols - 1)
    found = jnp.take(flat_piece, local, axis=0)
    far_flat = jnp.where(inside[:, None, None], found, empty)
    far_blocks = far_flat.reshape(block_count, far_slots, samples, pixels)
    far_terms = lax.dot_general(
        far_blocks,
        far_factor.reshape(pixels, far_slots, pixels),
        (((1, 3), (1, 2)), ((), ())),
        preferred_element_type=jnp.float32,
    )
    level_flat = block_level.reshape(block_count)
    partial_value = jnp.where(level_flat[:, None, None] == 1, near_terms, far_terms)
    mean_half = lax.psum_scatter(partial_value, "sub", scatter_dimension=1, tiled=True)
    own_half = lax.dynamic_slice_in_dim(flat_tile, sub_index * half_count, half_count, 1)
    whitened = (own_half.astype(jnp.float32) - mean_half).astype(jnp.bfloat16)
    return whitened.reshape(tile_rows, tile_cols, half_count, pixels)


def solution(mesh):
    placed = (
        P(("fields", "rows"), "cols", None, None),
        P(("fields", "rows"), "cols"),
        P(("fields", "rows"), "cols", "sub"),
        P(("fields", "rows"), "cols", "sub"),
        P(None, "sub"),
        P(None, "sub"),
    )
    return jax.shard_map(
        on_device,
        mesh=mesh,
        in_specs=placed,
        out_specs=P(("fields", "rows"), "cols", "sub", None),
        check_vma=False,
    )
```

profile of v0, /device:TPU:0, one launch (start us, length us, event | category | flops | bytes accessed | tf_op | source)
XLA Modules:
  0.0 126.5 jit_solution(18052864852191408466)
XLA Ops:
  6.5 0.0 copy-start
  6.5 0.0 copy-start.4
  6.5 0.0 copy-start.5
  6.5 0.0 copy-start.6
  6.5 0.0 all-gather.2.cloned.1.call-start
  6.6 0.7 all-gather.2.cloned.1.call-update
  7.3 0.0 reduce-scatter.2.cloned.1.call-start
  7.3 1.3 %fusion.15 = (bf16[2,16,16,512]{3,2,1,0:T(8,128)(2,1)S(1)}, bf16[2,16,16,512]{3,2,1,0:T(8,128)(2,1)S(1)}) fusion(bf16[4,16,16,512]{3,2,1,0:T(8,128)(2,1)} %param.6), kind=kLoop, calls=%fused_computation.56 | loop fusion | bytes 2097152 | tf_op jit(solution)/shard_map/slice | solution.py:13
  8.6 1.3 %collective-permute-start.1 = (bf16[2,16,16,512]{3,2,1,0:T(8,128)(2,1)S(1)}, bf16[2,16,16,512]{3,2,1,0:T(8,128)(2,1)S(1)}, u32[]{:S(2)}, u32[]{:S(2)}) collective-permute-start(bf16[2,16,16,512]{3,2,1,0:T(8,128)(2,1)S(1)} %get-tuple-element.7), channel_id=1, source_target_pairs={{4,0},{8,4},{12,8},{5,1},{9,5},{13,9},{6,2},{10,6},{14,10},{7,3},{... | collective-permute-start | bytes 1572872 | tf_op jit(solution)/shard_map/ppermute | solution.py:15
  9.9 5.6 %collective-permute-start = (bf16[2,16,16,512]{3,2,1,0:T(8,128)(2,1)S(1)}, bf16[2,16,16,512]{3,2,1,0:T(8,128)(2,1)S(1)}, u32[]{:S(2)}, u32[]{:S(2)}) collective-permute-start(bf16[2,16,16,512]{3,2,1,0:T(8,128)(2,1)S(1)} %get-tuple-element.8), channel_id=1, source_target_pairs={{0,4},{4,8},{8,12},{1,5},{5,9},{9,13},{2,6},{6,10},{10,14},{3,7},{... | collective-permute-start | bytes 1572872 | tf_op jit(solution)/shard_map/ppermute | solution.py:14
  15.5 0.0 copy-done.4
  15.5 0.1 copy.23
  15.6 0.1 mul.32
  15.8 0.1 mul.31
  15.9 0.0 copy-done.5
  15.9 0.1 copy.19
  16.0 0.1 reshape.243
  16.2 0.0 copy-done.6
  16.2 17.5 %collective-permute-done = bf16[2,16,16,512]{3,2,1,0:T(8,128)(2,1)S(1)} collective-permute-done((bf16[2,16,16,512]{3,2,1,0:T(8,128)(2,1)S(1)}, bf16[2,16,16,512]{3,2,1,0:T(8,128)(2,1)S(1)}, u32[]{:S(2)}, u32[]{:S(2)}) %collective-permute-start) | collective-permute-done | bytes 524320 | tf_op jit(solution)/shard_map/ppermute | solution.py:14
  33.8 0.0 copy-done
  33.8 0.1 constant_dynamic-update-slice_fusion.1
  33.9 0.0 collective-permute-done.1
  34.0 0.0 copy-start.2
  34.0 1.4 %copy-done.2 = bf16[8,16,16,512]{3,2,1,0:T(8,128)(2,1)} copy-done((bf16[8,16,16,512]{3,2,1,0:T(8,128)(2,1)}, bf16[8,16,16,512]{3,2,1,0:T(8,128)(2,1)S(1)}, u32[]{:S(2)}) %copy-start.2) | copy-done | bytes 2097176
  35.4 3.8 %collective-permute-start.2 = (bf16[8,2,16,512]{3,2,1,0:T(8,128)(2,1)S(1)}, bf16[8,2,16,512]{3,2,1,0:T(8,128)(2,1)S(1)}, u32[]{:S(2)}, u32[]{:S(2)}) collective-permute-start(bf16[8,2,16,512]{3,2,1,0:T(8,128)(2,1)S(1)} %get-tuple-element.5), channel_id=1, source_target_pairs={{0,2},{1,3},{4,6},{5,7},{8,10},{9,11},{12,14},{13,15},{16,18},{17,... | collective-permute-start | bytes 786440 | tf_op jit(solution)/shard_map/ppermute | solution.py:14
  39.2 1.3 %collective-permute-start.3 = (bf16[8,2,16,512]{3,2,1,0:T(8,128)(2,1)S(1)}, bf16[8,2,16,512]{3,2,1,0:T(8,128)(2,1)S(1)}, u32[]{:S(2)}, u32[]{:S(2)}) collective-permute-start(bf16[8,2,16,512]{3,2,1,0:T(8,128)(2,1)S(1)} %get-tuple-element.6), channel_id=1, source_target_pairs={{2,0},{3,1},{6,4},{7,5},{10,8},{11,9},{14,12},{15,13},{18,16},{19,... | collective-permute-start | bytes 786440 | tf_op jit(solution)/shard_map/ppermute | solution.py:15
  40.5 0.1 reshape.241
  40.6 0.1 eq.20
  40.7 0.1 copy.22
  40.8 0.2 and.85
  41.0 2.1 %collective-permute-done.2 = bf16[8,2,16,512]{3,2,1,0:T(8,128)(2,1)S(1)} collective-permute-done((bf16[8,2,16,512]{3,2,1,0:T(8,128)(2,1)S(1)}, bf16[8,2,16,512]{3,2,1,0:T(8,128)(2,1)S(1)}, u32[]{:S(2)}, u32[]{:S(2)}) %collective-permute-start.2) | collective-permute-done | bytes 262176 | tf_op jit(solution)/shard_map/ppermute | solution.py:14
  43.1 4.4 %collective-permute-done.3 = bf16[8,2,16,512]{3,2,1,0:T(8,128)(2,1)S(1)} collective-permute-done((bf16[8,2,16,512]{3,2,1,0:T(8,128)(2,1)S(1)}, bf16[8,2,16,512]{3,2,1,0:T(8,128)(2,1)S(1)}, u32[]{:S(2)}, u32[]{:S(2)}) %collective-permute-start.3) | collective-permute-done | bytes 262176 | tf_op jit(solution)/shard_map/ppermute | solution.py:15
  47.5 1.9 %pad_maximum_fusion = bf16[8,20,16,512]{3,2,1,0:T(8,128)(2,1)S(1)} fusion(bf16[8,2,16,512]{3,2,1,0:T(8,128)(2,1)S(1)} %collective-permute-done.3, bf16[8,16,16,512]{3,2,1,0:T(8,128)(2,1)} %copy-done.2, bf16[8,2,16,512]{3,2,1,0:T(8,128)(2,1)S(1)} %collective-permute-done.2), kind=kLoop, calls=%fused_computation.3 | loop fusion | flops 2621440 | bytes 5242880 | tf_op jit(solution)/shard_map/concatenate | solution.py:16
  49.4 2.8 %gather_fusion = bf16[256,16,512]{2,1,0:T(8,128)(2,1)} fusion(bf16[160,16,512]{2,1,0:T(8,128)(2,1)S(1)} %bitcast.35, s32[1024]{0:T(1024)S(1)} %pad_clamp_fusion.1), kind=kCustom, calls=%fused_computation | custom fusion | bytes 8389632 | tf_op jit(solution)/shard_map/jit(_take)/gather | solution.py:31
  52.2 4.1 %broadcast_select_fusion = bf16[256,16,512]{2,1,0:T(8,128)(2,1)} fusion(bf16[256,16,512]{2,1,0:T(8,128)(2,1)} %gather_fusion, pred[256]{0:T(512)(128)(4,1)S(1)} %compare_and_fusion.2), kind=kLoop, calls=%fused_computation.2 | loop fusion | flops 2097152 | bytes 8388864 | tf_op jit(solution)/shard_map/jit(_take)/select_n | solution.py:31
  56.3 38.5 %all-gather.2.cloned.1.call-done = bf16[16,16,16,512]{3,2,1,0:T(8,128)(2,1)} async-done(((bf16[4,16,16,512]{3,2,1,0:T(8,128)(2,1)}), bf16[16,16,16,512]{3,2,1,0:T(8,128)(2,1)}) %all-gather.2.cloned.1.call-update) | async-done | bytes 4194320 | tf_op jit(solution)/shard_map/all_gather | solution.py:45
  94.8 2.9 %gather_fusion.1 = bf16[128,16,512]{2,1,0:T(8,128)(2,1)S(1)} fusion(bf16[256,16,512]{2,1,0:T(8,128)(2,1)} %bitcast.39, s32[1024]{0:T(1024)S(1)} %pad_clamp_fusion), kind=kCustom, calls=%fused_computation.1 | custom fusion | bytes 4194816 | tf_op jit(solution)/shard_map/jit(_take)/gather | solution.py:51
  97.7 0.0 copy-start.8
  97.7 0.7 select_select_fusion
  98.5 0.5 copy-done.8
  99.0 1.3 %fusion.2 = f32[64,16,512,1]{2,1,3,0:T(8,128)S(1)} fusion(bf16[64,2,16,512]{3,2,1,0:T(8,128)(2,1)S(1)} %bitcast.38, bf16[64,2,8,512]{3,2,1,0:T(8,128)(2,1)S(1)} %bitcast.42), kind=kOutput, calls=%fused_computation.10 | convolution fusion | flops 1073741824 | bytes 5242880 | tf_op jit(solution)/shard_map/dot_general | solution.py:54
  100.2 0.9 copy-done.3
  101.1 0.7 copy-done.7
  101.8 3.7 %bitcast_select_fusion = f32[64,16,512]{2,1,0:T(8,128)} fusion(f32[64,16,512,1]{2,1,3,0:T(8,128)S(1)} %fusion.2, bf16[64,4,16,512]{3,2,1,0:T(8,128)(2,1)S(1)} %bitcast.37, bf16[64,4,8,512]{3,2,1,0:T(8,128)(2,1)S(1)} %bitcast.41, pred[64]{0:T(512)(128)(4,1)S(1)} %eq.20), kind=kOutput, calls=%fused_computation.7 | convolution fusion | flops 2148007936 | bytes 10485824 | tf_op jit(solution)/shard_map/dot_general | solution.py:34
  105.5 0.0 reduce-scatter.2.cloned.1.call-update
  105.5 11.9 %reduce-scatter.2.cloned.1.call-done = f32[64,8,512]{2,1,0:T(8,128)} async-done(((f32[64,16,512]{2,1,0:T(8,128)}), f32[64,8,512]{2,1,0:T(8,128)}) %reduce-scatter.2.cloned.1.call-update) | async-done | bytes 1048592 | tf_op jit(solution)/shard_map/reduce_scatter | solution.py:62
  117.4 0.0 copy-done.1
  117.4 2.2 %subtract_convert_fusion = bf16[64,8,512]{2,1,0:T(8,128)(2,1)} fusion(f32[64,8,512]{2,1,0:T(8,128)} %reduce-scatter.2.cloned.1.call-done, bf16[64,16,512]{2,1,0:T(8,128)(2,1)S(1)} %bitcast.36, s32[]{:T(128)S(6)} %select_n.123), kind=kLoop, calls=%fused_computation.12 | loop fusion | flops 786432 | bytes 2097156 | tf_op jit(solution)/shard_map/convert_element_type | solution.py:64
  (16 shorter events, 0.2 us)
Async XLA Ops:
  6.5 27.3 %copy-start = (bf16[4,16,16,512]{3,2,1,0:T(8,128)(2,1)S(1)}, bf16[4,16,16,512]{3,2,1,0:T(8,128)(2,1)}, u32[]{:S(2)}) copy-start(bf16[4,16,16,512]{3,2,1,0:T(8,128)(2,1)} %param.6) | copy-start | bytes 3145732
  6.5 9.0 %copy-start.4 = (s32[4,16,2]{1,2,0:T(2,128)S(1)}, s32[4,16,2]{1,2,0:T(2,128)}, u32[]{:S(2)}) copy-start(s32[4,16,2]{1,2,0:T(2,128)} %param.9) | copy-start | bytes 1540
  6.5 9.4 %copy-start.5 = (s32[4,16,4]{1,2,0:T(4,128)S(1)}, s32[4,16,4]{1,2,0:T(4,128)}, u32[]{:S(2)}) copy-start(s32[4,16,4]{1,2,0:T(4,128)} %param.8) | copy-start | bytes 3076
  6.5 9.6 %copy-start.6 = (s32[4,16]{1,0:T(4,128)S(1)}, s32[4,16]{1,0:T(4,128)}, u32[]{:S(2)}) copy-start(s32[4,16]{1,0:T(4,128)} %param.7) | copy-start | bytes 772
  6.5 88.3 %all-gather.2.cloned.1.call-start = ((), (), s32[]{:S(2)}) async-start(), calls=%async_computation.1 | async-start | bytes 5242880 | tf_op jit(solution)/shard_map/all_gather | solution.py:45
  7.3 110.1 %reduce-scatter.2.cloned.1.call-start = ((), (), s32[]{:S(2)}) async-start(), calls=%async_computation.2 | async-start | bytes 3145728 | tf_op jit(solution)/shard_map/reduce_scatter | solution.py:62
  8.6 25.3 %collective-permute-start.1 = (bf16[2,16,16,512]{3,2,1,0:T(8,128)(2,1)S(1)}, bf16[2,16,16,512]{3,2,1,0:T(8,128)(2,1)S(1)}, u32[]{:S(2)}, u32[]{:S(2)}) collective-permute-start(bf16[2,16,16,512]{3,2,1,0:T(8,128)(2,1)S(1)} %get-tuple-element.7), channel_id=1, source_target_pairs={{4,0},{8,4},{12,8},{5,1},{9,5},{13,9},{6,2},{10,6},{14,10},{7,3},{... | collective-permute-start | bytes 1572872 | tf_op jit(solution)/shard_map/ppermute | solution.py:15
  9.9 23.9 %collective-permute-start = (bf16[2,16,16,512]{3,2,1,0:T(8,128)(2,1)S(1)}, bf16[2,16,16,512]{3,2,1,0:T(8,128)(2,1)S(1)}, u32[]{:S(2)}, u32[]{:S(2)}) collective-permute-start(bf16[2,16,16,512]{3,2,1,0:T(8,128)(2,1)S(1)} %get-tuple-element.8), channel_id=1, source_target_pairs={{0,4},{4,8},{8,12},{1,5},{5,9},{9,13},{2,6},{6,10},{10,14},{3,7},{... | collective-permute-start | bytes 1572872 | tf_op jit(solution)/shard_map/ppermute | solution.py:14
  34.0 1.4 %copy-start.2 = (bf16[8,16,16,512]{3,2,1,0:T(8,128)(2,1)}, bf16[8,16,16,512]{3,2,1,0:T(8,128)(2,1)S(1)}, u32[]{:S(2)}) copy-start(bf16[8,16,16,512]{3,2,1,0:T(8,128)(2,1)S(1)} %constant_dynamic-update-slice_fusion) | copy-start | bytes 6291460
  35.4 7.7 %collective-permute-start.2 = (bf16[8,2,16,512]{3,2,1,0:T(8,128)(2,1)S(1)}, bf16[8,2,16,512]{3,2,1,0:T(8,128)(2,1)S(1)}, u32[]{:S(2)}, u32[]{:S(2)}) collective-permute-start(bf16[8,2,16,512]{3,2,1,0:T(8,128)(2,1)S(1)} %get-tuple-element.5), channel_id=1, source_target_pairs={{0,2},{1,3},{4,6},{5,7},{8,10},{9,11},{12,14},{13,15},{16,18},{17,... | collective-permute-start | bytes 786440 | tf_op jit(solution)/shard_map/ppermute | solution.py:14
  39.2 8.3 %collective-permute-start.3 = (bf16[8,2,16,512]{3,2,1,0:T(8,128)(2,1)S(1)}, bf16[8,2,16,512]{3,2,1,0:T(8,128)(2,1)S(1)}, u32[]{:S(2)}, u32[]{:S(2)}) collective-permute-start(bf16[8,2,16,512]{3,2,1,0:T(8,128)(2,1)S(1)} %get-tuple-element.6), channel_id=1, source_target_pairs={{2,0},{3,1},{6,4},{7,5},{10,8},{11,9},{14,12},{15,13},{18,16},{19,... | collective-permute-start | bytes 786440 | tf_op jit(solution)/shard_map/ppermute | solution.py:15
  97.7 1.2 copy-start.8
  98.9 2.2 %copy-start.3 = (bf16[256,16,512]{2,1,0:T(8,128)(2,1)S(1)}, bf16[256,16,512]{2,1,0:T(8,128)(2,1)}, u32[]{:S(2)}) copy-start(bf16[256,16,512]{2,1,0:T(8,128)(2,1)} %broadcast_select_fusion) | copy-start | bytes 12582916
  99.0 2.9 %copy-start.7 = (bf16[512,2048]{1,0:T(8,128)(2,1)S(1)}, bf16[512,2048]{1,0:T(8,128)(2,1)}, u32[]{:S(2)}) copy-start(bf16[512,2048]{1,0:T(8,128)(2,1)} %param.10) | copy-start | bytes 6291460
  105.5 11.9 %copy-start.1 = (bf16[4,16,16,512]{3,2,1,0:T(8,128)(2,1)S(1)}, bf16[4,16,16,512]{3,2,1,0:T(8,128)(2,1)}, u32[]{:S(2)}) copy-start(bf16[4,16,16,512]{3,2,1,0:T(8,128)(2,1)} %param.6) | copy-start | bytes 3145732
Sparse Core Ops, SparseCore 0:
  8.9 85.8 all-gather.1
  105.7 11.7 reduce-scatter.1
where the time goes:
time: 127 us; the launch traced here: 126 us
  waiting for transfers between devices  75.1 us (59%)
  between operations  13.6 us (11%)
  starting transfers between devices  12.1 us (10%)
  local copies, waits for them, and re-layouts  11.6 us (9%)
  other arithmetic  9.03 us (7%)
  matrix products  4.99 us (4%)
    all_gather x1, waiting for transfers between devices, on_device(): piece = lax.all_gather(convergence, 'rows', axis=0, tiled=True)  38.5 us
    ppermute x2, waiting for transfers between devices, padded(): before = lax.ppermute(last, axis, up)  19.6 us
    reduce_scatter x1, waiting for transfers between devices, on_device(): lax.psum_scatter(partial_value, 'sub', scatter_dimension=1, tiled=True)  11.9 us
    ppermute x2, starting transfers between devices, padded(): before = lax.ppermute(last, axis, up)  9.42 us
    ppermute x2, waiting for transfers between devices, padded(): after = lax.ppermute(first, axis, down)  4.41 us
    select_n x2, other arithmetic, on_device(): jnp.take(flat_ext, near_index.reshape(-1), axis=0)  4.09 us
    dot_general x1, matrix products, on_device(): lax.dot_general(near_blocks, near_factor.reshape(pixels, near_slots, pixe...  3.7 us
    unnamed x20, local copies, waits for them, and re-layouts  3.55 us
  transfers between devices with their start and end apart: 6, of which 5 were waited for; matrix products, arithmetic and copies ran while one was open for 9% of the time, Pallas kernels for 0%

commit v1 on v0

v1 whole, which is shorter than its diff:
```python
import jax
import jax.numpy as jnp
from jax import lax
from jax.sharding import PartitionSpec as P

REACH = 2
CHUNKS = 2


def exchange(array, axis, parity):
    count, subs = lax.axis_size(axis), lax.axis_size("sub")
    partner = list(range(count))
    for i in range(parity, count - 1, 2):
        partner[i], partner[i + 1] = i + 1, i
    pairs = []
    for i in range(count):
        for s in range(subs):
            other = s if partner[i] != i else subs - 1 - s
            pairs.append((i * subs + s, partner[i] * subs + other))
    return lax.ppermute(array, (axis, "sub"), pairs)


def swap_sub(array):
    subs = lax.axis_size("sub")
    return lax.ppermute(array, "sub", [(s, subs - 1 - s) for s in range(subs)])


def mean_of(flat, index, factors):
    total = None
    slots = index.shape[1] // len(factors)
    for part, factor in enumerate(factors):
        chosen = index[:, part * slots : (part + 1) * slots]
        blocks = flat.at[chosen.reshape(-1)].get(mode="promise_in_bounds")
        blocks = blocks.reshape(chosen.shape + flat.shape[1:])
        term = lax.dot_general(
            blocks, factor, (((1, 3), (1, 2)), ((), ())), preferred_element_type=jnp.float32
        )
        total = term if total is None else total + term
    return total


def on_device(convergence, block_level, near_codes, far_rows, near_factor, far_factor):
    tile_rows, tile_cols, samples, pixels = convergence.shape
    rows, cols = lax.axis_size("rows"), lax.axis_size("cols")
    row, col, sub = lax.axis_index("rows"), lax.axis_index("cols"), lax.axis_index("sub")
    half = samples // lax.axis_size("sub")
    near_slots, far_slots = near_codes.shape[2], far_rows.shape[2]
    width = tile_cols // CHUNKS
    even_row, even_col = row % 2 == 0, col % 2 == 0

    own = [
        lax.dynamic_slice(
            convergence, (0, c * width, sub * half, 0), (tile_rows, width, half, pixels)
        )
        for c in range(CHUNKS)
    ]

    even = [[exchange(x, "rows", 0) for x in own]]
    odd = [[exchange(x, "rows", 1) for x in own]]
    inner = rows > 4
    for step in range(1, rows - 2):
        if inner and step < rows - 3:
            even.append([exchange(x, "rows", 0) for x in odd[step - 1]])
        odd.append([exchange(x, "rows", 1) for x in even[step - 1]])

    partner_rows = exchange(far_rows, "rows", 0)
    codes = jnp.concatenate([near_codes, far_rows, partner_rows], axis=2)
    other = swap_sub(codes)
    near_all = jnp.concatenate([near_codes, other[:, :, :near_slots]], axis=2)
    far_all = jnp.concatenate([far_rows, other[:, :, near_slots : near_slots + far_slots]], axis=2)
    partner_all = jnp.concatenate([partner_rows, other[:, :, near_slots + far_slots :]], axis=2)
    near_factors = [f.reshape(pixels, near_slots, pixels) for f in (near_factor, swap_sub(near_factor))]
    far_factors = [f.reshape(pixels, far_slots, pixels) for f in (far_factor, swap_sub(far_factor))]

    stack = jnp.concatenate(
        [jnp.concatenate(x, axis=1) for x in (own, even[0], odd[0])], axis=0
    )
    pieces = [stack]
    for parity in range(min(cols - 1, 2)):
        start = jnp.where(even_col == (parity == 0), tile_cols - REACH, 0)
        edge = lax.dynamic_slice_in_dim(stack, start, REACH, axis=1)
        pieces.append(exchange(edge, "cols", parity))
    wide = jnp.concatenate(pieces, axis=1)
    wide_cols = wide.shape[1]
    flat = wide.reshape((-1, half, pixels))
    flat = jnp.concatenate([flat, jnp.zeros((1, half, pixels), flat.dtype)], axis=0)
    at_row = jnp.arange(tile_rows, dtype=jnp.int32)[:, None, None] + near_all // 5 - REACH
    at_col = jnp.arange(tile_cols, dtype=jnp.int32)[None, :, None] + near_all % 5 - REACH
    up, down = jnp.where(even_row, 2, 1) * tile_rows, jnp.where(even_row, 1, 2) * tile_rows
    left = tile_cols + jnp.where(even_col, REACH, 0)
    right = tile_cols + jnp.where(even_col, 0, REACH)
    from_row = jnp.where(
        at_row < 0,
        up + at_row + tile_rows,
        jnp.where(at_row >= tile_rows, down + at_row - tile_rows, at_row),
    )
    from_col = jnp.where(
        at_col < 0,
        left + at_col + REACH,
        jnp.where(at_col >= tile_cols, right + at_col - tile_cols, at_col),
    )
    whole_row, whole_col = at_row + row * tile_rows, at_col + col * tile_cols
    inside = (
        (whole_row >= 0) & (whole_row < rows * tile_rows)
        & (whole_col >= 0) & (whole_col < cols * tile_cols)
    )
    near_index = jnp.where(inside, from_row * wide_cols + from_col, flat.shape[0] - 1)
    near_mean = mean_of(flat, near_index.reshape(-1, near_index.shape[2]), near_factors)
    near_mean = near_mean.reshape(tile_rows, tile_cols, half, pixels)

    shards = [own]
    place_even, place_odd = [0] * rows, [0] * rows
    for step in range(len(odd)):
        if step < len(even):
            place_even[step + 1] = len(shards)
            shards.append(even[step])
        place_odd[step + 1] = len(shards)
        shards.append(odd[step])
    place_even = jnp.array(place_even, jnp.int32)
    place_odd = jnp.array(place_odd, jnp.int32)
    source = jnp.arange(rows, dtype=jnp.int32)
    away = jnp.abs(source - row)
    by_even = (source > row) == even_row
    place = jnp.where(by_even, place_even[away], place_odd[away]) * (away > 0)

    def far_chunk(c, requests):
        flat_shards = jnp.concatenate([x[c] for x in shards], axis=0).reshape(-1, half, pixels)
        wanted = requests[:, c * width : (c + 1) * width]
        at = place[wanted // tile_rows] * tile_rows + wanted % tile_rows
        at = at * width + jnp.arange(width, dtype=jnp.int32)[None, :, None]
        mean = mean_of(flat_shards, at.reshape(-1, at.shape[2]), far_factors)
        return mean.reshape(tile_rows, width, half, pixels)

    at_end = (row == 0) | (row == rows - 1)
    done = []
    for c in range(CHUNKS):
        cols_here = slice(c * width, (c + 1) * width)
        ready = even[0][c].astype(jnp.float32) - far_chunk(c, partner_all)
        ready = exchange(ready.astype(jnp.bfloat16), "rows", 0)
        field = own[c].astype(jnp.float32)
        far_own = (field - far_chunk(c, far_all)).astype(jnp.bfloat16)
        near_own = (field - near_mean[:, cols_here]).astype(jnp.bfloat16)
        level = block_level[:, cols_here, None, None]
        done.append(jnp.where(level == 1, near_own, jnp.where(at_end, ready, far_own)))
    return jnp.concatenate(done, axis=1)


def solution(mesh):
    placed = (
        P(("fields", "rows"), "cols", None, None),
        P(("fields", "rows"), "cols"),
        P(("fields", "rows"), "cols", "sub"),
        P(("fields", "rows"), "cols", "sub"),
        P(None, "sub"),
        P(None, "sub"),
    )
    return jax.shard_map(
        on_device,
        mesh=mesh,
        in_specs=placed,
        out_specs=P(("fields", "rows"), "cols", "sub", None),
        check_vma=False,
    )
```

time: 127 us -> 88 us (0.69)
  waiting for transfers between devices: 75.1 us -> 16 us
  local copies, waits for them, and re-layouts: 11.6 us -> 32.8 us
  between operations: 13.6 us -> 0.7 us
  matrix products: 4.99 us -> 17.7 us
    all_gather x1 -> x0, waiting for transfers between devices: 38.5 us -> none  [on_device(): piece = lax.all_gather(convergence, 'rows', axis=0, tiled=True)]
    gather x2 -> x16, local copies, waits for them, and re-layouts: 5.68 us -> 22.1 us  [the longest x10 14.6 us: mean_of(): blocks = flat.at[chosen.reshape(-1)].get(mode='promise_in_bounds')]
    dot_general x2 -> x10, matrix products: 4.99 us -> 17.7 us  [mean_of(): lax.dot_general(blocks, factor, (((1, 3), (1, 2)), ((), ())), preferred_e...]
    reduce_scatter x1 -> x0, waiting for transfers between devices: 11.9 us -> none  [on_device(): lax.psum_scatter(partial_value, 'sub', scatter_dimension=1, tiled=True)]
    ppermute x4 -> x13, waiting for transfers between devices: 24 us -> 16 us  [the longest x10 16 us: exchange(): return lax.ppermute(array, (axis, 'sub'), pairs)]
    select_n x4 -> x12, other arithmetic: 4.83 us -> 0.4 us  [the longest x1 0.26 us: on_device(): jnp.where(level == 1, near_own, jnp.where(at_end, ready, far_own))]
    concatenate x1 -> x8, other arithmetic: 1.93 us -> 5.68 us  [the longest x2 2.33 us: far_chunk(): jnp.concatenate([x[c] for x in shards], axis=0).reshape(-1, half, pixels)]
    unnamed x20 -> x47, local copies, waits for them, and re-layouts: 3.55 us -> 6.76 us
  transfers between devices with their start and end apart: 6 -> 13, of which waited for: 5 -> 4; matrix products, arithmetic and copies ran while one was open for 9% -> 64% of each run, Pallas kernels for 0% -> 0%
where the time goes in v1:
time: 88 us; the launch traced here: 87.4 us
  local copies, waits for them, and re-layouts  32.8 us (37%)
  matrix products  17.7 us (20%)
  waiting for transfers between devices  16 us (18%)
  starting transfers between devices  11.8 us (13%)
  other arithmetic  8.44 us (10%)
    dot_general x10, matrix products, mean_of(): lax.dot_general(blocks, factor, (((1, 3), (1, 2)), ((), ())), preferred_e...  17.7 us
    ppermute x10, waiting for transfers between devices, exchange(): return lax.ppermute(array, (axis, 'sub'), pairs)  16 us
    gather x10, local copies, waits for them, and re-layouts, mean_of(): blocks = flat.at[chosen.reshape(-1)].get(mode='promise_in_bounds')  14.6 us
    ppermute x10, starting transfers between devices, exchange(): return lax.ppermute(array, (axis, 'sub'), pairs)  11.1 us
    unnamed x47, local copies, waits for them, and re-layouts  6.76 us
    gather x4, local copies, waits for them, and re-layouts, far_chunk(): at = place[wanted // tile_rows] * tile_rows + wanted % tile_rows  4.91 us
    gather x2, local copies, waits for them, and re-layouts, on_device(): place = jnp.where(by_even, place_even[away], place_odd[away]) * (away > 0)  2.59 us
    concatenate x2, other arithmetic, far_chunk(): jnp.concatenate([x[c] for x in shards], axis=0).reshape(-1, half, pixels)  2.33 us
  transfers between devices with their start and end apart: 13, of which 4 were waited for; matrix products, arithmetic and copies ran while one was open for 64% of the time, Pallas kernels for 0%

profile of v1, /device:TPU:0, one launch (start us, length us, event | category | flops | bytes accessed | tf_op | source)
XLA Modules:
  0.0 87.4 jit_solution(14178806636308405755)
XLA Ops:
  0.0 1.1 %constant_dynamic-slice_fusion.1 = (bf16[4,8,8,512]{3,2,1,0:T(8,128)(2,1)S(1)}, bf16[4,8,8,512]{3,2,1,0:T(8,128)(2,1)S(1)}) fusion(bf16[4,16,16,512]{3,2,1,0:T(8,128)(2,1)} %param.8, s32[]{:T(128)S(6)} %select_n.244), kind=kLoop, calls=%fused_computation.168 | loop fusion | bytes 1048580 | tf_op jit(solution)/shard_map/dynamic_slice | solution.py:52
  1.1 3.1 %collective-permute-start = (bf16[4,8,8,512]{3,2,1,0:T(8,128)(2,1)S(1)}, bf16[4,8,8,512]{3,2,1,0:T(8,128)(2,1)}, u32[]{:S(2)}, u32[]{:S(2)}) collective-permute-start(bf16[4,8,8,512]{3,2,1,0:T(8,128)(2,1)S(1)} %get-tuple-element.7), channel_id=1, source_target_pairs={{0,4},{1,5},{4,0},{5,1},{8,12},{9,13},{12,8},{13,9},{2,6},{3,7},{6... | collective-permute-start | bytes 786440 | tf_op jit(solution)/shard_map/ppermute | solution.py:20
  4.2 3.1 %collective-permute-start.1 = (bf16[4,8,8,512]{3,2,1,0:T(8,128)(2,1)S(1)}, bf16[4,8,8,512]{3,2,1,0:T(8,128)(2,1)}, u32[]{:S(2)}, u32[]{:S(2)}) collective-permute-start(bf16[4,8,8,512]{3,2,1,0:T(8,128)(2,1)S(1)} %get-tuple-element.8), channel_id=1, source_target_pairs={{0,4},{1,5},{4,0},{5,1},{8,12},{9,13},{12,8},{13,9},{2,6},{3,7},{6... | collective-permute-start | bytes 786440 | tf_op jit(solution)/shard_map/ppermute | solution.py:20
  7.4 0.4 collective-permute-start.5
  7.8 1.3 %gather_fusion.2 = s32[4]{0:T(128)S(1)} fusion(s32[4]{0:T(128)} %constant.152.clone, s32[1024]{0:T(1024)S(1)} %pad_clamp_fusion.12), kind=kCustom, calls=%fused_computation.2 | custom fusion | bytes 48 | tf_op jit(solution)/shard_map/gather | solution.py:124
  9.1 1.3 %gather_fusion.3 = s32[4]{0:T(128)S(1)} fusion(s32[4]{0:T(128)} %constant.153.clone, s32[1024]{0:T(1024)S(1)} %pad_clamp_fusion.12), kind=kCustom, calls=%fused_computation.3 | custom fusion | bytes 48 | tf_op jit(solution)/shard_map/gather | solution.py:124
  10.5 5.8 %collective-permute-done.5 = s32[4,16,2]{1,2,0:T(2,128)S(1)} collective-permute-done((s32[4,16,2]{1,2,0:T(2,128)}, s32[4,16,2]{1,2,0:T(2,128)S(1)}, u32[]{:S(2)}, u32[]{:S(2)}) %collective-permute-start.5) | collective-permute-done | bytes 544 | tf_op jit(solution)/shard_map/ppermute | solution.py:20
  16.7 4.0 %copy.67 = bf16[512,2048]{0,1:T(8,128)(2,1)} copy(bf16[512,2048]{1,0:T(8,128)(2,1)} %param.12) | data formatting | bytes 4194304 | tf_op args[4]
  20.8 1.3 %copy.74 = bf16[512,1024]{0,1:T(8,128)(2,1)} copy(bf16[512,1024]{1,0:T(8,128)(2,1)S(1)} %copy-done.11) | data formatting | bytes 2097152 | tf_op args[5]
  22.1 0.4 collective-permute-start.7
  23.4 1.2 %gather_fusion.10 = s32[128]{0:T(128)S(1)} fusion(s32[4]{0:T(128)S(1)} %compare_select_fusion.18, s32[1024]{0:T(1024)S(1)} %pad_clamp_fusion.5), kind=kCustom, calls=%fused_computation.10 | custom fusion | bytes 1536 | tf_op jit(solution)/shard_map/gather | solution.py:129
  25.5 1.2 %gather_fusion.13 = s32[128]{0:T(128)S(1)} fusion(s32[4]{0:T(128)S(1)} %compare_select_fusion.18, s32[1024]{0:T(1024)S(1)} %pad_clamp_fusion.2), kind=kCustom, calls=%fused_computation.13 | custom fusion | bytes 1536 | tf_op jit(solution)/shard_map/gather | solution.py:129
  27.4 1.2 %gather_fusion.7 = s32[128]{0:T(128)S(1)} fusion(s32[4]{0:T(128)S(1)} %compare_select_fusion.18, s32[1024]{0:T(1024)S(1)} %pad_clamp_fusion.8), kind=kCustom, calls=%fused_computation.7 | custom fusion | bytes 1536 | tf_op jit(solution)/shard_map/gather | solution.py:129
  29.3 1.2 %gather_fusion.4 = s32[128]{0:T(128)S(1)} fusion(s32[4]{0:T(128)S(1)} %compare_select_fusion.18, s32[1024]{0:T(1024)S(1)} %pad_clamp_fusion.11), kind=kCustom, calls=%fused_computation.4 | custom fusion | bytes 1536 | tf_op jit(solution)/shard_map/gather | solution.py:129
  31.2 1.1 %maximum_maximum_fusion = bf16[12,2,8,512]{3,2,1,0:T(8,128)(2,1)S(1)} fusion(s32[]{:T(128)S(6)} %select_n.246, bf16[4,8,8,512]{3,2,1,0:T(8,128)(2,1)S(1)} %collective-permute-done.3, bf16[4,8,8,512]{3,2,1,0:T(8,128)(2,1)S(1)} %collective-permute-done.2, bf16[4,8,8,512]{3,2,1,0:T(8,128)(2,1)} %collective-permute-done.1, ...), kind=kLoop, calls=%fused_computation.66 | loop fusion | flops 491520 | bytes 1769476 | tf_op jit(solution)/shard_map/concatenate | solution.py:75
  32.3 1.7 %collective-permute-start.4 = (bf16[12,2,8,512]{3,2,1,0:T(8,128)(2,1)S(1)}, bf16[12,2,8,512]{3,2,1,0:T(8,128)(2,1)S(1)}, u32[]{:S(2)}, u32[]{:S(2)}) collective-permute-start(bf16[12,2,8,512]{3,2,1,0:T(8,128)(2,1)S(1)} %maximum_maximum_fusion), channel_id=1, source_target_pairs={{0,2},{1,3},{2,0},{3,1},{4,6},{5,7},{6,4},{7,5},{8,10},{9,11},{10,... | collective-permute-start | bytes 589832 | tf_op jit(solution)/shard_map/ppermute | solution.py:20
  34.3 0.3 collective-permute-start.8
  34.6 5.0 %collective-permute-done.4 = bf16[12,2,8,512]{3,2,1,0:T(8,128)(2,1)S(1)} collective-permute-done((bf16[12,2,8,512]{3,2,1,0:T(8,128)(2,1)S(1)}, bf16[12,2,8,512]{3,2,1,0:T(8,128)(2,1)S(1)}, u32[]{:S(2)}, u32[]{:S(2)}) %collective-permute-start.4) | collective-permute-done | bytes 196640 | tf_op jit(solution)/shard_map/ppermute | solution.py:20
  39.6 1.2 %pad_maximum_fusion = bf16[12,18,8,512]{3,2,1,0:T(8,128)(2,1)S(1)} fusion(bf16[12,2,8,512]{3,2,1,0:T(8,128)(2,1)S(1)} %collective-permute-done.4, bf16[4,8,8,512]{3,2,1,0:T(8,128)(2,1)S(1)} %collective-permute-done.3, bf16[4,8,8,512]{3,2,1,0:T(8,128)(2,1)S(1)} %collective-permute-done.2, bf16[4,8,8,512]{3,2,1,0:T(8,128)(2,1)} %collective-permute-done.1, ...), kind=kLoop, calls=%fused_computation.19 | loop fusion | flops 5308416 | bytes 3538944 | tf_op jit(solution)/shard_map/concatenate | solution.py:83
  41.0 2.2 %gather_fusion = bf16[256,8,512]{2,1,0:T(8,128)(2,1)} fusion(bf16[217,8,512]{2,1,0:T(8,128)(2,1)S(1)} %concatenate.51, s32[1024]{0:T(1024)S(1)} %pad_clamp_fusion.14), kind=kCustom, calls=%fused_computation | custom fusion | bytes 4195328 | tf_op jit(solution)/shard_map/gather | solution.py:33
  43.2 2.1 %gather_fusion.1 = bf16[256,8,512]{2,1,0:T(8,128)(2,1)} fusion(bf16[217,8,512]{2,1,0:T(8,128)(2,1)S(1)} %concatenate.51, s32[1024]{0:T(1024)S(1)} %pad_clamp_fusion.13), kind=kCustom, calls=%fused_computation.1 | custom fusion | bytes 4195328 | tf_op jit(solution)/shard_map/gather | solution.py:33
  45.3 4.5 %fusion.2 = f32[64,8,512]{2,1,0:T(8,128)} fusion(bf16[64,4,8,512]{3,2,1,0:T(8,128)(2,1)} %bitcast.155, bf16[64,4,8,512]{3,2,1,0:T(8,128)(2,1)} %bitcast.162), kind=kOutput, calls=%fused_computation.26 | convolution fusion | flops 1073741824 | bytes 5242880 | tf_op jit(solution)/shard_map/dot_general | solution.py:35
  49.8 1.2 %pad_maximum_fusion.2 = bf16[16,8,8,512]{3,2,1,0:T(8,128)(2,1)S(1)} fusion(bf16[4,8,8,512]{3,2,1,0:T(8,128)(2,1)} %collective-permute-done.11, bf16[4,8,8,512]{3,2,1,0:T(8,128)(2,1)S(1)} %copy-done.5, bf16[4,8,8,512]{3,2,1,0:T(8,128)(2,1)} %collective-permute-done.1, bf16[4,8,8,512]{3,2,1,0:T(8,128)(2,1)S(1)} %get-tuple-element.8), kind=kLoop, calls=%fused_computation.43 | loop fusion | flops 1572864 | bytes 2097152 | tf_op jit(solution)/shard_map/concatenate | solution.py:127
  51.0 1.4 %gather_fusion.11 = bf16[64,8,512]{2,1,0:T(8,128)(2,1)} fusion(bf16[128,8,512]{2,1,0:T(8,128)(2,1)S(1)} %bitcast.145, s32[1024]{0:T(1024)S(1)} %pad_clamp_fusion.4), kind=kCustom, calls=%fused_computation.11 | custom fusion | bytes 1048832 | tf_op jit(solution)/shard_map/gather | solution.py:33
  52.4 2.7 %convolution_bitcast_fusion.4 = f32[32,8,512]{2,1,0:T(8,128)} fusion(bf16[32,2,8,512]{3,2,1,0:T(8,128)(2,1)} %bitcast.172, bf16[64,2,8,512]{3,2,1,0:T(8,128)(2,1)} %bitcast.166), kind=kOutput, calls=%fused_computation.32 | convolution fusion | flops 268435456 | bytes 2097152 | tf_op jit(solution)/shard_map/dot_general | solution.py:35
  55.1 1.4 %gather_fusion.14 = bf16[64,8,512]{2,1,0:T(8,128)(2,1)} fusion(bf16[128,8,512]{2,1,0:T(8,128)(2,1)S(1)} %bitcast.146, s32[1024]{0:T(1024)S(1)} %pad_clamp_fusion.1), kind=kCustom, calls=%fused_computation.14 | custom fusion | bytes 1048832 | tf_op jit(solution)/shard_map/gather | solution.py:33
  56.5 2.3 %convolution_bitcast_fusion.2 = f32[32,8,512]{2,1,0:T(8,128)} fusion(bf16[32,2,8,512]{3,2,1,0:T(8,128)(2,1)} %bitcast.173, bf16[64,2,8,512]{3,2,1,0:T(8,128)(2,1)S(1)} %bitcast.169), kind=kOutput, calls=%fused_computation.30 | convolution fusion | flops 268435456 | bytes 2097152 | tf_op jit(solution)/shard_map/dot_general | solution.py:35
  58.8 1.2 %pad_maximum_fusion.1 = bf16[16,8,8,512]{3,2,1,0:T(8,128)(2,1)S(1)} fusion(bf16[4,8,8,512]{3,2,1,0:T(8,128)(2,1)} %collective-permute-done.8, bf16[4,8,8,512]{3,2,1,0:T(8,128)(2,1)S(1)} %copy-done.3, bf16[4,8,8,512]{3,2,1,0:T(8,128)(2,1)} %collective-permute-done, bf16[4,8,8,512]{3,2,1,0:T(8,128)(2,1)S(1)} %get-tuple-element.7), kind=kLoop, calls=%fused_computation.42 | loop fusion | flops 1572864 | bytes 2097152 | tf_op jit(solution)/shard_map/concatenate | solution.py:127
  60.0 1.4 %gather_fusion.12 = bf16[64,8,512]{2,1,0:T(8,128)(2,1)} fusion(bf16[128,8,512]{2,1,0:T(8,128)(2,1)S(1)} %bitcast.147, s32[1024]{0:T(1024)S(1)} %pad_clamp_fusion.3), kind=kCustom, calls=%fused_computation.12 | custom fusion | bytes 1048832 | tf_op jit(solution)/shard_map/gather | solution.py:33
  61.4 1.4 %gather_fusion.15 = bf16[64,8,512]{2,1,0:T(8,128)(2,1)} fusion(bf16[128,8,512]{2,1,0:T(8,128)(2,1)S(1)} %bitcast.148, s32[1024]{0:T(1024)S(1)} %pad_clamp_fusion), kind=kCustom, calls=%fused_computation.15 | custom fusion | bytes 1048832 | tf_op jit(solution)/shard_map/gather | solution.py:33
  62.8 0.6 gather_fusion.8
  63.4 1.4 %gather_fusion.9 = bf16[64,8,512]{2,1,0:T(8,128)(2,1)} fusion(bf16[128,8,512]{2,1,0:T(8,128)(2,1)S(1)} %bitcast.150, s32[1024]{0:T(1024)S(1)} %pad_clamp_fusion.6), kind=kCustom, calls=%fused_computation.9 | custom fusion | bytes 1048832 | tf_op jit(solution)/shard_map/gather | solution.py:33
  64.8 1.4 %gather_fusion.6 = bf16[64,8,512]{2,1,0:T(8,128)(2,1)} fusion(bf16[128,8,512]{2,1,0:T(8,128)(2,1)S(1)} %bitcast.151, s32[1024]{0:T(1024)S(1)} %pad_clamp_fusion.9), kind=kCustom, calls=%fused_computation.6 | custom fusion | bytes 1048832 | tf_op jit(solution)/shard_map/gather | solution.py:33
  66.2 1.4 %gather_fusion.5 = bf16[64,8,512]{2,1,0:T(8,128)(2,1)} fusion(bf16[128,8,512]{2,1,0:T(8,128)(2,1)S(1)} %bitcast.152, s32[1024]{0:T(1024)S(1)} %pad_clamp_fusion.10), kind=kCustom, calls=%fused_computation.5 | custom fusion | bytes 1048832 | tf_op jit(solution)/shard_map/gather | solution.py:33
  67.6 1.8 %convolution_bitcast_fusion.6 = f32[32,8,512]{2,1,0:T(8,128)S(1)} fusion(bf16[32,2,8,512]{3,2,1,0:T(8,128)(2,1)S(1)} %bitcast.170, bf16[64,2,8,512]{3,2,1,0:T(8,128)(2,1)} %bitcast.167), kind=kOutput, calls=%fused_computation.34 | convolution fusion | flops 268435456 | bytes 2097152 | tf_op jit(solution)/shard_map/dot_general | solution.py:35
  69.4 1.7 %convolution_bitcast_fusion.8 = f32[32,8,512]{2,1,0:T(8,128)S(1)} fusion(bf16[32,2,8,512]{3,2,1,0:T(8,128)(2,1)S(1)} %bitcast.171, bf16[64,2,8,512]{3,2,1,0:T(8,128)(2,1)} %bitcast.168), kind=kOutput, calls=%fused_computation.36 | convolution fusion | flops 268435456 | bytes 2097152 | tf_op jit(solution)/shard_map/dot_general | solution.py:35
  71.2 0.4 fusion.6
  71.6 1.0 %subtract_convert_fusion = bf16[4,8,8,512]{3,2,1,0:T(8,128)(2,1)S(1)} fusion(f32[4,8,8,512]{3,2,1,0:T(8,128)S(1)} %bitcast.156, bf16[4,8,8,512]{3,2,1,0:T(8,128)(2,1)} %collective-permute-done.1), kind=kLoop, calls=%fused_computation.57 | loop fusion | flops 393216 | bytes 1048576 | tf_op jit(solution)/shard_map/convert_element_type | solution.py:139
  72.7 1.8 %collective-permute-start.12 = (bf16[4,8,8,512]{3,2,1,0:T(8,128)(2,1)S(1)}, bf16[4,8,8,512]{3,2,1,0:T(8,128)(2,1)S(1)}, u32[]{:S(2)}, u32[]{:S(2)}) collective-permute-start(bf16[4,8,8,512]{3,2,1,0:T(8,128)(2,1)S(1)} %subtract_convert_fusion), channel_id=1, source_target_pairs={{0,4},{1,5},{4,0},{5,1},{8,12},{9,13},{12,8},{13,9},{2,6},{3,7},{6... | collective-permute-start | bytes 786440 | tf_op jit(solution)/shard_map/ppermute | solution.py:20
  74.5 0.4 fusion.4
  74.9 1.1 %subtract_convert_fusion.1 = bf16[4,8,8,512]{3,2,1,0:T(8,128)(2,1)S(1)} fusion(f32[4,8,8,512]{3,2,1,0:T(8,128)S(1)} %bitcast.157, bf16[4,8,8,512]{3,2,1,0:T(8,128)(2,1)} %collective-permute-done), kind=kLoop, calls=%fused_computation.58 | loop fusion | flops 393216 | bytes 1048576 | tf_op jit(solution)/shard_map/convert_element_type | solution.py:139
  76.4 0.4 fusion.7
  76.8 0.4 fusion.5
  77.3 0.7 copy-done.6
  78.2 2.9 %fusion.3 = f32[64,8,512]{2,1,0:T(8,128)S(1)} fusion(f32[64,8,512]{2,1,0:T(8,128)S(1)} %copy-done.19, bf16[64,4,8,512]{3,2,1,0:T(8,128)(2,1)S(1)} %bitcast.154, bf16[512,4,512,1]{0,2,1,3:T(8,128)(2,1)} %bitcast.9), kind=kOutput, calls=%fused_computation.28 | convolution fusion | flops 1074003968 | bytes 6291456 | tf_op jit(solution)/shard_map/dot_general | solution.py:35
  81.1 0.8 collective-permute-done.12
  82.0 4.4 %collective-permute-done.10 = bf16[4,8,8,512]{3,2,1,0:T(8,128)(2,1)S(1)} collective-permute-done((bf16[4,8,8,512]{3,2,1,0:T(8,128)(2,1)S(1)}, bf16[4,8,8,512]{3,2,1,0:T(8,128)(2,1)S(1)}, u32[]{:S(2)}, u32[]{:S(2)}) %collective-permute-start.10) | collective-permute-done | bytes 262176 | tf_op jit(solution)/shard_map/ppermute | solution.py:20
  86.6 0.8 pad_maximum_fusion.3
  (134 shorter events, 5.2 us)
Async XLA Ops:
  0.0 16.3 %copy-start.17 = (s32[4,16,2]{1,2,0:T(2,128)S(1)}, s32[4,16,2]{1,2,0:T(2,128)}, u32[]{:S(2)}) copy-start(s32[4,16,2]{1,2,0:T(2,128)} %param.11) | copy-start | bytes 1540
  0.0 10.4 %copy-start.18 = (s32[4,16]{1,0:T(4,128)S(1)}, s32[4,16]{1,0:T(4,128)}, u32[]{:S(2)}) copy-start(s32[4,16]{1,0:T(4,128)} %param.9) | copy-start | bytes 772
  0.0 16.3 %copy-start.16 = (s32[4,16,4]{1,2,0:T(4,128)S(1)}, s32[4,16,4]{1,2,0:T(4,128)}, u32[]{:S(2)}) copy-start(s32[4,16,4]{1,2,0:T(4,128)} %param.10) | copy-start | bytes 3076
  1.1 48.7 %copy-start = (bf16[4,8,8,512]{3,2,1,0:T(8,128)(2,1)}, bf16[4,8,8,512]{3,2,1,0:T(8,128)(2,1)S(1)}, u32[]{:S(2)}) copy-start(bf16[4,8,8,512]{3,2,1,0:T(8,128)(2,1)S(1)} %get-tuple-element.8) | copy-start | bytes 786436
  1.1 29.9 %collective-permute-start = (bf16[4,8,8,512]{3,2,1,0:T(8,128)(2,1)S(1)}, bf16[4,8,8,512]{3,2,1,0:T(8,128)(2,1)}, u32[]{:S(2)}, u32[]{:S(2)}) collective-permute-start(bf16[4,8,8,512]{3,2,1,0:T(8,128)(2,1)S(1)} %get-tuple-element.7), channel_id=1, source_target_pairs={{0,4},{1,5},{4,0},{5,1},{8,12},{9,13},{12,8},{13,9},{2,6},{3,7},{6... | collective-permute-start | bytes 786440 | tf_op jit(solution)/shard_map/ppermute | solution.py:20
  4.2 26.9 %collective-permute-start.2 = (bf16[4,8,8,512]{3,2,1,0:T(8,128)(2,1)S(1)}, bf16[4,8,8,512]{3,2,1,0:T(8,128)(2,1)S(1)}, u32[]{:S(2)}, u32[]{:S(2)}) collective-permute-start(bf16[4,8,8,512]{3,2,1,0:T(8,128)(2,1)S(1)} %get-tuple-element.7), channel_id=1, source_target_pairs={{0,1},{1,0},{4,8},{5,9},{8,4},{9,5},{12,13},{13,12},{2,3},{3,2},{6... | collective-permute-start | bytes 786440 | tf_op jit(solution)/shard_map/ppermute | solution.py:20
  4.2 26.9 %collective-permute-start.1 = (bf16[4,8,8,512]{3,2,1,0:T(8,128)(2,1)S(1)}, bf16[4,8,8,512]{3,2,1,0:T(8,128)(2,1)}, u32[]{:S(2)}, u32[]{:S(2)}) collective-permute-start(bf16[4,8,8,512]{3,2,1,0:T(8,128)(2,1)S(1)} %get-tuple-element.8), channel_id=1, source_target_pairs={{0,4},{1,5},{4,0},{5,1},{8,12},{9,13},{12,8},{13,9},{2,6},{3,7},{6... | collective-permute-start | bytes 786440 | tf_op jit(solution)/shard_map/ppermute | solution.py:20
  7.4 23.8 %collective-permute-start.3 = (bf16[4,8,8,512]{3,2,1,0:T(8,128)(2,1)S(1)}, bf16[4,8,8,512]{3,2,1,0:T(8,128)(2,1)S(1)}, u32[]{:S(2)}, u32[]{:S(2)}) collective-permute-start(bf16[4,8,8,512]{3,2,1,0:T(8,128)(2,1)S(1)} %get-tuple-element.8), channel_id=1, source_target_pairs={{0,1},{1,0},{4,8},{5,9},{8,4},{9,5},{12,13},{13,12},{2,3},{3,2},{6... | collective-permute-start | bytes 786440 | tf_op jit(solution)/shard_map/ppermute | solution.py:20
  7.4 8.9 %collective-permute-start.5 = (s32[4,16,2]{1,2,0:T(2,128)}, s32[4,16,2]{1,2,0:T(2,128)S(1)}, u32[]{:S(2)}, u32[]{:S(2)}) collective-permute-start(s32[4,16,2]{1,2,0:T(2,128)} %param.11), channel_id=1, source_target_pairs={{0,4},{1,5},{4,0},{5,1},{8,12},{9,13},{12,8},{13,9},{2,6},{3,7},{6... | collective-permute-start | bytes 1544 | tf_op jit(solution)/shard_map/ppermute | solution.py:20
  16.3 5.8 %collective-permute-start.6 = (s32[4,16,8]{1,2,0:T(8,128)S(1)}, s32[4,16,8]{1,2,0:T(8,128)S(1)}, u32[]{:S(2)}, u32[]{:S(2)}) collective-permute-start(s32[4,16,8]{1,2,0:T(8,128)S(1)} %pad_add_fusion), channel_id=1, source_target_pairs={{0,1},{1,0},{2,3},{3,2},{4,5},{5,4},{6,7},{7,6},{8,9},{9,8},{10,11... | collective-permute-start | bytes 6152 | tf_op jit(solution)/shard_map/ppermute | solution.py:25
  16.7 4.0 %copy-start.11 = (bf16[512,1024]{1,0:T(8,128)(2,1)S(1)}, bf16[512,1024]{1,0:T(8,128)(2,1)}, u32[]{:S(2)}) copy-start(bf16[512,1024]{1,0:T(8,128)(2,1)} %param.13) | copy-start | bytes 3145732
  22.1 55.2 %collective-permute-start.7 = (bf16[512,2048]{0,1:T(8,128)(2,1)}, bf16[512,2048]{0,1:T(8,128)(2,1)}, u32[]{:S(2)}, u32[]{:S(2)}) collective-permute-start(bf16[512,2048]{0,1:T(8,128)(2,1)} %copy.67), channel_id=1, source_target_pairs={{0,1},{1,0},{2,3},{3,2},{4,5},{5,4},{6,7},{7,6},{8,9},{9,8},{10,11... | collective-permute-start | bytes 6291464 | tf_op jit(solution)/shard_map/ppermute | solution.py:25
  31.0 40.2 %collective-permute-start.9 = (bf16[512,1024]{0,1:T(8,128)(2,1)}, bf16[512,1024]{0,1:T(8,128)(2,1)S(1)}, u32[]{:S(2)}, u32[]{:S(2)}) collective-permute-start(bf16[512,1024]{0,1:T(8,128)(2,1)} %copy.74), channel_id=1, source_target_pairs={{0,1},{1,0},{2,3},{3,2},{4,5},{5,4},{6,7},{7,6},{8,9},{9,8},{10,11... | collective-permute-start | bytes 3145736 | tf_op jit(solution)/shard_map/ppermute | solution.py:25
  31.2 9.7 %copy-start.2 = (bf16[4,8,8,512]{3,2,1,0:T(8,128)(2,1)}, bf16[4,8,8,512]{3,2,1,0:T(8,128)(2,1)S(1)}, u32[]{:S(2)}) copy-start(bf16[4,8,8,512]{3,2,1,0:T(8,128)(2,1)S(1)} %collective-permute-done.2) | copy-start | bytes 786436
  31.2 9.7 %copy-start.4 = (bf16[4,8,8,512]{3,2,1,0:T(8,128)(2,1)}, bf16[4,8,8,512]{3,2,1,0:T(8,128)(2,1)S(1)}, u32[]{:S(2)}) copy-start(bf16[4,8,8,512]{3,2,1,0:T(8,128)(2,1)S(1)} %collective-permute-done.3) | copy-start | bytes 786436
  32.3 7.3 %collective-permute-start.4 = (bf16[12,2,8,512]{3,2,1,0:T(8,128)(2,1)S(1)}, bf16[12,2,8,512]{3,2,1,0:T(8,128)(2,1)S(1)}, u32[]{:S(2)}, u32[]{:S(2)}) collective-permute-start(bf16[12,2,8,512]{3,2,1,0:T(8,128)(2,1)S(1)} %maximum_maximum_fusion), channel_id=1, source_target_pairs={{0,2},{1,3},{2,0},{3,1},{4,6},{5,7},{6,4},{7,5},{8,10},{9,11},{10,... | collective-permute-start | bytes 589832 | tf_op jit(solution)/shard_map/ppermute | solution.py:20
  34.0 15.8 %collective-permute-start.11 = (bf16[4,8,8,512]{3,2,1,0:T(8,128)(2,1)}, bf16[4,8,8,512]{3,2,1,0:T(8,128)(2,1)}, u32[]{:S(2)}, u32[]{:S(2)}) collective-permute-start(bf16[4,8,8,512]{3,2,1,0:T(8,128)(2,1)} %collective-permute-done.1), channel_id=1, source_target_pairs={{0,1},{1,0},{4,8},{5,9},{8,4},{9,5},{12,13},{13,12},{2,3},{3,2},{6... | collective-permute-start | bytes 786440 | tf_op jit(solution)/shard_map/ppermute | solution.py:20
  34.3 24.6 %collective-permute-start.8 = (bf16[4,8,8,512]{3,2,1,0:T(8,128)(2,1)}, bf16[4,8,8,512]{3,2,1,0:T(8,128)(2,1)}, u32[]{:S(2)}, u32[]{:S(2)}) collective-permute-start(bf16[4,8,8,512]{3,2,1,0:T(8,128)(2,1)} %collective-permute-done), channel_id=1, source_target_pairs={{0,1},{1,0},{4,8},{5,9},{8,4},{9,5},{12,13},{13,12},{2,3},{3,2},{6... | collective-permute-start | bytes 786440 | tf_op jit(solution)/shard_map/ppermute | solution.py:20
  45.3 4.5 %copy-start.5 = (bf16[4,8,8,512]{3,2,1,0:T(8,128)(2,1)S(1)}, bf16[4,8,8,512]{3,2,1,0:T(8,128)(2,1)}, u32[]{:S(2)}) copy-start(bf16[4,8,8,512]{3,2,1,0:T(8,128)(2,1)} %copy-done.4) | copy-start | bytes 786436
  51.0 5.5 %copy-start.12 = (bf16[512,1024]{1,0:T(8,128)(2,1)S(1)}, bf16[512,1024]{1,0:T(8,128)(2,1)}, u32[]{:S(2)}) copy-start(bf16[512,1024]{1,0:T(8,128)(2,1)} %param.13) | copy-start | bytes 3145732
  56.5 2.4 %copy-start.3 = (bf16[4,8,8,512]{3,2,1,0:T(8,128)(2,1)S(1)}, bf16[4,8,8,512]{3,2,1,0:T(8,128)(2,1)}, u32[]{:S(2)}) copy-start(bf16[4,8,8,512]{3,2,1,0:T(8,128)(2,1)} %copy-done.2) | copy-start | bytes 786436
  67.6 1.8 %copy-start.15 = (bf16[64,8,512]{2,1,0:T(8,128)(2,1)S(1)}, bf16[64,8,512]{2,1,0:T(8,128)(2,1)}, u32[]{:S(2)}) copy-start(bf16[64,8,512]{2,1,0:T(8,128)(2,1)} %gather_fusion.5) | copy-start | bytes 1572868
  67.6 3.6 %copy-start.9 = (bf16[64,8,512]{2,1,0:T(8,128)(2,1)S(1)}, bf16[64,8,512]{2,1,0:T(8,128)(2,1)}, u32[]{:S(2)}) copy-start(bf16[64,8,512]{2,1,0:T(8,128)(2,1)} %gather_fusion.12) | copy-start | bytes 1572868
  67.6 3.6 %copy-start.14 = (f32[32,8,512]{2,1,0:T(8,128)S(1)}, f32[32,8,512]{2,1,0:T(8,128)}, u32[]{:S(2)}) copy-start(f32[32,8,512]{2,1,0:T(8,128)} %convolution_bitcast_fusion.4) | copy-start | bytes 1572868
  71.2 3.3 %copy-start.10 = (bf16[64,8,512]{2,1,0:T(8,128)(2,1)S(1)}, bf16[64,8,512]{2,1,0:T(8,128)(2,1)}, u32[]{:S(2)}) copy-start(bf16[64,8,512]{2,1,0:T(8,128)(2,1)} %gather_fusion.6) | copy-start | bytes 1572868
  72.7 3.7 %copy-start.7 = (bf16[64,8,512]{2,1,0:T(8,128)(2,1)S(1)}, bf16[64,8,512]{2,1,0:T(8,128)(2,1)}, u32[]{:S(2)}) copy-start(bf16[64,8,512]{2,1,0:T(8,128)(2,1)} %gather_fusion.15) | copy-start | bytes 1572868
  72.7 3.7 %copy-start.13 = (f32[32,8,512]{2,1,0:T(8,128)S(1)}, f32[32,8,512]{2,1,0:T(8,128)}, u32[]{:S(2)}) copy-start(f32[32,8,512]{2,1,0:T(8,128)} %convolution_bitcast_fusion.2) | copy-start | bytes 1572868
  72.7 9.3 %collective-permute-start.12 = (bf16[4,8,8,512]{3,2,1,0:T(8,128)(2,1)S(1)}, bf16[4,8,8,512]{3,2,1,0:T(8,128)(2,1)S(1)}, u32[]{:S(2)}, u32[]{:S(2)}) collective-permute-start(bf16[4,8,8,512]{3,2,1,0:T(8,128)(2,1)S(1)} %subtract_convert_fusion), channel_id=1, source_target_pairs={{0,4},{1,5},{4,0},{5,1},{8,12},{9,13},{12,8},{13,9},{2,6},{3,7},{6... | collective-permute-start | bytes 786440 | tf_op jit(solution)/shard_map/ppermute | solution.py:20
  74.9 1.9 %copy-start.8 = (bf16[64,8,512]{2,1,0:T(8,128)(2,1)S(1)}, bf16[64,8,512]{2,1,0:T(8,128)(2,1)}, u32[]{:S(2)}) copy-start(bf16[64,8,512]{2,1,0:T(8,128)(2,1)} %gather_fusion.9) | copy-start | bytes 1572868
  76.0 10.3 %collective-permute-start.10 = (bf16[4,8,8,512]{3,2,1,0:T(8,128)(2,1)S(1)}, bf16[4,8,8,512]{3,2,1,0:T(8,128)(2,1)S(1)}, u32[]{:S(2)}, u32[]{:S(2)}) collective-permute-start(bf16[4,8,8,512]{3,2,1,0:T(8,128)(2,1)S(1)} %subtract_convert_fusion.1), channel_id=1, source_target_pairs={{0,4},{1,5},{4,0},{5,1},{8,12},{9,13},{12,8},{13,9},{2,6},{3,7},{6... | collective-permute-start | bytes 786440 | tf_op jit(solution)/shard_map/ppermute | solution.py:20
  76.4 1.6 %copy-start.6 = (bf16[256,8,512]{2,1,0:T(8,128)(2,1)S(1)}, bf16[256,8,512]{2,1,0:T(8,128)(2,1)}, u32[]{:S(2)}) copy-start(bf16[256,8,512]{2,1,0:T(8,128)(2,1)} %gather_fusion.1) | copy-start | bytes 6291460
  76.4 1.9 %copy-start.19 = (f32[64,8,512]{2,1,0:T(8,128)S(1)}, f32[64,8,512]{2,1,0:T(8,128)}, u32[]{:S(2)}) copy-start(f32[64,8,512]{2,1,0:T(8,128)} %fusion.2) | copy-start | bytes 3145732
  78.2 8.1 %copy-start.1 = (bf16[4,8,8,512]{3,2,1,0:T(8,128)(2,1)S(1)}, bf16[4,8,8,512]{3,2,1,0:T(8,128)(2,1)}, u32[]{:S(2)}) copy-start(bf16[4,8,8,512]{3,2,1,0:T(8,128)(2,1)} %copy-done) | copy-start | bytes 786436

commit v2 on v1

v2 whole, which is shorter than its diff:
```python
import functools

import jax
import jax.numpy as jnp
from jax import lax
from jax.experimental import pallas as pl
from jax.experimental.pallas import tpu as pltpu
from jax.sharding import PartitionSpec as P

REACH = 2
CHUNKS = 2
VMEM_BYTES = 48 * 2**20
CONTRACT_LAST = (((1,), (1,)), ((), ()))


def exchange(array, axis, parity):
    count, subs = lax.axis_size(axis), lax.axis_size("sub")
    partner = list(range(count))
    for i in range(parity, count - 1, 2):
        partner[i], partner[i + 1] = i + 1, i
    pairs = []
    for i in range(count):
        for s in range(subs):
            other = s if partner[i] != i else subs - 1 - s
            pairs.append((i * subs + s, partner[i] * subs + other))
    return lax.ppermute(array, (axis, "sub"), pairs)


def swap_sub(array):
    subs = lax.axis_size("sub")
    return lax.ppermute(array, "sub", [(s, subs - 1 - s) for s in range(subs)])


def whole(ref_space=pltpu.VMEM):
    return pl.BlockSpec(memory_space=ref_space)


def call(kernel, rows, pixels, ints, arrays, scratch, flops):
    moved = 2 * sum(a.size for a in arrays) + 2 * rows * pixels
    return pl.pallas_call(
        kernel,
        out_shape=jax.ShapeDtypeStruct((rows, pixels), jnp.bfloat16),
        in_specs=[whole(pltpu.SMEM)] * len(ints) + [whole()] * len(arrays),
        out_specs=whole(),
        scratch_shapes=scratch,
        compiler_params=pltpu.CompilerParams(vmem_limit_bytes=VMEM_BYTES),
        cost_estimate=pl.CostEstimate(flops=flops, bytes_accessed=moved, transcendentals=0),
    )(*ints, *arrays)


def as_blocks(rows16, half):
    return rows16.astype(jnp.float32).reshape(-1, half, rows16.shape[-1])


def gather(blocks, chosen, index_of, groups, width, slots, half, pixels):
    per_step = 2 * half

    def one_group(g, carry):
        for j in range(0, width, 2):
            at = pl.multiple_of((g * width + j) * half, per_step)
            for k in range(slots):
                pair = [blocks[index_of(g, j + i, k)] for i in range(2)]
                chosen[pl.ds(at, per_step), k * pixels : (k + 1) * pixels] = (
                    jnp.concatenate(pair, axis=0).astype(jnp.bfloat16)
                )
        return carry

    lax.fori_loop(0, groups, one_group, 0)


def product(chosen, factors):
    total = None
    start = 0
    for factor in factors:
        depth = factor.shape[1]
        term = lax.dot_general(
            chosen[:, start : start + depth], factor[...], CONTRACT_LAST,
            preferred_element_type=jnp.float32,
        )
        total = term if total is None else total + term
        start += depth
    return total


def far_kernel(dims, names, position, requests, *refs):
    rows, tile_rows, width, first, half, pixels, slots = dims
    shards = refs[: len(names)]
    field, near_half, far_half, out, blocks, chosen = refs[len(names) :]
    row = position[0]
    sign = jnp.where(row % 2 == 0, 1, -1)
    count = tile_rows * width
    for (parity, step), shard in zip(names, shards):
        away = 0 if step < 0 else (1 + step) * (sign if parity == 0 else -sign)
        source = row + away
        source = jnp.where((source >= 0) & (source < rows), source, rows)
        for g in range(tile_rows):
            piece = shard[g * width * half : (g + 1) * width * half, :]
            blocks[pl.ds(source * count + g * width, width)] = as_blocks(piece, half)

    def index_of(g, j, k):
        return requests[g, first + j, k] * width + j

    gather(blocks, chosen, index_of, tile_rows, width, slots, half, pixels)
    mean = product(chosen, (near_half, far_half))
    out[...] = (field[...].astype(jnp.float32) - mean).astype(jnp.bfloat16)


def near_kernel(dims, position, index, *refs):
    rows, cols, tile_rows, tile_cols, width, half, pixels, slots = dims
    chunks = tile_cols // width
    own, even, odd = (refs[i * chunks : (i + 1) * chunks] for i in range(3))
    sides = min(cols - 1, 2)
    halos = refs[3 * chunks : 3 * chunks + sides]
    own_half, other_half, out, blocks, chosen = refs[3 * chunks + sides :]
    row, col = position[0], position[1]
    wide = tile_cols + 2 * REACH
    even_row, even_col = row % 2 == 0, col % 2 == 0
    blocks[...] = jnp.zeros_like(blocks)

    def put(at, piece):
        data = as_blocks(piece, half)
        blocks[pl.ds(at, data.shape[0])] = data

    def put_rows(refs_of, source_row, at_row, count):
        for c, ref in enumerate(refs_of):
            for g in range(count):
                begin = (source_row + g) * width * half
                put((at_row + g) * wide + REACH + c * width, ref[begin : begin + width * half, :])

    put_rows(own, 0, REACH, tile_rows)
    above, below = row > 0, row < rows - 1
    last = tile_rows - REACH

    @pl.when(above & even_row)
    def _():
        put_rows(odd, last, 0, REACH)

    @pl.when(above & jnp.logical_not(even_row))
    def _():
        put_rows(even, last, 0, REACH)

    @pl.when(below & even_row)
    def _():
        put_rows(even, 0, tile_rows + REACH, REACH)

    @pl.when(below & jnp.logical_not(even_row))
    def _():
        put_rows(odd, 0, tile_rows + REACH, REACH)

    step = REACH * half
    for parity, halo in enumerate(halos):
        on_right = even_col == (parity == 0)
        present = jnp.where(on_right, col < cols - 1, col > 0)
        at_col = jnp.where(on_right, tile_cols + REACH, 0)

        @pl.when(present)
        def _():
            for g in range(tile_rows):
                put((g + REACH) * wide + at_col, halo[g * step : (g + 1) * step, :])

        @pl.when(present & above)
        def _():
            source = jnp.where(even_row, 2, 1) * tile_rows + last
            for g in range(REACH):
                begin = pl.multiple_of((source + g) * step, step)
                put(g * wide + at_col, halo[pl.ds(begin, step), :])

        @pl.when(present & below)
        def _():
            source = jnp.where(even_row, 1, 2) * tile_rows
            for g in range(REACH):
                begin = pl.multiple_of((source + g) * step, step)
                put((tile_rows + REACH + g) * wide + at_col, halo[pl.ds(begin, step), :])

    def index_of(g, j, k):
        return index[g, j, k]

    gather(blocks, chosen, index_of, tile_rows, tile_cols, slots, half, pixels)
    mean = product(chosen, (own_half, other_half))
    for g in range(tile_rows):
        for c in range(chunks):
            at = (g * tile_cols + c * width) * half
            field = own[c][g * width * half : (g + 1) * width * half, :]
            value = field.astype(jnp.float32) - mean[at : at + width * half, :]
            out[at : at + width * half, :] = value.astype(jnp.bfloat16)


def on_device(convergence, block_level, near_codes, far_rows, near_factor, far_factor):
    tile_rows, tile_cols, samples, pixels = convergence.shape
    rows, cols = lax.axis_size("rows"), lax.axis_size("cols")
    row, col, sub = lax.axis_index("rows"), lax.axis_index("cols"), lax.axis_index("sub")
    half = samples // lax.axis_size("sub")
    near_slots, far_slots = near_codes.shape[2], far_rows.shape[2]
    width = tile_cols // CHUNKS
    position = jnp.stack([row, col]).astype(jnp.int32)

    own = [
        lax.dynamic_slice(
            convergence, (0, c * width, sub * half, 0), (tile_rows, width, half, pixels)
        ).reshape(-1, pixels)
        for c in range(CHUNKS)
    ]

    even = [[exchange(x, "rows", 0) for x in own]]
    odd = [[exchange(x, "rows", 1) for x in own]]
    inner = rows > 4
    for step in range(1, rows - 2):
        if inner and step < rows - 3:
            even.append([exchange(x, "rows", 0) for x in odd[step - 1]])
        odd.append([exchange(x, "rows", 1) for x in even[step - 1]])

    partner_rows = exchange(far_rows, "rows", 0)
    codes = jnp.concatenate([near_codes, far_rows, partner_rows], axis=2)
    other = swap_sub(codes)
    near_all = jnp.concatenate([near_codes, other[:, :, :near_slots]], axis=2)
    far_all = jnp.concatenate([far_rows, other[:, :, near_slots : near_slots + far_slots]], axis=2)
    partner_all = jnp.concatenate([partner_rows, other[:, :, near_slots + far_slots :]], axis=2)
    near_other, far_other = swap_sub(near_factor), swap_sub(far_factor)

    wide = tile_cols + 2 * REACH
    at_row = jnp.arange(tile_rows, dtype=jnp.int32)[:, None, None] + near_all // 5
    at_col = jnp.arange(tile_cols, dtype=jnp.int32)[None, :, None] + near_all % 5
    near_index = at_row * wide + at_col
    halos = []
    for parity in range(min(cols - 1, 2)):
        from_last = (col % 2 == 0) == (parity == 0)
        edge = []
        for source in (own, even[0], odd[0]):
            shaped = [x.reshape(tile_rows, width, half, pixels) for x in source]
            edge.append(jnp.where(from_last, shaped[-1][:, width - REACH :], shaped[0][:, :REACH]))
        edge = jnp.concatenate(edge, axis=0).reshape(-1, pixels)
        halos.append(exchange(edge, "cols", parity))
    tile = tile_rows * tile_cols * half
    near_depth = 2 * near_slots * pixels
    dims = (rows, cols, tile_rows, tile_cols, width, half, pixels, 2 * near_slots)
    near_own = call(
        functools.partial(near_kernel, dims),
        tile, pixels, [position, near_index],
        [*own, *even[0], *odd[0], *halos, near_factor, near_other],
        [
            pltpu.VMEM(((tile_rows + 2 * REACH) * wide, half, pixels), jnp.float32),
            pltpu.VMEM((tile, near_depth), jnp.bfloat16),
        ],
        2 * tile * near_depth * pixels,
    ).reshape(tile_rows, tile_cols, half, pixels)

    names = [(0, -1)]
    shards = [own]
    for step in range(len(odd)):
        if step < len(even):
            names.append((0, step))
            shards.append(even[step])
        names.append((1, step))
        shards.append(odd[step])

    def far_chunk(c, requests, field):
        dims = (rows, tile_rows, width, c * width, half, pixels, 2 * far_slots)
        here = tile_rows * width
        depth = 2 * far_slots * pixels
        return call(
            functools.partial(far_kernel, dims, names),
            here * half, pixels, [position, requests],
            [*(x[c] for x in shards), field, far_factor, far_other],
            [
                pltpu.VMEM(((rows + 1) * here, half, pixels), jnp.float32),
                pltpu.VMEM((here * half, depth), jnp.bfloat16),
            ],
            2 * here * half * depth * pixels,
        )

    at_end = (row == 0) | (row == rows - 1)
    done = []
    for c in range(CHUNKS):
        ready = exchange(far_chunk(c, partner_all, even[0][c]), "rows", 0)
        far_own = far_chunk(c, far_all, own[c])
        far = jnp.where(at_end, ready, far_own).reshape(tile_rows, width, half, pixels)
        level = block_level[:, c * width : (c + 1) * width, None, None]
        done.append(jnp.where(level == 1, near_own[:, c * width : (c + 1) * width], far))
    return jnp.concatenate(done, axis=1)


def solution(mesh):
    placed = (
        P(("fields", "rows"), "cols", None, None),
        P(("fields", "rows"), "cols"),
        P(("fields", "rows"), "cols", "sub"),
        P(("fields", "rows"), "cols", "sub"),
        P(None, "sub"),
        P(None, "sub"),
    )
    return jax.shard_map(
        on_device,
        mesh=mesh,
        in_specs=placed,
        out_specs=P(("fields", "rows"), "cols", "sub", None),
        check_vma=False,
    )
```

time: 88 us -> 53.4 us (0.61)
  local copies, waits for them, and re-layouts: 32.8 us -> 3.62 us
  matrix products: 17.7 us -> 0 us
  Pallas kernels: 0 us -> 14.1 us
  starting transfers between devices: 11.8 us -> 20.3 us
  other arithmetic: 8.44 us -> 2.53 us
  waiting for transfers between devices: 16 us -> 12.2 us
    gather x16 -> x0, local copies, waits for them, and re-layouts: 22.1 us -> none  [the longest x10 14.6 us: mean_of(): blocks = flat.at[chosen.reshape(-1)].get(mode='promise_in_bounds')]
    dot_general x10 -> x0, matrix products: 17.7 us -> none  [mean_of(): lax.dot_general(blocks, factor, (((1, 3), (1, 2)), ((), ())), preferred_e...]
    pallas_call x0 -> x5, Pallas kernels: none -> 14.1 us  [call(): pl.pallas_call(kernel, out_shape=jax.ShapeDtypeStruct((rows, pixels), jnp...]
    ppermute x10, starting transfers between devices: 11.1 us -> 19.7 us  [exchange(): return lax.ppermute(array, (axis, 'sub'), pairs)]
    concatenate x5 -> x1, other arithmetic: 5.52 us -> 0.02 us  [on_device(): edge = jnp.concatenate(edge, axis=0).reshape(-1, pixels)]
    ppermute x10, waiting for transfers between devices: 16 us -> 11.1 us  [exchange(): return lax.ppermute(array, (axis, 'sub'), pairs)]
    unnamed x47 -> x10, local copies, waits for them, and re-layouts: 6.76 us -> 2.38 us
    convert_element_type x2 -> x0, other arithmetic: 2.1 us -> none  [on_device(): ready = exchange(ready.astype(jnp.bfloat16), 'rows', 0)]
  transfers between devices with their start and end apart: 13 -> 13, of which waited for: 4 -> 5; matrix products, arithmetic and copies ran while one was open for 64% -> 7% of each run, Pallas kernels for 0% -> 16%
where the time goes in v2:
time: 53.4 us; the launch traced here: 53.1 us
  starting transfers between devices  20.3 us (38%)
  Pallas kernels  14.1 us (26%)
  waiting for transfers between devices  12.2 us (23%)
  local copies, waits for them, and re-layouts  3.62 us (7%)
  other arithmetic  2.53 us (5%)
    ppermute x10, starting transfers between devices, exchange(): return lax.ppermute(array, (axis, 'sub'), pairs)  19.7 us
    pallas_call x5, Pallas kernels, call(): pl.pallas_call(kernel, out_shape=jax.ShapeDtypeStruct((rows, pixels), jnp...  14.1 us
    ppermute x10, waiting for transfers between devices, exchange(): return lax.ppermute(array, (axis, 'sub'), pairs)  11.1 us
    unnamed x10, local copies, waits for them, and re-layouts  2.38 us
    dynamic_slice x1, local copies, waits for them, and re-layouts, on_device(): lax.dynamic_slice(convergence, (0, c * width, sub * half, 0), (tile_rows,...  1.17 us
    ppermute x3, waiting for transfers between devices, swap_sub(): return lax.ppermute(array, 'sub', [(s, subs - 1 - s) for s in range(subs)])  1.12 us
  transfers between devices with their start and end apart: 13, of which 5 were waited for; matrix products, arithmetic and copies ran while one was open for 7% of the time, Pallas kernels for 16%

profile of v2, /device:TPU:0, one launch (start us, length us, event | category | flops | bytes accessed | tf_op | source)
XLA Modules:
  0.0 53.1 jit_solution(2500121172208513474)
XLA Ops:
  0.0 1.2 %constant_dynamic-slice_fusion.1 = (bf16[4,8,8,512]{3,2,1,0:T(8,128)(2,1)S(1)}, bf16[4,8,8,512]{3,2,1,0:T(8,128)(2,1)S(1)}) fusion(bf16[4,16,16,512]{3,2,1,0:T(8,128)(2,1)} %param.6, s32[]{:T(128)S(6)} %select_n.59), kind=kLoop, calls=%fused_computation.25 | loop fusion | bytes 1048580 | tf_op jit(solution)/shard_map/dynamic_slice | solution.py:198
  1.2 0.5 collective-permute-start.4
  1.7 4.2 %collective-permute-start.2 = (bf16[256,512]{1,0:T(8,128)(2,1)S(1)}, bf16[256,512]{1,0:T(8,128)(2,1)S(1)}, u32[]{:S(2)}, u32[]{:S(2)}) collective-permute-start(bf16[256,512]{1,0:T(8,128)(2,1)S(1)} %bitcast.14), channel_id=1, source_target_pairs={{0,4},{1,5},{4,0},{5,1},{8,12},{9,13},{12,8},{13,9},{2,6},{3,7},{6... | collective-permute-start | bytes 786440 | tf_op jit(solution)/shard_map/ppermute | solution.py:26
  5.9 0.8 %copy.25 = s32[4,16,2]{2,1,0:T(8,128)S(1)} copy(s32[4,16,2]{1,2,0:T(2,128)} %param.9) | data formatting | bytes 1024 | tf_op args[3]
  6.6 0.0 collective-permute-start
  6.7 0.1 collective-permute-start.9
  6.8 0.5 collective-permute-start.7
  7.3 0.8 %slice_compare_fusion.1 = (pred[4,8]{1,0:T(4,128)(4,1)S(1)}, pred[4,8]{1,0:T(4,128)(4,1)S(1)}) fusion(s32[4,16]{1,0:T(4,128)} %param.7), kind=kLoop, calls=%fused_computation.23 | loop fusion | flops 64 | bytes 320 | tf_op jit(solution)/shard_map/eq | solution.py:278
  8.1 0.9 %dynamic-slice_select_fusion = bf16[4,2,8,512]{3,2,1,0:T(8,128)(2,1)S(1)} fusion(bf16[4,16,16,512]{3,2,1,0:T(8,128)(2,1)} %param.6, s32[]{:T(128)S(6)} %select_n.59, s32[]{:T(128)S(6)} %add.48, pred[]{:T(512)S(6)} %eq.22), kind=kLoop, calls=%fused_computation.8 | loop fusion | flops 32768 | bytes 196617 | tf_op jit(solution)/shard_map/jit(_where)/select_n | solution.py:230
  9.0 0.8 %copy.26 = s32[4,16,4]{2,1,0:T(8,128)S(1)} copy(s32[4,16,4]{1,2,0:T(4,128)} %param.8) | data formatting | bytes 2048 | tf_op args[2]
  9.8 2.8 %collective-permute-done = s32[4,16,2]{2,1,0:T(8,128)S(1)} collective-permute-done((s32[4,16,2]{2,1,0:T(8,128)S(1)}, s32[4,16,2]{2,1,0:T(8,128)S(1)}, u32[]{:S(2)}, u32[]{:S(2)}) %collective-permute-start) | collective-permute-done | bytes 544 | tf_op jit(solution)/shard_map/ppermute | solution.py:26
  12.6 0.1 pad_add_fusion
  12.7 0.1 collective-permute-start.1
  12.7 0.1 pad_add_fusion.4.position
  12.8 1.1 %collective-permute-done.1 = s32[4,16,8]{2,1,0:T(8,128)S(1)} collective-permute-done((s32[4,16,8]{2,1,0:T(8,128)S(1)}, s32[4,16,8]{2,1,0:T(8,128)S(1)}, u32[]{:S(2)}, u32[]{:S(2)}) %collective-permute-start.1) | collective-permute-done | bytes 2080 | tf_op jit(solution)/shard_map/ppermute | solution.py:31
  13.9 0.2 collective-permute-start.5
  14.1 0.1 fusion.5
  14.2 0.1 fusion.2.index
  14.3 0.1 pad_add_fusion.3.requests
  14.4 1.1 %collective-permute-done.5.refs_5_.refs_2_ = bf16[256,512]{1,0:T(8,128)(2,1)S(1)} collective-permute-done((bf16[256,512]{1,0:T(8,128)(2,1)S(1)}, bf16[256,512]{1,0:T(8,128)(2,1)S(1)}, u32[]{:S(2)}, u32[]{:S(2)}) %collective-permute-start.5) | collective-permute-done | bytes 262176 | tf_op jit(solution)/shard_map/ppermute | solution.py:26
  15.5 8.6 %collective-permute-start.3 = (bf16[256,512]{1,0:T(8,128)(2,1)S(1)}, bf16[256,512]{1,0:T(8,128)(2,1)S(1)}, u32[]{:S(2)}, u32[]{:S(2)}) collective-permute-start(bf16[256,512]{1,0:T(8,128)(2,1)S(1)} %bitcast.20), channel_id=1, source_target_pairs={{0,4},{1,5},{4,0},{5,1},{8,12},{9,13},{12,8},{13,9},{2,6},{3,7},{6... | collective-permute-start | bytes 786440 | tf_op jit(solution)/shard_map/ppermute | solution.py:26
  24.0 0.1 pad_add_fusion.2.requests
  24.1 0.0 collective-permute-done.2.refs_2_.refs_1_.refs_4_
  24.1 0.1 collective-permute-start.8
  24.2 0.0 collective-permute-done.4.refs_4_.refs_2_
  24.2 5.6 %collective-permute-done.3.refs_3_.refs_1_.refs_4_ = bf16[256,512]{1,0:T(8,128)(2,1)S(1)} collective-permute-done((bf16[256,512]{1,0:T(8,128)(2,1)S(1)}, bf16[256,512]{1,0:T(8,128)(2,1)S(1)}, u32[]{:S(2)}, u32[]{:S(2)}) %collective-permute-start.3) | collective-permute-done | bytes 262176 | tf_op jit(solution)/shard_map/ppermute | solution.py:26
  29.8 0.0 collective-permute-start.11
  29.9 0.0 collective-permute-done.8.refs_3_
  29.9 0.0 collective-permute-done.9.refs_6_
  29.9 0.0 copy-done
  29.9 2.2 %shard_map.65 = bf16[256,512]{1,0:T(8,128)(2,1)S(1)} custom-call(s32[2]{0:T(128)S(1)} %pad_add_fusion.4.position, s32[4,16,4]{2,1,0:T(8,128)S(1)} %pad_add_fusion.2.requests, bf16[256,512]{1,0:T(8,128)(2,1)S(1)} %bitcast.15, bf16[256,512]{1,0:T(8,128)(2,1)S(1)} %collective-permute-done.2.refs_2_.refs_1_.refs_4_, ...), custom_call_target="tpu_custom_call" | custom-call | flops 536870912 | bytes 3670016 | tf_op jit(solution)/shard_map/pallas_call | solution.py:40
  32.1 2.6 %collective-permute-start.10 = (bf16[256,512]{1,0:T(8,128)(2,1)S(1)}, bf16[256,512]{1,0:T(8,128)(2,1)S(1)}, u32[]{:S(2)}, u32[]{:S(2)}) collective-permute-start(bf16[256,512]{1,0:T(8,128)(2,1)S(1)} %shard_map.65), channel_id=1, source_target_pairs={{0,4},{1,5},{4,0},{5,1},{8,12},{9,13},{12,8},{13,9},{2,6},{3,7},{6... | collective-permute-start | bytes 786440 | tf_op jit(solution)/shard_map/ppermute | solution.py:26
  34.7 1.6 %collective-permute-start.6 = (bf16[192,512]{1,0:T(8,128)(2,1)S(1)}, bf16[192,512]{1,0:T(8,128)(2,1)S(1)}, u32[]{:S(2)}, u32[]{:S(2)}) collective-permute-start(bf16[192,512]{1,0:T(8,128)(2,1)S(1)} %bitcast.33), channel_id=1, source_target_pairs={{0,2},{1,3},{2,0},{3,1},{4,6},{5,7},{6,4},{7,5},{8,10},{9,11},{10,... | collective-permute-start | bytes 589832 | tf_op jit(solution)/shard_map/ppermute | solution.py:26
  36.3 0.0 collective-permute-done.11.refs_3_
  36.3 2.2 %shard_map.67 = bf16[256,512]{1,0:T(8,128)(2,1)S(1)} custom-call(s32[2]{0:T(128)S(1)} %pad_add_fusion.4.position, s32[4,16,4]{2,1,0:T(8,128)S(1)} %pad_add_fusion.2.requests, bf16[256,512]{1,0:T(8,128)(2,1)S(1)} %bitcast.21, bf16[256,512]{1,0:T(8,128)(2,1)S(1)} %collective-permute-done.3.refs_3_.refs_1_.refs_4_, ...), custom_call_target="tpu_custom_call" | custom-call | flops 536870912 | bytes 3670016 | tf_op jit(solution)/shard_map/pallas_call | solution.py:40
  38.5 2.0 %collective-permute-start.12 = (bf16[256,512]{1,0:T(8,128)(2,1)S(1)}, bf16[256,512]{1,0:T(8,128)(2,1)S(1)}, u32[]{:S(2)}, u32[]{:S(2)}) collective-permute-start(bf16[256,512]{1,0:T(8,128)(2,1)S(1)} %shard_map.67), channel_id=1, source_target_pairs={{0,4},{1,5},{4,0},{5,1},{8,12},{9,13},{12,8},{13,9},{2,6},{3,7},{6... | collective-permute-start | bytes 786440 | tf_op jit(solution)/shard_map/ppermute | solution.py:26
  40.5 2.2 %shard_map.68 = bf16[256,512]{1,0:T(8,128)(2,1)S(1)} custom-call(s32[2]{0:T(128)S(1)} %pad_add_fusion.4.position, s32[4,16,4]{2,1,0:T(8,128)S(1)} %pad_add_fusion.3.requests, bf16[256,512]{1,0:T(8,128)(2,1)S(1)} %bitcast.22, bf16[256,512]{1,0:T(8,128)(2,1)S(1)} %collective-permute-done.3.refs_3_.refs_1_.refs_4_, ...), custom_call_target="tpu_custom_call" | custom-call | flops 536870912 | bytes 3670016 | tf_op jit(solution)/shard_map/pallas_call | solution.py:40
  42.6 0.0 copy-start.1
  42.7 2.2 %shard_map.66 = bf16[256,512]{1,0:T(8,128)(2,1)S(1)} custom-call(s32[2]{0:T(128)S(1)} %pad_add_fusion.4.position, s32[4,16,4]{2,1,0:T(8,128)S(1)} %pad_add_fusion.3.requests, bf16[256,512]{1,0:T(8,128)(2,1)S(1)} %bitcast.16, bf16[256,512]{1,0:T(8,128)(2,1)S(1)} %collective-permute-done.2.refs_2_.refs_1_.refs_4_, ...), custom_call_target="tpu_custom_call" | custom-call | flops 536870912 | bytes 3670016 | tf_op jit(solution)/shard_map/pallas_call | solution.py:40
  44.9 0.0 collective-permute-done.10
  44.9 1.6 %collective-permute-done.12 = bf16[256,512]{1,0:T(8,128)(2,1)S(1)} collective-permute-done((bf16[256,512]{1,0:T(8,128)(2,1)S(1)}, bf16[256,512]{1,0:T(8,128)(2,1)S(1)}, u32[]{:S(2)}, u32[]{:S(2)}) %collective-permute-start.12) | collective-permute-done | bytes 262176 | tf_op jit(solution)/shard_map/ppermute | solution.py:26
  46.5 0.0 copy-start.2
  46.5 0.0 collective-permute-done.6.refs_6_
  46.5 0.0 collective-permute-done.7.refs_8_
  46.6 5.4 %shard_map.64 = bf16[512,512]{1,0:T(8,128)(2,1)S(1)} custom-call(s32[2]{0:T(128)S(1)} %pad_add_fusion.4.position, s32[4,16,8]{2,1,0:T(8,128)S(1)} %fusion.2.index, bf16[256,512]{1,0:T(8,128)(2,1)S(1)} %bitcast.18, bf16[256,512]{1,0:T(8,128)(2,1)S(1)} %bitcast.24, bf16[256,512]{1,0:T(8,128)(2,1)S(1)} %collective-permute-done.2.refs_2_.refs_1_.refs_4_, ...), custom_call_target="tpu_custom_call" | custom-call | flops 2147483648 | bytes 6488064 | tf_op jit(solution)/shard_map/pallas_call | solution.py:40
  52.0 0.3 slice_select_fusion.1
  52.3 0.0 copy-start.3
  52.3 0.8 %copy-done.3 = bf16[4,16,8,512]{3,2,1,0:T(8,128)(2,1)} copy-done((bf16[4,16,8,512]{3,2,1,0:T(8,128)(2,1)}, bf16[4,16,8,512]{3,2,1,0:T(8,128)(2,1)S(1)}, u32[]{:S(2)}) %copy-start.3) | copy-done | bytes 524312
  (9 shorter events, 0.1 us)
Async XLA Ops:
  0.0 29.9 %copy-start = (bf16[512,1024]{1,0:T(8,128)(2,1)S(1)}, bf16[512,1024]{1,0:T(8,128)(2,1)}, u32[]{:S(2)}) copy-start(bf16[512,1024]{1,0:T(8,128)(2,1)} %refs_5_.7) | copy-start | bytes 3145732
  1.2 23.0 %collective-permute-start.4 = (bf16[256,512]{1,0:T(8,128)(2,1)S(1)}, bf16[256,512]{1,0:T(8,128)(2,1)S(1)}, u32[]{:S(2)}, u32[]{:S(2)}) collective-permute-start(bf16[256,512]{1,0:T(8,128)(2,1)S(1)} %bitcast.13), channel_id=1, source_target_pairs={{0,1},{1,0},{4,8},{5,9},{8,4},{9,5},{12,13},{13,12},{2,3},{3,2},{6... | collective-permute-start | bytes 786440 | tf_op jit(solution)/shard_map/ppermute | solution.py:26
  1.7 22.4 %collective-permute-start.2 = (bf16[256,512]{1,0:T(8,128)(2,1)S(1)}, bf16[256,512]{1,0:T(8,128)(2,1)S(1)}, u32[]{:S(2)}, u32[]{:S(2)}) collective-permute-start(bf16[256,512]{1,0:T(8,128)(2,1)S(1)} %bitcast.14), channel_id=1, source_target_pairs={{0,4},{1,5},{4,0},{5,1},{8,12},{9,13},{12,8},{13,9},{2,6},{3,7},{6... | collective-permute-start | bytes 786440 | tf_op jit(solution)/shard_map/ppermute | solution.py:26
  6.6 5.9 %collective-permute-start = (s32[4,16,2]{2,1,0:T(8,128)S(1)}, s32[4,16,2]{2,1,0:T(8,128)S(1)}, u32[]{:S(2)}, u32[]{:S(2)}) collective-permute-start(s32[4,16,2]{2,1,0:T(8,128)S(1)} %copy.25), channel_id=1, source_target_pairs={{0,4},{1,5},{4,0},{5,1},{8,12},{9,13},{12,8},{13,9},{2,6},{3,7},{6... | collective-permute-start | bytes 1544 | tf_op jit(solution)/shard_map/ppermute | solution.py:26
  6.7 23.2 %collective-permute-start.9 = (bf16[512,1024]{1,0:T(8,128)(2,1)}, bf16[512,1024]{1,0:T(8,128)(2,1)S(1)}, u32[]{:S(2)}, u32[]{:S(2)}) collective-permute-start(bf16[512,1024]{1,0:T(8,128)(2,1)} %refs_5_.7), channel_id=1, source_target_pairs={{0,1},{1,0},{2,3},{3,2},{4,5},{5,4},{6,7},{7,6},{8,9},{9,8},{10,11... | collective-permute-start | bytes 3145736 | tf_op jit(solution)/shard_map/ppermute | solution.py:31
  6.8 39.8 %collective-permute-start.7 = (bf16[512,2048]{1,0:T(8,128)(2,1)}, bf16[512,2048]{1,0:T(8,128)(2,1)}, u32[]{:S(2)}, u32[]{:S(2)}) collective-permute-start(bf16[512,2048]{1,0:T(8,128)(2,1)} %refs_7_.1), channel_id=1, source_target_pairs={{0,1},{1,0},{2,3},{3,2},{4,5},{5,4},{6,7},{7,6},{8,9},{9,8},{10,11... | collective-permute-start | bytes 6291464 | tf_op jit(solution)/shard_map/ppermute | solution.py:31
  12.7 1.3 %collective-permute-start.1 = (s32[4,16,8]{2,1,0:T(8,128)S(1)}, s32[4,16,8]{2,1,0:T(8,128)S(1)}, u32[]{:S(2)}, u32[]{:S(2)}) collective-permute-start(s32[4,16,8]{2,1,0:T(8,128)S(1)} %pad_add_fusion), channel_id=1, source_target_pairs={{0,1},{1,0},{2,3},{3,2},{4,5},{5,4},{6,7},{7,6},{8,9},{9,8},{10,11... | collective-permute-start | bytes 6152 | tf_op jit(solution)/shard_map/ppermute | solution.py:31
  13.9 1.5 %collective-permute-start.5 = (bf16[256,512]{1,0:T(8,128)(2,1)S(1)}, bf16[256,512]{1,0:T(8,128)(2,1)S(1)}, u32[]{:S(2)}, u32[]{:S(2)}) collective-permute-start(bf16[256,512]{1,0:T(8,128)(2,1)S(1)} %bitcast.19), channel_id=1, source_target_pairs={{0,1},{1,0},{4,8},{5,9},{8,4},{9,5},{12,13},{13,12},{2,3},{3,2},{6... | collective-permute-start | bytes 786440 | tf_op jit(solution)/shard_map/ppermute | solution.py:26
  15.5 14.4 %collective-permute-start.3 = (bf16[256,512]{1,0:T(8,128)(2,1)S(1)}, bf16[256,512]{1,0:T(8,128)(2,1)S(1)}, u32[]{:S(2)}, u32[]{:S(2)}) collective-permute-start(bf16[256,512]{1,0:T(8,128)(2,1)S(1)} %bitcast.20), channel_id=1, source_target_pairs={{0,4},{1,5},{4,0},{5,1},{8,12},{9,13},{12,8},{13,9},{2,6},{3,7},{6... | collective-permute-start | bytes 786440 | tf_op jit(solution)/shard_map/ppermute | solution.py:26
  24.1 5.7 %collective-permute-start.8 = (bf16[256,512]{1,0:T(8,128)(2,1)S(1)}, bf16[256,512]{1,0:T(8,128)(2,1)S(1)}, u32[]{:S(2)}, u32[]{:S(2)}) collective-permute-start(bf16[256,512]{1,0:T(8,128)(2,1)S(1)} %collective-permute-done.2.refs_2_.refs_1_.refs_4_), channel_id=1, source_target_pairs={{0,1},{1,0},{4,8},{5,9},{8,4},{9,5},{12,13},{13,12},{2,3},{3,2},{6... | collective-permute-start | bytes 786440 | tf_op jit(solution)/shard_map/ppermute | solution.py:26
  29.8 6.4 %collective-permute-start.11 = (bf16[256,512]{1,0:T(8,128)(2,1)S(1)}, bf16[256,512]{1,0:T(8,128)(2,1)S(1)}, u32[]{:S(2)}, u32[]{:S(2)}) collective-permute-start(bf16[256,512]{1,0:T(8,128)(2,1)S(1)} %collective-permute-done.3.refs_3_.refs_1_.refs_4_), channel_id=1, source_target_pairs={{0,1},{1,0},{4,8},{5,9},{8,4},{9,5},{12,13},{13,12},{2,3},{3,2},{6... | collective-permute-start | bytes 786440 | tf_op jit(solution)/shard_map/ppermute | solution.py:26
  32.1 12.8 %collective-permute-start.10 = (bf16[256,512]{1,0:T(8,128)(2,1)S(1)}, bf16[256,512]{1,0:T(8,128)(2,1)S(1)}, u32[]{:S(2)}, u32[]{:S(2)}) collective-permute-start(bf16[256,512]{1,0:T(8,128)(2,1)S(1)} %shard_map.65), channel_id=1, source_target_pairs={{0,4},{1,5},{4,0},{5,1},{8,12},{9,13},{12,8},{13,9},{2,6},{3,7},{6... | collective-permute-start | bytes 786440 | tf_op jit(solution)/shard_map/ppermute | solution.py:26
  34.7 11.8 %collective-permute-start.6 = (bf16[192,512]{1,0:T(8,128)(2,1)S(1)}, bf16[192,512]{1,0:T(8,128)(2,1)S(1)}, u32[]{:S(2)}, u32[]{:S(2)}) collective-permute-start(bf16[192,512]{1,0:T(8,128)(2,1)S(1)} %bitcast.33), channel_id=1, source_target_pairs={{0,2},{1,3},{2,0},{3,1},{4,6},{5,7},{6,4},{7,5},{8,10},{9,11},{10,... | collective-permute-start | bytes 589832 | tf_op jit(solution)/shard_map/ppermute | solution.py:26
  38.5 8.0 %collective-permute-start.12 = (bf16[256,512]{1,0:T(8,128)(2,1)S(1)}, bf16[256,512]{1,0:T(8,128)(2,1)S(1)}, u32[]{:S(2)}, u32[]{:S(2)}) collective-permute-start(bf16[256,512]{1,0:T(8,128)(2,1)S(1)} %shard_map.67), channel_id=1, source_target_pairs={{0,4},{1,5},{4,0},{5,1},{8,12},{9,13},{12,8},{13,9},{2,6},{3,7},{6... | collective-permute-start | bytes 786440 | tf_op jit(solution)/shard_map/ppermute | solution.py:26
  42.6 3.9 %copy-start.1 = (bf16[512,2048]{1,0:T(8,128)(2,1)S(1)}, bf16[512,2048]{1,0:T(8,128)(2,1)}, u32[]{:S(2)}) copy-start(bf16[512,2048]{1,0:T(8,128)(2,1)} %refs_7_.1) | copy-start | bytes 6291460
  46.5 5.5 %copy-start.2 = (bf16[4,16,8,512]{3,2,1,0:T(8,128)(2,1)S(1)}, bf16[4,16,8,512]{3,2,1,0:T(8,128)(2,1)}, u32[]{:S(2)}) copy-start(bf16[4,16,8,512]{3,2,1,0:T(8,128)(2,1)} %custom-call) | copy-start | bytes 1572868
  52.3 0.8 %copy-start.3 = (bf16[4,16,8,512]{3,2,1,0:T(8,128)(2,1)}, bf16[4,16,8,512]{3,2,1,0:T(8,128)(2,1)S(1)}, u32[]{:S(2)}) copy-start(bf16[4,16,8,512]{3,2,1,0:T(8,128)(2,1)S(1)} %get-tuple-element.39) | copy-start | bytes 1572868

commit v3 on v0

v3 whole, which is shorter than its diff:
```python
import functools

import jax
import jax.numpy as jnp
from jax import lax
from jax.experimental import pallas as pl
from jax.experimental.pallas import tpu as pltpu
from jax.sharding import PartitionSpec as P

REACH = 2
PARTS = (1, 1)
VMEM_BYTES = 48 * 2**20
CONTRACT_LAST = (((1,), (1,)), ((), ()))


def exchange(array, axis, parity):
    count, subs = lax.axis_size(axis), lax.axis_size("sub")
    partner = list(range(count))
    for i in range(parity, count - 1, 2):
        partner[i], partner[i + 1] = i + 1, i
    pairs = []
    for i in range(count):
        for s in range(subs):
            other = s if partner[i] != i else subs - 1 - s
            pairs.append((i * subs + s, partner[i] * subs + other))
    return lax.ppermute(array, (axis, "sub"), pairs)


def swap_sub(array):
    subs = lax.axis_size("sub")
    return lax.ppermute(array, "sub", [(s, subs - 1 - s) for s in range(subs)])


def after(arrays, *first):
    return lax.optimization_barrier((tuple(arrays), first))[0]


def call(kernel, rows, pixels, ints, arrays, scratch, outputs=1):
    shape = jax.ShapeDtypeStruct((rows, pixels), jnp.bfloat16)
    vmem, smem = (pl.BlockSpec(memory_space=space) for space in (pltpu.VMEM, pltpu.SMEM))
    return pl.pallas_call(
        kernel,
        out_shape=[shape] * outputs,
        in_specs=[smem] * len(ints) + [vmem] * len(arrays),
        out_specs=[vmem] * outputs,
        scratch_shapes=scratch,
        compiler_params=pltpu.CompilerParams(vmem_limit_bytes=VMEM_BYTES),
    )(*ints, *arrays)


class Tile:
    def __init__(self, rows, cols, tile_rows, tile_cols, half, pixels):
        self.rows, self.cols = rows, cols
        self.tile_rows, self.tile_cols = tile_rows, tile_cols
        self.half, self.pixels = half, pixels
        self.split = tile_rows // 2
        self.units = tile_cols // REACH
        self.group = REACH * half
        self.unit = self.split * self.group
        self.wide = tile_cols + 2 * REACH

    def read(self, pieces, flag, row, unit, g):
        at = unit * self.unit + (g % self.split) * self.group
        first, second = (p[at : at + self.group, :].astype(jnp.float32) for p in pieces)
        later = row % 2 == flag
        return jnp.where(later, *((first, second) if g >= self.split else (second, first)))

    def blocks(self, value):
        return value.reshape(REACH, self.half, self.pixels)

    def gather(self, blocks, chosen, base, index_of, units, slots):
        def one_row(g, carry):
            for unit in range(units):
                at = pl.multiple_of(base + (unit * self.tile_rows + g) * self.group, self.group)
                for k in range(slots):
                    pair = [blocks[index_of(g, unit * REACH + i, k)] for i in range(REACH)]
                    chosen[pl.ds(at, self.group), k * self.pixels : (k + 1) * self.pixels] = (
                        jnp.concatenate(pair, axis=0).astype(jnp.bfloat16)
                    )
            return carry

        lax.fori_loop(0, self.tile_rows, one_row, 0)


def product(chosen, factors):
    total = None
    start = 0
    for factor in factors:
        depth = factor.shape[1]
        term = lax.dot_general(
            chosen[:, start : start + depth], factor[...], CONTRACT_LAST,
            preferred_element_type=jnp.float32,
        )
        total = term if total is None else total + term
        start += depth
    return total


def far_kernel(tile, names, first, units, wanted, slots, ints, *refs):
    row = lax.axis_index("rows")
    sign = jnp.where(row % 2 == 0, 1, -1)
    width = units * REACH
    shards = {}
    taken = 0
    for name, flag, start in names[:-1]:
        shards[name] = (refs[taken : taken + 2], flag, start)
        taken += 2
    size = units * tile.unit
    pieces = [refs[taken].at[pl.ds(at, size), :] for at in (0, size)]
    shards[names[-1][0]] = (pieces, *names[-1][1:])
    taken += 1
    own_half, other_half, *outs = refs[taken : taken + 2 + len(wanted)]
    blocks, chosen = refs[taken + 2 + len(wanted) :]
    for (parity, step), (pieces, flag, start) in shards.items():
        away = 0 if step < 0 else (1 + step) * (sign if parity == 0 else -sign)
        source = row + away
        source = jnp.where((source >= 0) & (source < tile.rows), source, tile.rows)
        for half, piece in enumerate(pieces):
            later = (row % 2 == flag) == (half == 0)
            base = source * tile.tile_rows + jnp.where(later, tile.split, 0)
            for unit in range(units):
                for g in range(tile.split):
                    at = (unit + first - start) * tile.unit + g * tile.group
                    value = piece[at : at + tile.group, :].astype(jnp.float32)
                    blocks[pl.ds((base + g) * width + unit * REACH, REACH)] = tile.blocks(value)

    count = tile.tile_rows * units * tile.group
    for n, (plane, _) in enumerate(wanted):

        def index_of(g, j, k):
            return ints[g, plane[k], first * REACH + j] * width + j

        tile.gather(blocks, chosen, n * count, index_of, units, 2 * slots)
    mean = product(chosen, (own_half, other_half))
    for n, (_, name) in enumerate(wanted):
        pieces, flag, start = shards[name]
        for unit in range(units):
            for g in range(tile.tile_rows):
                at = (unit * tile.tile_rows + g) * tile.group
                field = tile.read(pieces, flag, row, unit + first - start, g)
                value = field - mean[n * count + at : n * count + at + tile.group, :]
                outs[n][at : at + tile.group, :] = value.astype(jnp.bfloat16)


def halo(tile, row, even, odd, unit, r):
    above = r < REACH
    g = (tile.split - REACH + r) if above else (r - REACH - tile.tile_rows)
    at = unit * tile.unit + g * tile.group
    from_even, from_odd = (p[at : at + tile.group, :].astype(jnp.float32) for p in (even, odd))
    return jnp.where((row % 2 == 0) == above, from_odd, from_even)


def edge_kernel(tile, parity, first, second, even, odd, out):
    row, col = lax.axis_index("rows"), lax.axis_index("cols")
    for r in range(tile.tile_rows + 2 * REACH):
        sides = []
        for unit in (0, tile.units - 1):
            g = r - REACH
            if 0 <= g < tile.tile_rows:
                sides.append(tile.read((first, second), 0, row, unit, g))
            else:
                sides.append(halo(tile, row, even, odd, unit, r))
        value = jnp.where(col % 2 == parity, sides[1], sides[0])
        out[r * tile.group : (r + 1) * tile.group, :] = value.astype(jnp.bfloat16)


def near_kernel(tile, slots, sides, ints, first, second, even, odd, *refs):
    halos = refs[:sides]
    own_half, other_half, out, blocks, chosen = refs[sides:]
    row, col = lax.axis_index("rows"), lax.axis_index("cols")
    above, below = row > 0, row < tile.rows - 1
    wide, last = tile.wide, tile.tile_rows + REACH
    nothing = jnp.zeros((REACH, tile.half, tile.pixels), jnp.float32)
    for r in range(last + REACH):
        inside = above if r < REACH else below if r >= last else None
        for unit in range(tile.units):
            if inside is None:
                value = tile.read((first, second), 0, row, unit, r - REACH)
            else:
                value = jnp.where(inside, halo(tile, row, even, odd, unit, r), 0.0)
            blocks[pl.ds(r * wide + REACH + unit * REACH, REACH)] = tile.blocks(value)
        left, right = nothing, nothing
        for parity in range(sides):
            value = halos[parity][r * tile.group : (r + 1) * tile.group, :].astype(jnp.float32)
            if inside is not None:
                value = jnp.where(inside, value, 0.0)
            value = tile.blocks(value)
            on_right = col % 2 == parity
            right = jnp.where(on_right & (col < tile.cols - 1), value, right)
            left = jnp.where(jnp.logical_not(on_right) & (col > 0), value, left)
        blocks[pl.ds(r * wide, REACH)] = left
        blocks[pl.ds(r * wide + REACH + tile.tile_cols, REACH)] = right

    def index_of(g, j, k):
        return ints[g, k, j]

    tile.gather(blocks, chosen, 0, index_of, tile.units, 2 * slots)
    mean = product(chosen, (own_half, other_half))
    for unit in range(tile.units):
        for g in range(tile.tile_rows):
            at = (unit * tile.tile_rows + g) * tile.group
            value = tile.read((first, second), 0, row, unit, g) - mean[at : at + tile.group, :]
            out[at : at + tile.group, :] = value.astype(jnp.bfloat16)


def pick_kernel(tile, parts, level, near, *refs):
    ready, own, out = refs[: len(parts)], refs[len(parts) : 2 * len(parts)], refs[-1]
    row = lax.axis_index("rows")
    at_end = (row == 0) | (row == tile.rows - 1)
    lower = lax.broadcasted_iota(jnp.int32, (tile.group, tile.pixels), 0) // tile.half
    first = 0
    for c, units in enumerate(parts):
        for unit in range(units):
            for g in range(tile.tile_rows):
                at = (unit * tile.tile_rows + g) * tile.group
                far = [x[c][at : at + tile.group, :].astype(jnp.float32) for x in (ready, own)]
                far = jnp.where(at_end, *far)
                at = ((first + unit) * tile.tile_rows + g) * tile.group
                fine = near[at : at + tile.group, :].astype(jnp.float32)
                levels = level[g, (first + unit) * REACH]
                for i in range(1, REACH):
                    levels = jnp.where(lower == i, level[g, (first + unit) * REACH + i], levels)
                at = (g * tile.units + first + unit) * tile.group
                out[at : at + tile.group, :] = jnp.where(levels == 1, fine, far).astype(jnp.bfloat16)
        first += units


def on_device(convergence, block_level, near_codes, far_rows, near_factor, far_factor):
    tile_rows, tile_cols, samples, pixels = convergence.shape
    rows, cols = lax.axis_size("rows"), lax.axis_size("cols")
    row, sub = lax.axis_index("rows"), lax.axis_index("sub")
    half = samples // lax.axis_size("sub")
    near_slots, far_slots = near_codes.shape[2], far_rows.shape[2]
    tile = Tile(rows, cols, tile_rows, tile_cols, half, pixels)
    parts = [tile.units * part // sum(PARTS) for part in PARTS]
    starts = [sum(parts[:c]) for c in range(len(parts))]

    own = []
    for later in (row % 2 == 0, row % 2 != 0):
        start = jnp.where(later, tile.split, 0)
        piece = lax.dynamic_slice(
            convergence, (start, 0, sub * half, 0), (tile.split, tile_cols, half, pixels)
        ).reshape(tile.split, tile.units, REACH, half, pixels)
        own.append(jnp.transpose(piece, (1, 0, 2, 3, 4)).reshape(-1, pixels))

    requests = jnp.transpose(far_rows, (0, 2, 1))
    partners = exchange(requests, "rows", 0)
    far_other = swap_sub(far_factor)
    near_other = swap_sub(near_factor)

    first = exchange(own[0], "rows", 0)
    side = exchange(own[1], "rows", 1)
    held = after(own, partners, far_other, near_other)
    even = [[first, exchange(held[1], "rows", 0)]]
    odd = [[side, exchange(held[0], "rows", 1)]]

    beside = [*own, even[0][0], odd[0][0]]
    edges = [
        call(
            functools.partial(edge_kernel, tile, parity),
            (tile_rows + 2 * REACH) * tile.group, pixels, [], beside, [],
        )[0]
        for parity in range(min(cols - 1, 2))
    ]
    halos = [exchange(edge, "cols", parity) for parity, edge in enumerate(edges)]

    near_index = jnp.transpose(near_codes, (0, 2, 1))
    near_index = near_index + (tile.wide - 2 * REACH - 1) * (near_index // (2 * REACH + 1))
    near_index = near_index + tile.wide * jnp.arange(tile_rows, dtype=jnp.int32)[:, None, None]
    near_index = near_index + jnp.arange(tile_cols, dtype=jnp.int32)[None, None, :]
    codes = jnp.concatenate([near_index, requests, partners], axis=1)
    other = swap_sub(codes)
    near_ints = jnp.concatenate([near_index, other[:, :near_slots]], axis=1)
    far_ints = jnp.concatenate([codes[:, near_slots:], other[:, near_slots:]], axis=1)

    inner = rows > 4
    for step in range(1, rows - 3):
        if inner:
            even.append([exchange(x, "rows", 0) for x in odd[step - 1]])
        odd.append([exchange(x, "rows", 1) for x in even[step - 1]])
    source = after(even[rows - 4], near_ints, far_ints, *halos)
    last = []
    for start, units in zip(starts, parts):
        spots = slice(start * tile.unit, (start + units) * tile.unit)
        last.append(exchange(jnp.concatenate([x[spots] for x in source], axis=0), "rows", 1))

    size = tile_rows * tile_cols * half
    (near_own,) = call(
        functools.partial(near_kernel, tile, near_slots, len(halos)),
        size, pixels, [near_ints], [*beside, *halos, near_factor, near_other],
        [
            pltpu.VMEM(((tile_rows + 2 * REACH) * tile.wide, half, pixels), jnp.float32),
            pltpu.VMEM((size, 2 * near_slots * pixels), jnp.bfloat16),
        ],
    )

    def far_chunk(c, wanted, *before):
        names, arrays = [((0, -1), 0, 0)], [*own]
        for step in range(len(odd)):
            if step < len(even):
                names.append(((0, step), 1, 0))
                arrays += even[step]
            names.append(((1, step), 0, 0))
            arrays += odd[step]
        final = len(odd)
        names.append(((1, final), 0, starts[c]))
        arrays.append(last[c])
        if before:
            arrays = list(after(arrays[:1], *before)) + arrays[1:]
        here = tile_rows * parts[c] * tile.group
        return call(
            functools.partial(far_kernel, tile, names, starts[c], parts[c], wanted, far_slots),
            here, pixels, [far_ints], [*arrays, far_factor, far_other],
            [
                pltpu.VMEM(((rows + 1) * tile_rows * parts[c] * REACH, half, pixels), jnp.float32),
                pltpu.VMEM((len(wanted) * here, 2 * far_slots * pixels), jnp.bfloat16),
            ],
            len(wanted),
        )

    slots = [k + 2 * far_slots * s for s in range(2) for k in range(far_slots)]
    partner = ([far_slots + k for k in slots], (0, 0))
    mine = (slots, (0, -1))
    ready, far_own = [], []
    sent = near_own
    for c in range(len(parts)):
        if c < len(parts) - 1:
            sent, kept = far_chunk(c, [partner, mine], sent)
        else:
            (sent,) = far_chunk(c, [partner], sent)
            (kept,) = far_chunk(c, [mine])
        ready.append(exchange(sent, "rows", 0))
        far_own.append(kept)
    (result,) = call(
        functools.partial(pick_kernel, tile, parts),
        size, pixels, [block_level], [near_own, *ready, *far_own], [],
    )
    return result.reshape(tile_rows, tile_cols, half, pixels)


def solution(mesh):
    placed = (
        P(("fields", "rows"), "cols", None, None),
        P(("fields", "rows"), "cols"),
        P(("fields", "rows"), "cols", "sub"),
        P(("fields", "rows"), "cols", "sub"),
        P(None, "sub"),
        P(None, "sub"),
    )
    return jax.shard_map(
        on_device,
        mesh=mesh,
        in_specs=placed,
        out_specs=P(("fields", "rows"), "cols", "sub", None),
        check_vma=False,
    )
```

time: 127 us -> 44.9 us (0.35)
  waiting for transfers between devices: 75.1 us -> 17.5 us
  between operations: 13.6 us -> 0.2 us
  Pallas kernels: 0 us -> 12.8 us
  local copies, waits for them, and re-layouts: 11.6 us -> 1.17 us
  other arithmetic: 9.03 us -> 0.15 us
  matrix products: 4.99 us -> 0 us
    all_gather x1 -> x0, waiting for transfers between devices: 38.5 us -> none  [on_device(): piece = lax.all_gather(convergence, 'rows', axis=0, tiled=True)]
    pallas_call x0 -> x6, Pallas kernels: none -> 12.8 us  [call(): pl.pallas_call(kernel, out_shape=[shape] * outputs, in_specs=[smem] * len...]
    reduce_scatter x1 -> x0, waiting for transfers between devices: 11.9 us -> none  [on_device(): lax.psum_scatter(partial_value, 'sub', scatter_dimension=1, tiled=True)]
    ppermute x4 -> x13, waiting for transfers between devices: 24 us -> 17.5 us  [the longest x10 17.5 us: exchange(): return lax.ppermute(array, (axis, 'sub'), pairs)]
    gather x2 -> x0, local copies, waits for them, and re-layouts: 5.68 us -> none  [the longest x1 2.87 us: on_device(): found = jnp.take(flat_piece, local, axis=0)]
    dot_general x2 -> x0, matrix products: 4.99 us -> none  [the longest x1 3.7 us: on_device(): lax.dot_general(near_blocks, near_factor.reshape(pixels, near_slots, pixe...]
    select_n x4 -> x0, other arithmetic: 4.83 us -> none  [the longest x2 4.09 us: on_device(): jnp.take(flat_ext, near_index.reshape(-1), axis=0)]
    unnamed x20 -> x10, local copies, waits for them, and re-layouts: 3.55 us -> 0.03 us
  transfers between devices with their start and end apart: 6 -> 13, of which waited for: 5 -> 6; matrix products, arithmetic and copies ran while one was open for 9% -> 3% of each run, Pallas kernels for 0% -> 25%
where the time goes in v3:
time: 44.9 us; the launch traced here: 44.8 us
  waiting for transfers between devices  17.5 us (39%)
  starting transfers between devices  13 us (29%)
  Pallas kernels  12.8 us (29%)
  local copies, waits for them, and re-layouts  1.17 us (3%)
    ppermute x10, waiting for transfers between devices, exchange(): return lax.ppermute(array, (axis, 'sub'), pairs)  17.5 us
    pallas_call x6, Pallas kernels, call(): pl.pallas_call(kernel, out_shape=[shape] * outputs, in_specs=[smem] * len...  12.8 us
    ppermute x10, starting transfers between devices, exchange(): return lax.ppermute(array, (axis, 'sub'), pairs)  12.3 us
    dynamic_slice x1, local copies, waits for them, and re-layouts, on_device(): lax.dynamic_slice(convergence, (start, 0, sub * half, 0), (tile.split, ti...  1.06 us
  transfers between devices with their start and end apart: 13, of which 6 were waited for; matrix products, arithmetic and copies ran while one was open for 3% of the time, Pallas kernels for 25%

profile of v3, /device:TPU:0, one launch (start us, length us, event | category | flops | bytes accessed | tf_op | source)
XLA Modules:
  0.0 44.8 jit_solution(6102038338883849578)
XLA Ops:
  0.0 0.0 copy-start.3
  0.0 0.0 copy-start.4
  0.0 0.5 %collective-permute-start.5 = (bf16[512,2048]{1,0:T(8,128)(2,1)}, bf16[512,2048]{1,0:T(8,128)(2,1)S(1)}, u32[]{:S(2)}, u32[]{:S(2)}) collective-permute-start(bf16[512,2048]{1,0:T(8,128)(2,1)} %refs_1_.1), channel_id=1, source_target_pairs={{0,1},{1,0},{2,3},{3,2},{4,5},{5,4},{6,7},{7,6},{8,9},{9,8},{10,11... | collective-permute-start | bytes 6291464 | tf_op jit(solution)/shard_map/ppermute | solution.py:31
  0.5 0.1 collective-permute-start.6
  0.5 3.0 %collective-permute-start = (s32[4,2,16]{2,1,0:T(2,128)}, s32[4,2,16]{2,1,0:T(2,128)S(1)}, u32[]{:S(2)}, u32[]{:S(2)}) collective-permute-start(s32[4,2,16]{2,1,0:T(2,128)} %bitcast.47), channel_id=1, source_target_pairs={{0,4},{1,5},{4,0},{5,1},{8,12},{9,13},{12,8},{13,9},{2,6},{3,7},{6... | collective-permute-start | bytes 1544 | tf_op jit(solution)/shard_map/ppermute | solution.py:26
  3.5 1.1 %constant_dynamic-slice_fusion = (bf16[2,16,8,512]{3,2,1,0:T(8,128)(2,1)S(1)}, bf16[2,16,8,512]{3,2,1,0:T(8,128)(2,1)S(1)}) fusion(bf16[4,16,16,512]{3,2,1,0:T(8,128)(2,1)} %param.6, s32[]{:T(128)S(6)} %select_n.31, s32[]{:T(128)S(6)} %select_n.30, s32[]{:T(128)S(6)} %select_n.29), kind=kLoop, calls=%fused_computation.16 | loop fusion | bytes 1048588 | tf_op jit(solution)/shard_map/dynamic_slice | solution.py:241
  4.6 0.0 copy-start.1
  4.6 0.1 collective-permute-start.2
  4.8 0.1 collective-permute-start.3
  4.8 0.0 copy-done.4
  4.9 0.1 fusion.4
  4.9 0.4 collective-permute-done
  5.3 0.0 copy-done.3
  5.4 0.1 collective-permute-start.1
  5.5 7.2 %collective-permute-done.2.even.refs_2_ = bf16[256,512]{1,0:T(8,128)(2,1)S(1)} collective-permute-done((bf16[256,512]{1,0:T(8,128)(2,1)S(1)}, bf16[256,512]{1,0:T(8,128)(2,1)S(1)}, u32[]{:S(2)}, u32[]{:S(2)}) %collective-permute-start.2) | collective-permute-done | bytes 262176 | tf_op jit(solution)/shard_map/ppermute | solution.py:26
  12.7 0.0 collective-permute-done.3.odd.refs_4_
  12.7 0.1 shard_map.64
  12.8 1.6 %collective-permute-start.4 = (bf16[128,512]{1,0:T(8,128)(2,1)S(1)}, bf16[128,512]{1,0:T(8,128)(2,1)S(1)}, u32[]{:S(2)}, u32[]{:S(2)}) collective-permute-start(bf16[128,512]{1,0:T(8,128)(2,1)S(1)} %shard_map.64), channel_id=1, source_target_pairs={{0,2},{1,3},{2,0},{3,1},{4,6},{5,7},{6,4},{7,5},{8,10},{9,11},{10,... | collective-permute-start | bytes 393224 | tf_op jit(solution)/shard_map/ppermute | solution.py:26
  14.4 0.0 collective-permute-done.6.refs_8_
  14.4 0.0 collective-permute-done.5.refs_2_
  14.4 1.8 %collective-permute-start.7 = (bf16[256,512]{1,0:T(8,128)(2,1)S(1)}, bf16[256,512]{1,0:T(8,128)(2,1)S(1)}, u32[]{:S(2)}, u32[]{:S(2)}) collective-permute-start(bf16[256,512]{1,0:T(8,128)(2,1)S(1)} %bitcast.40), channel_id=1, source_target_pairs={{0,4},{1,5},{4,0},{5,1},{8,12},{9,13},{12,8},{13,9},{2,6},{3,7},{6... | collective-permute-start | bytes 786440 | tf_op jit(solution)/shard_map/ppermute | solution.py:26
  16.2 0.0 collective-permute-done.1
  16.2 0.1 collective-permute-start.8
  16.3 1.5 %collective-permute-done.4.refs_0_ = bf16[128,512]{1,0:T(8,128)(2,1)S(1)} collective-permute-done((bf16[128,512]{1,0:T(8,128)(2,1)S(1)}, bf16[128,512]{1,0:T(8,128)(2,1)S(1)}, u32[]{:S(2)}, u32[]{:S(2)}) %collective-permute-start.4) | collective-permute-done | bytes 131104 | tf_op jit(solution)/shard_map/ppermute | solution.py:26
  17.8 3.4 %collective-permute-done.7.refs_3_ = bf16[256,512]{1,0:T(8,128)(2,1)S(1)} collective-permute-done((bf16[256,512]{1,0:T(8,128)(2,1)S(1)}, bf16[256,512]{1,0:T(8,128)(2,1)S(1)}, u32[]{:S(2)}, u32[]{:S(2)}) %collective-permute-start.7) | collective-permute-done | bytes 262176 | tf_op jit(solution)/shard_map/ppermute | solution.py:26
  21.3 0.1 collective-permute-start.9
  21.4 0.0 copy-start
  21.4 0.6 %collective-permute-start.11 = (bf16[256,512]{1,0:T(8,128)(2,1)S(1)}, bf16[256,512]{1,0:T(8,128)(2,1)S(1)}, u32[]{:S(2)}, u32[]{:S(2)}) collective-permute-start(bf16[256,512]{1,0:T(8,128)(2,1)S(1)} %pad_maximum_fusion.1), channel_id=1, source_target_pairs={{0,1},{1,0},{4,8},{5,9},{8,4},{9,5},{12,13},{13,12},{2,3},{3,2},{6... | collective-permute-start | bytes 786440 | tf_op jit(solution)/shard_map/ppermute | solution.py:26
  22.0 0.0 copy-done.1
  22.0 4.6 %shard_map.65.near = bf16[512,512]{1,0:T(8,128)(2,1)S(1)} custom-call(s32[4,8,16]{2,1,0:T(8,128)S(1)} %get-tuple-element.29.ints, bf16[256,512]{1,0:T(8,128)(2,1)S(1)} %bitcast.34, bf16[256,512]{1,0:T(8,128)(2,1)S(1)} %bitcast.41, bf16[256,512]{1,0:T(8,128)(2,1)S(1)} %collective-permute-done.2.even.refs_2_, ...), custom_call_target="tpu_custom_call" | custom-call | tf_op jit(solution)/shard_map/pallas_call | solution.py:41
  26.5 0.0 collective-permute-done.8.refs_5_
  26.6 0.0 collective-permute-done.9.refs_6_
  26.6 0.0 copy-done
  26.6 2.7 %shard_map.66 = (bf16[256,512]{1,0:T(8,128)(2,1)S(1)}, bf16[256,512]{1,0:T(8,128)(2,1)S(1)}) custom-call(s32[4,8,16]{2,1,0:T(8,128)S(1)} %get-tuple-element.30.ints, bf16[256,512]{1,0:T(8,128)(2,1)S(1)} %bitcast.35, bf16[256,512]{1,0:T(8,128)(2,1)S(1)} %bitcast.42, bf16[256,512]{1,0:T(8,128)(2,1)S(1)} %collective-permute-done.2.even.refs_2_, ...), custom_call_target="tpu_custom_call" | custom-call | tf_op jit(solution)/shard_map/pallas_call | solution.py:41
  29.3 5.0 %collective-permute-start.10 = (bf16[256,512]{1,0:T(8,128)(2,1)S(1)}, bf16[256,512]{1,0:T(8,128)(2,1)S(1)}, u32[]{:S(2)}, u32[]{:S(2)}) collective-permute-start(bf16[256,512]{1,0:T(8,128)(2,1)S(1)} %get-tuple-element.18), channel_id=1, source_target_pairs={{0,4},{1,5},{4,0},{5,1},{8,12},{9,13},{12,8},{13,9},{2,6},{3,7},{6... | collective-permute-start | bytes 786440 | tf_op jit(solution)/shard_map/ppermute | solution.py:26
  34.3 0.0 collective-permute-done.11.refs_6_
  34.3 1.9 %shard_map.67 = bf16[256,512]{1,0:T(8,128)(2,1)S(1)} custom-call(s32[4,8,16]{2,1,0:T(8,128)S(1)} %get-tuple-element.30.ints, bf16[256,512]{1,0:T(8,128)(2,1)S(1)} %bitcast.36, bf16[256,512]{1,0:T(8,128)(2,1)S(1)} %bitcast.43, bf16[256,512]{1,0:T(8,128)(2,1)S(1)} %collective-permute-done.2.even.refs_2_, bf16[256,512]{1,0:T(8,128)(2,1)S(1)} %collective-permute-done.7.refs_3_, ...), custom_call_target="tpu_custom_call" | custom-call | tf_op jit(solution)/shard_map/pallas_call | solution.py:41
  36.2 0.0 copy-start.2
  36.2 0.1 collective-permute-start.12
  36.3 1.9 %shard_map.68.refs_3_ = bf16[256,512]{1,0:T(8,128)(2,1)S(1)} custom-call(s32[4,8,16]{2,1,0:T(8,128)S(1)} %get-tuple-element.30.ints, bf16[256,512]{1,0:T(8,128)(2,1)S(1)} %bitcast.37, bf16[256,512]{1,0:T(8,128)(2,1)S(1)} %bitcast.44, bf16[256,512]{1,0:T(8,128)(2,1)S(1)} %collective-permute-done.2.even.refs_2_, ...), custom_call_target="tpu_custom_call" | custom-call | tf_op jit(solution)/shard_map/pallas_call | solution.py:41
  38.2 2.2 %collective-permute-done.10.refs_0_ = bf16[256,512]{1,0:T(8,128)(2,1)S(1)} collective-permute-done((bf16[256,512]{1,0:T(8,128)(2,1)S(1)}, bf16[256,512]{1,0:T(8,128)(2,1)S(1)}, u32[]{:S(2)}, u32[]{:S(2)}) %collective-permute-start.10) | collective-permute-done | bytes 262176 | tf_op jit(solution)/shard_map/ppermute | solution.py:26
  40.4 2.8 %collective-permute-done.12.refs_1_ = bf16[256,512]{1,0:T(8,128)(2,1)S(1)} collective-permute-done((bf16[256,512]{1,0:T(8,128)(2,1)S(1)}, bf16[256,512]{1,0:T(8,128)(2,1)S(1)}, u32[]{:S(2)}, u32[]{:S(2)}) %collective-permute-start.12) | collective-permute-done | bytes 262176 | tf_op jit(solution)/shard_map/ppermute | solution.py:26
  43.2 0.0 copy-done.2
  43.2 1.6 %shard_map.69 = bf16[512,512]{1,0:T(8,128)(2,1)} custom-call(s32[4,16]{1,0:T(4,128)S(1)} %copy-done.2, bf16[512,512]{1,0:T(8,128)(2,1)S(1)} %shard_map.65.near, bf16[256,512]{1,0:T(8,128)(2,1)S(1)} %collective-permute-done.10.refs_0_, bf16[256,512]{1,0:T(8,128)(2,1)S(1)} %collective-permute-done.12.refs_1_, bf16[256,512]{1,0:T(8,128)(2,1)S(1)} %get-tuple-element.20.refs_2_, ...), custom_call_target="tpu_custom_call" | custom-call | tf_op jit(solution)/shard_map/pallas_call | solution.py:41
  (10 shorter events, 0.2 us)
Async XLA Ops:
  0.0 5.3 %copy-start.3 = (s32[4,16,2]{1,2,0:T(2,128)S(1)}, s32[4,16,2]{1,2,0:T(2,128)}, u32[]{:S(2)}) copy-start(s32[4,16,2]{1,2,0:T(2,128)} %param.9) | copy-start | bytes 1540
  0.0 4.8 %copy-start.4 = (s32[4,16,4]{1,2,0:T(4,128)S(1)}, s32[4,16,4]{1,2,0:T(4,128)}, u32[]{:S(2)}) copy-start(s32[4,16,4]{1,2,0:T(4,128)} %param.8) | copy-start | bytes 3076
  0.0 14.4 %collective-permute-start.5 = (bf16[512,2048]{1,0:T(8,128)(2,1)}, bf16[512,2048]{1,0:T(8,128)(2,1)S(1)}, u32[]{:S(2)}, u32[]{:S(2)}) collective-permute-start(bf16[512,2048]{1,0:T(8,128)(2,1)} %refs_1_.1), channel_id=1, source_target_pairs={{0,1},{1,0},{2,3},{3,2},{4,5},{5,4},{6,7},{7,6},{8,9},{9,8},{10,11... | collective-permute-start | bytes 6291464 | tf_op jit(solution)/shard_map/ppermute | solution.py:31
  0.5 13.9 %collective-permute-start.6 = (bf16[512,1024]{1,0:T(8,128)(2,1)}, bf16[512,1024]{1,0:T(8,128)(2,1)S(1)}, u32[]{:S(2)}, u32[]{:S(2)}) collective-permute-start(bf16[512,1024]{1,0:T(8,128)(2,1)} %refs_7_.5), channel_id=1, source_target_pairs={{0,1},{1,0},{2,3},{3,2},{4,5},{5,4},{6,7},{7,6},{8,9},{9,8},{10,11... | collective-permute-start | bytes 3145736 | tf_op jit(solution)/shard_map/ppermute | solution.py:31
  0.5 4.8 %collective-permute-start = (s32[4,2,16]{2,1,0:T(2,128)}, s32[4,2,16]{2,1,0:T(2,128)S(1)}, u32[]{:S(2)}, u32[]{:S(2)}) collective-permute-start(s32[4,2,16]{2,1,0:T(2,128)} %bitcast.47), channel_id=1, source_target_pairs={{0,4},{1,5},{4,0},{5,1},{8,12},{9,13},{12,8},{13,9},{2,6},{3,7},{6... | collective-permute-start | bytes 1544 | tf_op jit(solution)/shard_map/ppermute | solution.py:26
  4.6 17.3 %copy-start.1 = (bf16[512,2048]{1,0:T(8,128)(2,1)S(1)}, bf16[512,2048]{1,0:T(8,128)(2,1)}, u32[]{:S(2)}) copy-start(bf16[512,2048]{1,0:T(8,128)(2,1)} %refs_1_.1) | copy-start | bytes 6291460
  4.6 8.1 %collective-permute-start.2 = (bf16[256,512]{1,0:T(8,128)(2,1)S(1)}, bf16[256,512]{1,0:T(8,128)(2,1)S(1)}, u32[]{:S(2)}, u32[]{:S(2)}) collective-permute-start(bf16[256,512]{1,0:T(8,128)(2,1)S(1)} %bitcast.31), channel_id=1, source_target_pairs={{0,4},{1,5},{4,0},{5,1},{8,12},{9,13},{12,8},{13,9},{2,6},{3,7},{6... | collective-permute-start | bytes 786440 | tf_op jit(solution)/shard_map/ppermute | solution.py:26
  4.8 8.0 %collective-permute-start.3 = (bf16[256,512]{1,0:T(8,128)(2,1)S(1)}, bf16[256,512]{1,0:T(8,128)(2,1)S(1)}, u32[]{:S(2)}, u32[]{:S(2)}) collective-permute-start(bf16[256,512]{1,0:T(8,128)(2,1)S(1)} %bitcast.38), channel_id=1, source_target_pairs={{0,1},{1,0},{4,8},{5,9},{8,4},{9,5},{12,13},{13,12},{2,3},{3,2},{6... | collective-permute-start | bytes 786440 | tf_op jit(solution)/shard_map/ppermute | solution.py:26
  5.4 10.9 %collective-permute-start.1 = (s32[4,8,16]{2,1,0:T(8,128)S(1)}, s32[4,8,16]{2,1,0:T(8,128)S(1)}, u32[]{:S(2)}, u32[]{:S(2)}) collective-permute-start(s32[4,8,16]{2,1,0:T(8,128)S(1)} %fusion), channel_id=1, source_target_pairs={{0,1},{1,0},{2,3},{3,2},{4,5},{5,4},{6,7},{7,6},{8,9},{9,8},{10,11... | collective-permute-start | bytes 6152 | tf_op jit(solution)/shard_map/ppermute | solution.py:31
  12.8 5.0 %collective-permute-start.4 = (bf16[128,512]{1,0:T(8,128)(2,1)S(1)}, bf16[128,512]{1,0:T(8,128)(2,1)S(1)}, u32[]{:S(2)}, u32[]{:S(2)}) collective-permute-start(bf16[128,512]{1,0:T(8,128)(2,1)S(1)} %shard_map.64), channel_id=1, source_target_pairs={{0,2},{1,3},{2,0},{3,1},{4,6},{5,7},{6,4},{7,5},{8,10},{9,11},{10,... | collective-permute-start | bytes 393224 | tf_op jit(solution)/shard_map/ppermute | solution.py:26
  14.4 6.8 %collective-permute-start.7 = (bf16[256,512]{1,0:T(8,128)(2,1)S(1)}, bf16[256,512]{1,0:T(8,128)(2,1)S(1)}, u32[]{:S(2)}, u32[]{:S(2)}) collective-permute-start(bf16[256,512]{1,0:T(8,128)(2,1)S(1)} %bitcast.40), channel_id=1, source_target_pairs={{0,4},{1,5},{4,0},{5,1},{8,12},{9,13},{12,8},{13,9},{2,6},{3,7},{6... | collective-permute-start | bytes 786440 | tf_op jit(solution)/shard_map/ppermute | solution.py:26
  16.2 10.3 %collective-permute-start.8 = (bf16[256,512]{1,0:T(8,128)(2,1)S(1)}, bf16[256,512]{1,0:T(8,128)(2,1)S(1)}, u32[]{:S(2)}, u32[]{:S(2)}) collective-permute-start(bf16[256,512]{1,0:T(8,128)(2,1)S(1)} %bitcast.33), channel_id=1, source_target_pairs={{0,1},{1,0},{4,8},{5,9},{8,4},{9,5},{12,13},{13,12},{2,3},{3,2},{6... | collective-permute-start | bytes 786440 | tf_op jit(solution)/shard_map/ppermute | solution.py:26
  21.3 5.3 %collective-permute-start.9 = (bf16[256,512]{1,0:T(8,128)(2,1)S(1)}, bf16[256,512]{1,0:T(8,128)(2,1)S(1)}, u32[]{:S(2)}, u32[]{:S(2)}) collective-permute-start(bf16[256,512]{1,0:T(8,128)(2,1)S(1)} %pad_maximum_fusion), channel_id=1, source_target_pairs={{0,1},{1,0},{4,8},{5,9},{8,4},{9,5},{12,13},{13,12},{2,3},{3,2},{6... | collective-permute-start | bytes 786440 | tf_op jit(solution)/shard_map/ppermute | solution.py:26
  21.4 5.2 %copy-start = (bf16[512,1024]{1,0:T(8,128)(2,1)S(1)}, bf16[512,1024]{1,0:T(8,128)(2,1)}, u32[]{:S(2)}) copy-start(bf16[512,1024]{1,0:T(8,128)(2,1)} %refs_7_.5) | copy-start | bytes 3145732
  21.4 12.9 %collective-permute-start.11 = (bf16[256,512]{1,0:T(8,128)(2,1)S(1)}, bf16[256,512]{1,0:T(8,128)(2,1)S(1)}, u32[]{:S(2)}, u32[]{:S(2)}) collective-permute-start(bf16[256,512]{1,0:T(8,128)(2,1)S(1)} %pad_maximum_fusion.1), channel_id=1, source_target_pairs={{0,1},{1,0},{4,8},{5,9},{8,4},{9,5},{12,13},{13,12},{2,3},{3,2},{6... | collective-permute-start | bytes 786440 | tf_op jit(solution)/shard_map/ppermute | solution.py:26
  29.3 11.1 %collective-permute-start.10 = (bf16[256,512]{1,0:T(8,128)(2,1)S(1)}, bf16[256,512]{1,0:T(8,128)(2,1)S(1)}, u32[]{:S(2)}, u32[]{:S(2)}) collective-permute-start(bf16[256,512]{1,0:T(8,128)(2,1)S(1)} %get-tuple-element.18), channel_id=1, source_target_pairs={{0,4},{1,5},{4,0},{5,1},{8,12},{9,13},{12,8},{13,9},{2,6},{3,7},{6... | collective-permute-start | bytes 786440 | tf_op jit(solution)/shard_map/ppermute | solution.py:26
  36.2 7.0 %copy-start.2 = (s32[4,16]{1,0:T(4,128)S(1)}, s32[4,16]{1,0:T(4,128)}, u32[]{:S(2)}) copy-start(s32[4,16]{1,0:T(4,128)} %level.1) | copy-start | bytes 772
  36.2 7.0 %collective-permute-start.12 = (bf16[256,512]{1,0:T(8,128)(2,1)S(1)}, bf16[256,512]{1,0:T(8,128)(2,1)S(1)}, u32[]{:S(2)}, u32[]{:S(2)}) collective-permute-start(bf16[256,512]{1,0:T(8,128)(2,1)S(1)} %shard_map.67), channel_id=1, source_target_pairs={{0,4},{1,5},{4,0},{5,1},{8,12},{9,13},{12,8},{13,9},{2,6},{3,7},{6... | collective-permute-start | bytes 786440 | tf_op jit(solution)/shard_map/ppermute | solution.py:26

commit v4 on v3

--- a/solution.py
+++ b/solution.py
@@ -8,7 +8,7 @@
 from jax.sharding import PartitionSpec as P
 
 REACH = 2
-PARTS = (1, 1)
+PARTS = (3, 3, 2)
 VMEM_BYTES = 48 * 2**20
 CONTRACT_LAST = (((1,), (1,)), ((), ()))
 
@@ -35,15 +35,18 @@
     return lax.optimization_barrier((tuple(arrays), first))[0]
 
 
-def call(kernel, rows, pixels, ints, arrays, scratch, outputs=1):
+def call(kernel, rows, pixels, ints, arrays, scratch, outputs=1, left=0):
     shape = jax.ShapeDtypeStruct((rows, pixels), jnp.bfloat16)
-    vmem, smem = (pl.BlockSpec(memory_space=space) for space in (pltpu.VMEM, pltpu.SMEM))
+    vmem = pl.BlockSpec(memory_space=pltpu.VMEM)
     return pl.pallas_call(
         kernel,
         out_shape=[shape] * outputs,
-        in_specs=[smem] * len(ints) + [vmem] * len(arrays),
+        in_specs=[vmem] * (len(ints) + len(arrays) - left)
+        + [pl.BlockSpec(memory_space=pl.ANY)] * left,
         out_specs=[vmem] * outputs,
-        scratch_shapes=scratch,
+        scratch_shapes=scratch
+        + [pltpu.SMEM(x.shape, x.dtype) for x in ints]
+        + [pltpu.SemaphoreType.DMA] * len(ints),
         compiler_params=pltpu.CompilerParams(vmem_limit_bytes=VMEM_BYTES),
     )(*ints, *arrays)
 
@@ -68,10 +71,13 @@
     def blocks(self, value):
         return value.reshape(REACH, self.half, self.pixels)
 
-    def gather(self, blocks, chosen, base, index_of, units, slots):
+    def gather(self, blocks, chosen, base, index_of, units, slots, begin=0, count=None):
+        count = self.tile_rows if count is None else count
+
         def one_row(g, carry):
             for unit in range(units):
-                at = pl.multiple_of(base + (unit * self.tile_rows + g) * self.group, self.group)
+                at = base + (unit * count + g - begin) * self.group
+                at = pl.multiple_of(at, self.group)
                 for k in range(slots):
                     pair = [blocks[index_of(g, unit * REACH + i, k)] for i in range(REACH)]
                     chosen[pl.ds(at, self.group), k * self.pixels : (k + 1) * self.pixels] = (
@@ -79,7 +85,7 @@
                     )
             return carry
 
-        lax.fori_loop(0, self.tile_rows, one_row, 0)
+        lax.fori_loop(begin, begin + count, one_row, 0)
 
 
 def product(chosen, factors):
@@ -96,50 +102,59 @@
     return total
 
 
-def far_kernel(tile, names, first, units, wanted, slots, ints, *refs):
+def far_kernel(tile, names, first, units, wanted, slots, ints_in, *refs):
+    *refs, ints, arrived = refs
     row = lax.axis_index("rows")
-    sign = jnp.where(row % 2 == 0, 1, -1)
-    width = units * REACH
-    shards = {}
-    taken = 0
-    for name, flag, start in names[:-1]:
-        shards[name] = (refs[taken : taken + 2], flag, start)
-        taken += 2
-    size = units * tile.unit
-    pieces = [refs[taken].at[pl.ds(at, size), :] for at in (0, size)]
-    shards[names[-1][0]] = (pieces, *names[-1][1:])
-    taken += 1
-    own_half, other_half, *outs = refs[taken : taken + 2 + len(wanted)]
-    blocks, chosen = refs[taken + 2 + len(wanted) :]
-    for (parity, step), (pieces, flag, start) in shards.items():
-        away = 0 if step < 0 else (1 + step) * (sign if parity == 0 else -sign)
-        source = row + away
-        source = jnp.where((source >= 0) & (source < tile.rows), source, tile.rows)
-        for half, piece in enumerate(pieces):
-            later = (row % 2 == flag) == (half == 0)
-            base = source * tile.tile_rows + jnp.where(later, tile.split, 0)
+
+    @pl.when((row > 0) & (row < tile.rows - 1))
+    def _():
+        copy = pltpu.make_async_copy(ints_in, ints, arrived)
+        copy.start()
+        sign = jnp.where(row % 2 == 0, 1, -1)
+        width = units * REACH
+        shards = {}
+        taken = 0
+        size = units * tile.unit
+        for name, flag, start in names:
+            if start is None:
+                shards[name] = (refs[taken : taken + 2], flag, 0)
+                taken += 2
+            else:
+                pieces = [refs[taken].at[pl.ds(at, size), :] for at in (0, size)]
+                shards[name] = (pieces, flag, start)
+                taken += 1
+        own_half, other_half, *outs = refs[taken : taken + 2 + len(wanted)]
+        blocks, chosen = refs[taken + 2 + len(wanted) :]
+        for (parity, step), (pieces, flag, start) in shards.items():
+            away = 0 if step < 0 else (1 + step) * (sign if parity == 0 else -sign)
+            source = row + away
+            source = jnp.where((source >= 0) & (source < tile.rows), source, tile.rows)
+            for half, piece in enumerate(pieces):
+                later = (row % 2 == flag) == (half == 0)
+                base = source * tile.tile_rows + jnp.where(later, tile.split, 0)
+                for unit in range(units):
+                    for g in range(tile.split):
+                        at = (unit + first - start) * tile.unit + g * tile.group
+                        value = piece[at : at + tile.group, :].astype(jnp.float32)
+                        blocks[pl.ds((base + g) * width + unit * REACH, REACH)] = tile.blocks(value)
+
+        copy.wait()
+        count = tile.tile_rows * units * tile.group
+        for n, (plane, _) in enumerate(wanted):
+
+            def index_of(g, j, k):
+                return ints[g, plane[k] * tile.tile_cols + first * REACH + j] * width + j
+
+            tile.gather(blocks, chosen, n * count, index_of, units, 2 * slots)
+        mean = product(chosen, (own_half, other_half))
+        for n, (_, name) in enumerate(wanted):
+            pieces, flag, start = shards[name]
             for unit in range(units):
-                for g in range(tile.split):
-                    at = (unit + first - start) * tile.unit + g * tile.group
-                    value = piece[at : at + tile.group, :].astype(jnp.float32)
-                    blocks[pl.ds((base + g) * width + unit * REACH, REACH)] = tile.blocks(value)
-
-    count = tile.tile_rows * units * tile.group
-    for n, (plane, _) in enumerate(wanted):
-
-        def index_of(g, j, k):
-            return ints[g, plane[k], first * REACH + j] * width + j
-
-        tile.gather(blocks, chosen, n * count, index_of, units, 2 * slots)
-    mean = product(chosen, (own_half, other_half))
-    for n, (_, name) in enumerate(wanted):
-        pieces, flag, start = shards[name]
-        for unit in range(units):
-            for g in range(tile.tile_rows):
-                at = (unit * tile.tile_rows + g) * tile.group
-                field = tile.read(pieces, flag, row, unit + first - start, g)
-                value = field - mean[n * count + at : n * count + at + tile.group, :]
-                outs[n][at : at + tile.group, :] = value.astype(jnp.bfloat16)
+                for g in range(tile.tile_rows):
+                    at = (unit * tile.tile_rows + g) * tile.group
+                    field = tile.read(pieces, flag, row, unit + first - start, g)
+                    value = field - mean[n * count + at : n * count + at + tile.group, :]
+                    outs[n][at : at + tile.group, :] = value.astype(jnp.bfloat16)
 
 
 def halo(tile, row, even, odd, unit, r):
@@ -164,9 +179,16 @@
         out[r * tile.group : (r + 1) * tile.group, :] = value.astype(jnp.bfloat16)
 
 
-def near_kernel(tile, slots, sides, ints, first, second, even, odd, *refs):
+def near_kernel(tile, slots, sides, ints_in, first, second, even, odd, *refs):
+    *refs, ints, arrived = refs
+    copy = pltpu.make_async_copy(ints_in, ints, arrived)
+    copy.start()
     halos = refs[:sides]
-    own_half, other_half, out, blocks, chosen = refs[sides:]
+    own_half, other_half, out, blocks, chosen, *factors, factor_sem = refs[sides:]
+    loads = []
+    for i, source in enumerate((own_half, other_half)):
+        loads.append(pltpu.make_async_copy(source, factors[i], factor_sem.at[i]))
+        loads[i].start()
     row, col = lax.axis_index("rows"), lax.axis_index("cols")
     above, below = row > 0, row < tile.rows - 1
     wide, last = tile.wide, tile.tile_rows + REACH
@@ -192,19 +214,26 @@
         blocks[pl.ds(r * wide + REACH + tile.tile_cols, REACH)] = right
 
     def index_of(g, j, k):
-        return ints[g, k, j]
-
+        return ints[g, k * tile.tile_cols + j]
+
+    copy.wait()
     tile.gather(blocks, chosen, 0, index_of, tile.units, 2 * slots)
-    mean = product(chosen, (own_half, other_half))
+    for load in loads:
+        load.wait()
+    mean = product(chosen, factors)
     for unit in range(tile.units):
         for g in range(tile.tile_rows):
             at = (unit * tile.tile_rows + g) * tile.group
-            value = tile.read((first, second), 0, row, unit, g) - mean[at : at + tile.group, :]
-            out[at : at + tile.group, :] = value.astype(jnp.bfloat16)
-
-
-def pick_kernel(tile, parts, level, near, *refs):
-    ready, own, out = refs[: len(parts)], refs[len(parts) : 2 * len(parts)], refs[-1]
+            value = tile.read((first, second), 0, row, unit, g)
+            out[at : at + tile.group, :] = (value - mean[at : at + tile.group, :]).astype(jnp.bfloat16)
+
+
+def mix_kernel(tile, parts, level_in, near, *refs):
+    *refs, level, arrived = refs
+    copy = pltpu.make_async_copy(level_in, level, arrived)
+    copy.start()
+    copy.wait()
+    own, out, awaited = refs[: len(parts)], refs[-2], refs[-1]
     row = lax.axis_index("rows")
     at_end = (row == 0) | (row == tile.rows - 1)
     lower = lax.broadcasted_iota(jnp.int32, (tile.group, tile.pixels), 0) // tile.half
@@ -213,15 +242,33 @@
         for unit in range(units):
             for g in range(tile.tile_rows):
                 at = (unit * tile.tile_rows + g) * tile.group
-                far = [x[c][at : at + tile.group, :].astype(jnp.float32) for x in (ready, own)]
-                far = jnp.where(at_end, *far)
+                far = own[c][at : at + tile.group, :].astype(jnp.float32)
                 at = ((first + unit) * tile.tile_rows + g) * tile.group
                 fine = near[at : at + tile.group, :].astype(jnp.float32)
                 levels = level[g, (first + unit) * REACH]
                 for i in range(1, REACH):
                     levels = jnp.where(lower == i, level[g, (first + unit) * REACH + i], levels)
                 at = (g * tile.units + first + unit) * tile.group
-                out[at : at + tile.group, :] = jnp.where(levels == 1, fine, far).astype(jnp.bfloat16)
+                mixed = jnp.where(levels == 1, fine, far)
+                out[at : at + tile.group, :] = mixed.astype(jnp.bfloat16)
+                wait = jnp.where((levels != 1) & at_end, 1.0, 0.0)
+                awaited[at : at + tile.group, :] = wait.astype(jnp.bfloat16)
+        first += units
+
+
+def final_kernel(tile, parts, mixed, awaited, *refs):
+    out = refs[-1]
+    first = 0
+    for c, units in enumerate(parts):
+        for unit in range(units):
+            for g in range(tile.tile_rows):
+                at = (unit * tile.tile_rows + g) * tile.group
+                at_out = (g * tile.units + first + unit) * tile.group
+                spot = slice(at_out, at_out + tile.group)
+                far = refs[c][at : at + tile.group, :].astype(jnp.float32)
+                value = mixed[spot, :].astype(jnp.float32)
+                value = jnp.where(awaited[spot, :].astype(jnp.float32) > 0.5, far, value)
+                out[spot, :] = value.astype(jnp.bfloat16)
         first += units
 
 
@@ -272,17 +319,7 @@
     other = swap_sub(codes)
     near_ints = jnp.concatenate([near_index, other[:, :near_slots]], axis=1)
     far_ints = jnp.concatenate([codes[:, near_slots:], other[:, near_slots:]], axis=1)
-
-    inner = rows > 4
-    for step in range(1, rows - 3):
-        if inner:
-            even.append([exchange(x, "rows", 0) for x in odd[step - 1]])
-        odd.append([exchange(x, "rows", 1) for x in even[step - 1]])
-    source = after(even[rows - 4], near_ints, far_ints, *halos)
-    last = []
-    for start, units in zip(starts, parts):
-        spots = slice(start * tile.unit, (start + units) * tile.unit)
-        last.append(exchange(jnp.concatenate([x[spots] for x in source], axis=0), "rows", 1))
+    near_ints, far_ints = (x.reshape(tile_rows, -1) for x in (near_ints, far_ints))
 
     size = tile_rows * tile_cols * half
     (near_own,) = call(
@@ -291,25 +328,42 @@
         [
             pltpu.VMEM(((tile_rows + 2 * REACH) * tile.wide, half, pixels), jnp.float32),
             pltpu.VMEM((size, 2 * near_slots * pixels), jnp.bfloat16),
+            pltpu.VMEM(near_factor.shape, near_factor.dtype),
+            pltpu.VMEM(near_factor.shape, near_factor.dtype),
+            pltpu.SemaphoreType.DMA((2,)),
         ],
+        left=2,
     )
 
+    inner = rows > 4
+    for step in range(1, rows - 3):
+        if inner:
+            even.append([exchange(x, "rows", 0) for x in odd[step - 1]])
+        odd.append([exchange(x, "rows", 1) for x in even[step - 1]])
+    source = after(even[rows - 4], near_ints, far_ints, *halos, odd[0][1])
+    def cut(pieces, c):
+        spots = slice(starts[c] * tile.unit, (starts[c] + parts[c]) * tile.unit)
+        return jnp.concatenate([x[spots] for x in pieces], axis=0)
+
+    last = [exchange(cut(source, c), "rows", 1) for c in range(len(parts))]
+
     def far_chunk(c, wanted, *before):
-        names, arrays = [((0, -1), 0, 0)], [*own]
+        names, arrays = [((0, -1), 0, None)], [*own]
         for step in range(len(odd)):
             if step < len(even):
-                names.append(((0, step), 1, 0))
+                names.append(((0, step), 1, None))
                 arrays += even[step]
-            names.append(((1, step), 0, 0))
+            names.append(((1, step), 0, None))
             arrays += odd[step]
-        final = len(odd)
-        names.append(((1, final), 0, starts[c]))
+        names.append(((1, len(odd)), 0, starts[c]))
         arrays.append(last[c])
         if before:
             arrays = list(after(arrays[:1], *before)) + arrays[1:]
         here = tile_rows * parts[c] * tile.group
         return call(
-            functools.partial(far_kernel, tile, names, starts[c], parts[c], wanted, far_slots),
+            functools.partial(
+                far_kernel, tile, names, starts[c], parts[c], wanted, far_slots
+            ),
             here, pixels, [far_ints], [*arrays, far_factor, far_other],
             [
                 pltpu.VMEM(((rows + 1) * tile_rows * parts[c] * REACH, half, pixels), jnp.float32),
@@ -321,19 +375,19 @@
     slots = [k + 2 * far_slots * s for s in range(2) for k in range(far_slots)]
     partner = ([far_slots + k for k in slots], (0, 0))
     mine = (slots, (0, -1))
-    ready, far_own = [], []
+    ready = []
     sent = near_own
     for c in range(len(parts)):
-        if c < len(parts) - 1:
-            sent, kept = far_chunk(c, [partner, mine], sent)
-        else:
-            (sent,) = far_chunk(c, [partner], sent)
-            (kept,) = far_chunk(c, [mine])
+        (sent,) = far_chunk(c, [partner], sent)
         ready.append(exchange(sent, "rows", 0))
-        far_own.append(kept)
+    far_own = [far_chunk(c, [mine], sent)[0] for c in range(len(parts))]
+    mixed, awaited = call(
+        functools.partial(mix_kernel, tile, parts),
+        size, pixels, [block_level], [near_own, *far_own], [], 2,
+    )
     (result,) = call(
-        functools.partial(pick_kernel, tile, parts),
-        size, pixels, [block_level], [near_own, *ready, *far_own], [],
+        functools.partial(final_kernel, tile, parts),
+        size, pixels, [], [mixed, awaited, *ready], [],
     )
     return result.reshape(tile_rows, tile_cols, half, pixels)
 

time: 44.9 us -> 41 us (0.913)
  Pallas kernels: 12.8 us -> 6.11 us
  starting transfers between devices: 13 us -> 19.4 us
  waiting for transfers between devices: 17.5 us -> 12.9 us
  local copies, waits for them, and re-layouts: 1.17 us -> 1.96 us
    pallas_call x6 -> x10, Pallas kernels: 12.8 us -> 6.11 us  [call(): pl.pallas_call(kernel, out_shape=[shape] * outputs, in_specs=[vmem] * (le...]
    ppermute x10 -> x12, starting transfers between devices: 12.3 us -> 18.8 us  [exchange(): return lax.ppermute(array, (axis, 'sub'), pairs)]
    ppermute x10 -> x12, waiting for transfers between devices: 17.5 us -> 12.3 us  [exchange(): return lax.ppermute(array, (axis, 'sub'), pairs)]
    unnamed x10, local copies, waits for them, and re-layouts: 0.03 us -> 0.66 us
    ppermute x3, waiting for transfers between devices: 0.01 us -> 0.61 us  [swap_sub(): return lax.ppermute(array, 'sub', [(s, subs - 1 - s) for s in range(subs)])]
  transfers between devices with their start and end apart: 13 -> 15, of which waited for: 6 -> 6; matrix products, arithmetic and copies ran while one was open for 3% -> 3% of each run, Pallas kernels for 25% -> 13%
where the time goes in v4:
time: 41 us; the launch traced here: 40.8 us
  starting transfers between devices  19.4 us (47%)
  waiting for transfers between devices  12.9 us (31%)
  Pallas kernels  6.11 us (15%)
  local copies, waits for them, and re-layouts  1.96 us (5%)
    ppermute x12, starting transfers between devices, exchange(): return lax.ppermute(array, (axis, 'sub'), pairs)  18.8 us
    ppermute x12, waiting for transfers between devices, exchange(): return lax.ppermute(array, (axis, 'sub'), pairs)  12.3 us
    pallas_call x10, Pallas kernels, call(): pl.pallas_call(kernel, out_shape=[shape] * outputs, in_specs=[vmem] * (le...  6.11 us
    dynamic_slice x1, local copies, waits for them, and re-layouts, on_device(): lax.dynamic_slice(convergence, (start, 0, sub * half, 0), (tile.split, ti...  1.06 us
  transfers between devices with their start and end apart: 15, of which 6 were waited for; matrix products, arithmetic and copies ran while one was open for 3% of the time, Pallas kernels for 13%

profile of v4, /device:TPU:0, one launch (start us, length us, event | category | flops | bytes accessed | tf_op | source)
XLA Modules:
  0.0 40.8 jit_solution(9937680391139084608)
XLA Ops:
  0.0 0.0 copy-start.3
  0.0 0.0 copy-start.4
  0.0 0.5 %collective-permute-start.5 = (bf16[512,2048]{1,0:T(8,128)(2,1)}, bf16[512,2048]{1,0:T(8,128)(2,1)}, u32[]{:S(2)}, u32[]{:S(2)}) collective-permute-start(bf16[512,2048]{1,0:T(8,128)(2,1)} %refs_1_.1), channel_id=1, source_target_pairs={{0,1},{1,0},{2,3},{3,2},{4,5},{5,4},{6,7},{7,6},{8,9},{9,8},{10,11... | collective-permute-start | bytes 6291464 | tf_op jit(solution)/shard_map/ppermute | solution.py:31
  0.5 0.1 collective-permute-start.6
  0.5 3.0 %collective-permute-start = (s32[4,2,16]{2,1,0:T(2,128)}, s32[4,2,16]{2,1,0:T(2,128)S(1)}, u32[]{:S(2)}, u32[]{:S(2)}) collective-permute-start(s32[4,2,16]{2,1,0:T(2,128)} %bitcast.53), channel_id=1, source_target_pairs={{0,4},{1,5},{4,0},{5,1},{8,12},{9,13},{12,8},{13,9},{2,6},{3,7},{6... | collective-permute-start | bytes 1544 | tf_op jit(solution)/shard_map/ppermute | solution.py:26
  3.5 1.1 %constant_dynamic-slice_fusion = (bf16[2,16,8,512]{3,2,1,0:T(8,128)(2,1)S(1)}, bf16[2,16,8,512]{3,2,1,0:T(8,128)(2,1)S(1)}) fusion(bf16[4,16,16,512]{3,2,1,0:T(8,128)(2,1)} %param.6, s32[]{:T(128)S(6)} %select_n.31, s32[]{:T(128)S(6)} %select_n.30, s32[]{:T(128)S(6)} %select_n.29), kind=kLoop, calls=%fused_computation.17 | loop fusion | bytes 1048588 | tf_op jit(solution)/shard_map/dynamic_slice | solution.py:288
  4.6 0.1 collective-permute-start.2
  4.7 0.1 collective-permute-start.3
  4.8 0.0 copy-done.4
  4.8 0.1 fusion.4
  4.9 0.4 %collective-permute-done = s32[4,2,16]{2,1,0:T(2,128)S(1)} collective-permute-done((s32[4,2,16]{2,1,0:T(2,128)}, s32[4,2,16]{2,1,0:T(2,128)S(1)}, u32[]{:S(2)}, u32[]{:S(2)}) %collective-permute-start) | collective-permute-done | bytes 544 | tf_op jit(solution)/shard_map/ppermute | solution.py:26
  5.3 0.0 copy-done.3
  5.4 0.1 collective-permute-start.1
  5.5 0.4 collective-permute-done.6.refs_8_
  5.9 0.2 collective-permute-done.5.refs_2_
  6.1 2.9 %collective-permute-start.7 = (bf16[256,512]{1,0:T(8,128)(2,1)S(1)}, bf16[256,512]{1,0:T(8,128)(2,1)S(1)}, u32[]{:S(2)}, u32[]{:S(2)}) collective-permute-start(bf16[256,512]{1,0:T(8,128)(2,1)S(1)} %bitcast.42), channel_id=1, source_target_pairs={{0,4},{1,5},{4,0},{5,1},{8,12},{9,13},{12,8},{13,9},{2,6},{3,7},{6... | collective-permute-start | bytes 786440 | tf_op jit(solution)/shard_map/ppermute | solution.py:26
  9.0 0.0 collective-permute-start.8
  9.0 0.0 collective-permute-done.1
  9.0 4.9 %collective-permute-done.2.even.refs_2_ = bf16[256,512]{1,0:T(8,128)(2,1)S(1)} collective-permute-done((bf16[256,512]{1,0:T(8,128)(2,1)S(1)}, bf16[256,512]{1,0:T(8,128)(2,1)S(1)}, u32[]{:S(2)}, u32[]{:S(2)}) %collective-permute-start.2) | collective-permute-done | bytes 262176 | tf_op jit(solution)/shard_map/ppermute | solution.py:26
  13.9 0.0 collective-permute-done.3.odd.refs_4_
  13.9 0.1 shard_map.64
  14.0 1.6 %collective-permute-start.4 = (bf16[128,512]{1,0:T(8,128)(2,1)S(1)}, bf16[128,512]{1,0:T(8,128)(2,1)S(1)}, u32[]{:S(2)}, u32[]{:S(2)}) collective-permute-start(bf16[128,512]{1,0:T(8,128)(2,1)S(1)} %shard_map.64), channel_id=1, source_target_pairs={{0,2},{1,3},{2,0},{3,1},{4,6},{5,7},{6,4},{7,5},{8,10},{9,11},{10,... | collective-permute-start | bytes 393224 | tf_op jit(solution)/shard_map/ppermute | solution.py:26
  15.6 0.1 reshape.26.ints_in
  15.7 0.1 reshape.31.ints_in
  15.7 0.0 copy-start.1
  15.7 3.3 %collective-permute-done.4.refs_0_ = bf16[128,512]{1,0:T(8,128)(2,1)S(1)} collective-permute-done((bf16[128,512]{1,0:T(8,128)(2,1)S(1)}, bf16[128,512]{1,0:T(8,128)(2,1)S(1)}, u32[]{:S(2)}, u32[]{:S(2)}) %collective-permute-start.4) | collective-permute-done | bytes 131104 | tf_op jit(solution)/shard_map/ppermute | solution.py:26
  19.0 0.0 collective-permute-done.7.refs_3_
  19.0 0.0 collective-permute-done.8.refs_5_
  19.1 0.1 collective-permute-start.9
  19.2 0.6 %collective-permute-start.10 = (bf16[192,512]{1,0:T(8,128)(2,1)S(1)}, bf16[192,512]{1,0:T(8,128)(2,1)S(1)}, u32[]{:S(2)}, u32[]{:S(2)}) collective-permute-start(bf16[192,512]{1,0:T(8,128)(2,1)S(1)} %pad_maximum_fusion.1), channel_id=1, source_target_pairs={{0,1},{1,0},{4,8},{5,9},{8,4},{9,5},{12,13},{13,12},{2,3},{3,2},{6... | collective-permute-start | bytes 589832 | tf_op jit(solution)/shard_map/ppermute | solution.py:26
  19.8 0.0 copy-start
  19.8 0.1 collective-permute-start.11
  19.9 0.0 copy-done.1
  19.9 4.2 %shard_map.65.near = bf16[512,512]{1,0:T(8,128)(2,1)S(1)} custom-call(s32[4,128]{1,0:T(4,128)S(1)} %reshape.26.ints_in, bf16[256,512]{1,0:T(8,128)(2,1)S(1)} %bitcast.34, bf16[256,512]{1,0:T(8,128)(2,1)S(1)} %bitcast.44, bf16[256,512]{1,0:T(8,128)(2,1)S(1)} %collective-permute-done.2.even.refs_2_, bf16[256,512]{1,0:T(8,128)(2,1)S(1)} %collective-permute-done.3.odd.refs_4_, ...), custom_call_target="tpu_custom_call" | custom-call | tf_op jit(solution)/shard_map/pallas_call | solution.py:41
  24.1 0.0 collective-permute-done.9.refs_6_
  24.1 0.0 copy-done
  24.1 6.7 %collective-permute-start.12 = (bf16[192,512]{1,0:T(8,128)(2,1)S(1)}, bf16[192,512]{1,0:T(8,128)(2,1)S(1)}, u32[]{:S(2)}, u32[]{:S(2)}) collective-permute-start(bf16[192,512]{1,0:T(8,128)(2,1)S(1)} %shard_map.66), channel_id=1, source_target_pairs={{0,4},{1,5},{4,0},{5,1},{8,12},{9,13},{12,8},{13,9},{2,6},{3,7},{6... | collective-permute-start | bytes 589832 | tf_op jit(solution)/shard_map/ppermute | solution.py:26
  30.8 0.0 collective-permute-done.10.refs_6_
  30.8 2.1 %collective-permute-start.13 = (bf16[192,512]{1,0:T(8,128)(2,1)S(1)}, bf16[192,512]{1,0:T(8,128)(2,1)S(1)}, u32[]{:S(2)}, u32[]{:S(2)}) collective-permute-start(bf16[192,512]{1,0:T(8,128)(2,1)S(1)} %shard_map.67), channel_id=1, source_target_pairs={{0,4},{1,5},{4,0},{5,1},{8,12},{9,13},{12,8},{13,9},{2,6},{3,7},{6... | collective-permute-start | bytes 589832 | tf_op jit(solution)/shard_map/ppermute | solution.py:26
  33.0 0.0 collective-permute-done.11.refs_6_
  33.0 1.6 %collective-permute-start.14 = (bf16[128,512]{1,0:T(8,128)(2,1)S(1)}, bf16[128,512]{1,0:T(8,128)(2,1)S(1)}, u32[]{:S(2)}, u32[]{:S(2)}) collective-permute-start(bf16[128,512]{1,0:T(8,128)(2,1)S(1)} %shard_map.68), channel_id=1, source_target_pairs={{0,4},{1,5},{4,0},{5,1},{8,12},{9,13},{12,8},{13,9},{2,6},{3,7},{6... | collective-permute-start | bytes 393224 | tf_op jit(solution)/shard_map/ppermute | solution.py:26
  34.6 0.0 copy-start.2
  34.7 0.6 %copy-done.2 = s32[4,16]{1,0:T(4,128)S(1)} copy-done((s32[4,16]{1,0:T(4,128)S(1)}, s32[4,16]{1,0:T(4,128)}, u32[]{:S(2)}) %copy-start.2) | copy-done | bytes 280
  35.3 0.7 %shard_map.72 = (bf16[512,512]{1,0:T(8,128)(2,1)S(1)}, bf16[512,512]{1,0:T(8,128)(2,1)S(1)}) custom-call(s32[4,16]{1,0:T(4,128)S(1)} %copy-done.2, bf16[512,512]{1,0:T(8,128)(2,1)S(1)} %shard_map.65.near, bf16[192,512]{1,0:T(8,128)(2,1)S(1)} %shard_map.69.refs_0_, bf16[192,512]{1,0:T(8,128)(2,1)S(1)} %shard_map.70.refs_1_, ...), custom_call_target="tpu_custom_call" | custom-call | tf_op jit(solution)/shard_map/pallas_call | solution.py:41
  36.1 3.8 %collective-permute-done.14.refs_2_ = bf16[128,512]{1,0:T(8,128)(2,1)S(1)} collective-permute-done((bf16[128,512]{1,0:T(8,128)(2,1)S(1)}, bf16[128,512]{1,0:T(8,128)(2,1)S(1)}, u32[]{:S(2)}, u32[]{:S(2)}) %collective-permute-start.14) | collective-permute-done | bytes 131104 | tf_op jit(solution)/shard_map/ppermute | solution.py:26
  39.8 0.0 collective-permute-done.12.refs_0_
  39.8 0.0 collective-permute-done.13.refs_1_
  39.8 1.0 %shard_map.73 = bf16[512,512]{1,0:T(8,128)(2,1)} custom-call(bf16[512,512]{1,0:T(8,128)(2,1)S(1)} %get-tuple-element.23.mixed, bf16[512,512]{1,0:T(8,128)(2,1)S(1)} %get-tuple-element.24.awaited, bf16[192,512]{1,0:T(8,128)(2,1)S(1)} %collective-permute-done.12.refs_0_, bf16[192,512]{1,0:T(8,128)(2,1)S(1)} %collective-permute-done.13.refs_1_, ...), custom_call_target="tpu_custom_call" | custom-call | tf_op jit(solution)/shard_map/pallas_call | solution.py:41
  (19 shorter events, 0.3 us)
Async XLA Ops:
  0.0 5.3 %copy-start.3 = (s32[4,16,2]{1,2,0:T(2,128)S(1)}, s32[4,16,2]{1,2,0:T(2,128)}, u32[]{:S(2)}) copy-start(s32[4,16,2]{1,2,0:T(2,128)} %param.9) | copy-start | bytes 1540
  0.0 4.8 %copy-start.4 = (s32[4,16,4]{1,2,0:T(4,128)S(1)}, s32[4,16,4]{1,2,0:T(4,128)}, u32[]{:S(2)}) copy-start(s32[4,16,4]{1,2,0:T(4,128)} %param.8) | copy-start | bytes 3076
  0.0 6.1 %collective-permute-start.5 = (bf16[512,2048]{1,0:T(8,128)(2,1)}, bf16[512,2048]{1,0:T(8,128)(2,1)}, u32[]{:S(2)}, u32[]{:S(2)}) collective-permute-start(bf16[512,2048]{1,0:T(8,128)(2,1)} %refs_1_.1), channel_id=1, source_target_pairs={{0,1},{1,0},{2,3},{3,2},{4,5},{5,4},{6,7},{7,6},{8,9},{9,8},{10,11... | collective-permute-start | bytes 6291464 | tf_op jit(solution)/shard_map/ppermute | solution.py:31
  0.5 5.4 %collective-permute-start.6 = (bf16[512,1024]{1,0:T(8,128)(2,1)}, bf16[512,1024]{1,0:T(8,128)(2,1)S(1)}, u32[]{:S(2)}, u32[]{:S(2)}) collective-permute-start(bf16[512,1024]{1,0:T(8,128)(2,1)} %refs_7_.11), channel_id=1, source_target_pairs={{0,1},{1,0},{2,3},{3,2},{4,5},{5,4},{6,7},{7,6},{8,9},{9,8},{10,11... | collective-permute-start | bytes 3145736 | tf_op jit(solution)/shard_map/ppermute | solution.py:31
  0.5 4.8 %collective-permute-start = (s32[4,2,16]{2,1,0:T(2,128)}, s32[4,2,16]{2,1,0:T(2,128)S(1)}, u32[]{:S(2)}, u32[]{:S(2)}) collective-permute-start(s32[4,2,16]{2,1,0:T(2,128)} %bitcast.53), channel_id=1, source_target_pairs={{0,4},{1,5},{4,0},{5,1},{8,12},{9,13},{12,8},{13,9},{2,6},{3,7},{6... | collective-permute-start | bytes 1544 | tf_op jit(solution)/shard_map/ppermute | solution.py:26
  4.6 9.3 %collective-permute-start.2 = (bf16[256,512]{1,0:T(8,128)(2,1)S(1)}, bf16[256,512]{1,0:T(8,128)(2,1)S(1)}, u32[]{:S(2)}, u32[]{:S(2)}) collective-permute-start(bf16[256,512]{1,0:T(8,128)(2,1)S(1)} %bitcast.31), channel_id=1, source_target_pairs={{0,4},{1,5},{4,0},{5,1},{8,12},{9,13},{12,8},{13,9},{2,6},{3,7},{6... | collective-permute-start | bytes 786440 | tf_op jit(solution)/shard_map/ppermute | solution.py:26
  4.7 9.2 %collective-permute-start.3 = (bf16[256,512]{1,0:T(8,128)(2,1)S(1)}, bf16[256,512]{1,0:T(8,128)(2,1)S(1)}, u32[]{:S(2)}, u32[]{:S(2)}) collective-permute-start(bf16[256,512]{1,0:T(8,128)(2,1)S(1)} %bitcast.41), channel_id=1, source_target_pairs={{0,1},{1,0},{4,8},{5,9},{8,4},{9,5},{12,13},{13,12},{2,3},{3,2},{6... | collective-permute-start | bytes 786440 | tf_op jit(solution)/shard_map/ppermute | solution.py:26
  5.4 3.7 %collective-permute-start.1 = (s32[4,8,16]{2,1,0:T(8,128)S(1)}, s32[4,8,16]{2,1,0:T(8,128)S(1)}, u32[]{:S(2)}, u32[]{:S(2)}) collective-permute-start(s32[4,8,16]{2,1,0:T(8,128)S(1)} %fusion), channel_id=1, source_target_pairs={{0,1},{1,0},{2,3},{3,2},{4,5},{5,4},{6,7},{7,6},{8,9},{9,8},{10,11... | collective-permute-start | bytes 6152 | tf_op jit(solution)/shard_map/ppermute | solution.py:31
  6.1 12.9 %collective-permute-start.7 = (bf16[256,512]{1,0:T(8,128)(2,1)S(1)}, bf16[256,512]{1,0:T(8,128)(2,1)S(1)}, u32[]{:S(2)}, u32[]{:S(2)}) collective-permute-start(bf16[256,512]{1,0:T(8,128)(2,1)S(1)} %bitcast.42), channel_id=1, source_target_pairs={{0,4},{1,5},{4,0},{5,1},{8,12},{9,13},{12,8},{13,9},{2,6},{3,7},{6... | collective-permute-start | bytes 786440 | tf_op jit(solution)/shard_map/ppermute | solution.py:26
  9.0 10.0 %collective-permute-start.8 = (bf16[256,512]{1,0:T(8,128)(2,1)S(1)}, bf16[256,512]{1,0:T(8,128)(2,1)S(1)}, u32[]{:S(2)}, u32[]{:S(2)}) collective-permute-start(bf16[256,512]{1,0:T(8,128)(2,1)S(1)} %bitcast.32), channel_id=1, source_target_pairs={{0,1},{1,0},{4,8},{5,9},{8,4},{9,5},{12,13},{13,12},{2,3},{3,2},{6... | collective-permute-start | bytes 786440 | tf_op jit(solution)/shard_map/ppermute | solution.py:26
  14.0 5.0 %collective-permute-start.4 = (bf16[128,512]{1,0:T(8,128)(2,1)S(1)}, bf16[128,512]{1,0:T(8,128)(2,1)S(1)}, u32[]{:S(2)}, u32[]{:S(2)}) collective-permute-start(bf16[128,512]{1,0:T(8,128)(2,1)S(1)} %shard_map.64), channel_id=1, source_target_pairs={{0,2},{1,3},{2,0},{3,1},{4,6},{5,7},{6,4},{7,5},{8,10},{9,11},{10,... | collective-permute-start | bytes 393224 | tf_op jit(solution)/shard_map/ppermute | solution.py:26
  15.7 4.2 %copy-start.1 = (bf16[512,2048]{1,0:T(8,128)(2,1)S(1)}, bf16[512,2048]{1,0:T(8,128)(2,1)}, u32[]{:S(2)}) copy-start(bf16[512,2048]{1,0:T(8,128)(2,1)} %refs_1_.1) | copy-start | bytes 6291460
  19.1 5.0 %collective-permute-start.9 = (bf16[192,512]{1,0:T(8,128)(2,1)S(1)}, bf16[192,512]{1,0:T(8,128)(2,1)S(1)}, u32[]{:S(2)}, u32[]{:S(2)}) collective-permute-start(bf16[192,512]{1,0:T(8,128)(2,1)S(1)} %pad_maximum_fusion), channel_id=1, source_target_pairs={{0,1},{1,0},{4,8},{5,9},{8,4},{9,5},{12,13},{13,12},{2,3},{3,2},{6... | collective-permute-start | bytes 589832 | tf_op jit(solution)/shard_map/ppermute | solution.py:26
  19.2 11.6 %collective-permute-start.10 = (bf16[192,512]{1,0:T(8,128)(2,1)S(1)}, bf16[192,512]{1,0:T(8,128)(2,1)S(1)}, u32[]{:S(2)}, u32[]{:S(2)}) collective-permute-start(bf16[192,512]{1,0:T(8,128)(2,1)S(1)} %pad_maximum_fusion.1), channel_id=1, source_target_pairs={{0,1},{1,0},{4,8},{5,9},{8,4},{9,5},{12,13},{13,12},{2,3},{3,2},{6... | collective-permute-start | bytes 589832 | tf_op jit(solution)/shard_map/ppermute | solution.py:26
  19.8 4.3 %copy-start = (bf16[512,1024]{1,0:T(8,128)(2,1)S(1)}, bf16[512,1024]{1,0:T(8,128)(2,1)}, u32[]{:S(2)}) copy-start(bf16[512,1024]{1,0:T(8,128)(2,1)} %refs_7_.11) | copy-start | bytes 3145732
  19.8 13.2 %collective-permute-start.11 = (bf16[128,512]{1,0:T(8,128)(2,1)S(1)}, bf16[128,512]{1,0:T(8,128)(2,1)S(1)}, u32[]{:S(2)}, u32[]{:S(2)}) collective-permute-start(bf16[128,512]{1,0:T(8,128)(2,1)S(1)} %pad_maximum_fusion.2), channel_id=1, source_target_pairs={{0,1},{1,0},{4,8},{5,9},{8,4},{9,5},{12,13},{13,12},{2,3},{3,2},{6... | collective-permute-start | bytes 393224 | tf_op jit(solution)/shard_map/ppermute | solution.py:26
  24.1 15.7 %collective-permute-start.12 = (bf16[192,512]{1,0:T(8,128)(2,1)S(1)}, bf16[192,512]{1,0:T(8,128)(2,1)S(1)}, u32[]{:S(2)}, u32[]{:S(2)}) collective-permute-start(bf16[192,512]{1,0:T(8,128)(2,1)S(1)} %shard_map.66), channel_id=1, source_target_pairs={{0,4},{1,5},{4,0},{5,1},{8,12},{9,13},{12,8},{13,9},{2,6},{3,7},{6... | collective-permute-start | bytes 589832 | tf_op jit(solution)/shard_map/ppermute | solution.py:26
  30.8 9.0 %collective-permute-start.13 = (bf16[192,512]{1,0:T(8,128)(2,1)S(1)}, bf16[192,512]{1,0:T(8,128)(2,1)S(1)}, u32[]{:S(2)}, u32[]{:S(2)}) collective-permute-start(bf16[192,512]{1,0:T(8,128)(2,1)S(1)} %shard_map.67), channel_id=1, source_target_pairs={{0,4},{1,5},{4,0},{5,1},{8,12},{9,13},{12,8},{13,9},{2,6},{3,7},{6... | collective-permute-start | bytes 589832 | tf_op jit(solution)/shard_map/ppermute | solution.py:26
  33.0 6.9 %collective-permute-start.14 = (bf16[128,512]{1,0:T(8,128)(2,1)S(1)}, bf16[128,512]{1,0:T(8,128)(2,1)S(1)}, u32[]{:S(2)}, u32[]{:S(2)}) collective-permute-start(bf16[128,512]{1,0:T(8,128)(2,1)S(1)} %shard_map.68), channel_id=1, source_target_pairs={{0,4},{1,5},{4,0},{5,1},{8,12},{9,13},{12,8},{13,9},{2,6},{3,7},{6... | collective-permute-start | bytes 393224 | tf_op jit(solution)/shard_map/ppermute | solution.py:26
  34.6 0.7 %copy-start.2 = (s32[4,16]{1,0:T(4,128)S(1)}, s32[4,16]{1,0:T(4,128)}, u32[]{:S(2)}) copy-start(s32[4,16]{1,0:T(4,128)} %level_in.1) | copy-start | bytes 772

commit v5 on v4

--- a/solution.py
+++ b/solution.py
@@ -35,15 +35,15 @@
     return lax.optimization_barrier((tuple(arrays), first))[0]
 
 
-def call(kernel, rows, pixels, ints, arrays, scratch, outputs=1, left=0):
+def call(kernel, rows, pixels, ints, arrays, scratch, outputs=1, left=0, more=()):
     shape = jax.ShapeDtypeStruct((rows, pixels), jnp.bfloat16)
     vmem = pl.BlockSpec(memory_space=pltpu.VMEM)
     return pl.pallas_call(
         kernel,
-        out_shape=[shape] * outputs,
+        out_shape=[shape] * outputs + list(more),
         in_specs=[vmem] * (len(ints) + len(arrays) - left)
-        + [pl.BlockSpec(memory_space=pl.ANY)] * left,
-        out_specs=[vmem] * outputs,
+        + [pl.BlockSpec(memory_space=pltpu.HBM)] * left,
+        out_specs=[vmem] * (outputs + len(more)),
         scratch_shapes=scratch
         + [pltpu.SMEM(x.shape, x.dtype) for x in ints]
         + [pltpu.SemaphoreType.DMA] * len(ints),
@@ -71,13 +71,10 @@
     def blocks(self, value):
         return value.reshape(REACH, self.half, self.pixels)
 
-    def gather(self, blocks, chosen, base, index_of, units, slots, begin=0, count=None):
-        count = self.tile_rows if count is None else count
-
+    def gather(self, blocks, chosen, base, index_of, units, slots):
         def one_row(g, carry):
-            for unit in range(units):
-                at = base + (unit * count + g - begin) * self.group
-                at = pl.multiple_of(at, self.group)
+            for n, unit in enumerate(units):
+                at = pl.multiple_of(base + (n * self.tile_rows + g) * self.group, self.group)
                 for k in range(slots):
                     pair = [blocks[index_of(g, unit * REACH + i, k)] for i in range(REACH)]
                     chosen[pl.ds(at, self.group), k * self.pixels : (k + 1) * self.pixels] = (
@@ -85,7 +82,7 @@
                     )
             return carry
 
-        lax.fori_loop(begin, begin + count, one_row, 0)
+        lax.fori_loop(0, self.tile_rows, one_row, 0)
 
 
 def product(chosen, factors):
@@ -145,7 +142,7 @@
             def index_of(g, j, k):
                 return ints[g, plane[k] * tile.tile_cols + first * REACH + j] * width + j
 
-            tile.gather(blocks, chosen, n * count, index_of, units, 2 * slots)
+            tile.gather(blocks, chosen, n * count, index_of, range(units), 2 * slots)
         mean = product(chosen, (own_half, other_half))
         for n, (_, name) in enumerate(wanted):
             pieces, flag, start = shards[name]
@@ -179,28 +176,35 @@
         out[r * tile.group : (r + 1) * tile.group, :] = value.astype(jnp.bfloat16)
 
 
-def near_kernel(tile, slots, sides, ints_in, first, second, even, odd, *refs):
+def near_kernel(tile, slots, units, sides, ints_in, first, second, even, odd, *refs):
     *refs, ints, arrived = refs
     copy = pltpu.make_async_copy(ints_in, ints, arrived)
     copy.start()
     halos = refs[:sides]
-    own_half, other_half, out, blocks, chosen, *factors, factor_sem = refs[sides:]
-    loads = []
-    for i, source in enumerate((own_half, other_half)):
-        loads.append(pltpu.make_async_copy(source, factors[i], factor_sem.at[i]))
-        loads[i].start()
+    own_half, other_half, out, *refs = refs[sides:]
+    factors, loads = (own_half, other_half), []
+    if len(refs) > 2:
+        *factors, blocks, chosen, factor_sem = refs
+        for i, source in enumerate((own_half, other_half)):
+            loads.append(pltpu.make_async_copy(source, factors[i], factor_sem.at[i]))
+            loads[i].start()
+    else:
+        blocks, chosen = refs
     row, col = lax.axis_index("rows"), lax.axis_index("cols")
     above, below = row > 0, row < tile.rows - 1
     wide, last = tile.wide, tile.tile_rows + REACH
     nothing = jnp.zeros((REACH, tile.half, tile.pixels), jnp.float32)
+    read = sorted({u + i for u in units for i in (-1, 0, 1)} & set(range(tile.units)))
     for r in range(last + REACH):
         inside = above if r < REACH else below if r >= last else None
-        for unit in range(tile.units):
+        for unit in read:
             if inside is None:
                 value = tile.read((first, second), 0, row, unit, r - REACH)
             else:
                 value = jnp.where(inside, halo(tile, row, even, odd, unit, r), 0.0)
             blocks[pl.ds(r * wide + REACH + unit * REACH, REACH)] = tile.blocks(value)
+        if not {0, tile.units - 1} & set(units):
+            continue
         left, right = nothing, nothing
         for parity in range(sides):
             value = halos[parity][r * tile.group : (r + 1) * tile.group, :].astype(jnp.float32)
@@ -217,18 +221,18 @@
         return ints[g, k * tile.tile_cols + j]
 
     copy.wait()
-    tile.gather(blocks, chosen, 0, index_of, tile.units, 2 * slots)
+    tile.gather(blocks, chosen, 0, index_of, units, 2 * slots)
     for load in loads:
         load.wait()
     mean = product(chosen, factors)
-    for unit in range(tile.units):
+    for n, unit in enumerate(units):
         for g in range(tile.tile_rows):
-            at = (unit * tile.tile_rows + g) * tile.group
+            at = (n * tile.tile_rows + g) * tile.group
             value = tile.read((first, second), 0, row, unit, g)
             out[at : at + tile.group, :] = (value - mean[at : at + tile.group, :]).astype(jnp.bfloat16)
 
 
-def mix_kernel(tile, parts, level_in, near, *refs):
+def mix_kernel(tile, parts, inner, outer, level_in, near_in, near_out, *refs):
     *refs, level, arrived = refs
     copy = pltpu.make_async_copy(level_in, level, arrived)
     copy.start()
@@ -243,7 +247,10 @@
             for g in range(tile.tile_rows):
                 at = (unit * tile.tile_rows + g) * tile.group
                 far = own[c][at : at + tile.group, :].astype(jnp.float32)
-                at = ((first + unit) * tile.tile_rows + g) * tile.group
+                near, n = near_in, inner.index(first + unit) if first + unit in inner else 0
+                if first + unit in outer:
+                    near, n = near_out, outer.index(first + unit)
+                at = (n * tile.tile_rows + g) * tile.group
                 fine = near[at : at + tile.group, :].astype(jnp.float32)
                 levels = level[g, (first + unit) * REACH]
                 for i in range(1, REACH):
@@ -322,25 +329,31 @@
     near_ints, far_ints = (x.reshape(tile_rows, -1) for x in (near_ints, far_ints))
 
     size = tile_rows * tile_cols * half
-    (near_own,) = call(
-        functools.partial(near_kernel, tile, near_slots, len(halos)),
-        size, pixels, [near_ints], [*beside, *halos, near_factor, near_other],
-        [
+    inner_units, outer_units = list(range(1, tile.units - 1)), [0, tile.units - 1]
+
+    def near_part(units, sides, factors, bring):
+        count = tile_rows * len(units) * tile.group
+        scratch = [
             pltpu.VMEM(((tile_rows + 2 * REACH) * tile.wide, half, pixels), jnp.float32),
-            pltpu.VMEM((size, 2 * near_slots * pixels), jnp.bfloat16),
-            pltpu.VMEM(near_factor.shape, near_factor.dtype),
-            pltpu.VMEM(near_factor.shape, near_factor.dtype),
-            pltpu.SemaphoreType.DMA((2,)),
-        ],
-        left=2,
-    )
+            pltpu.VMEM((count, 2 * near_slots * pixels), jnp.bfloat16),
+        ]
+        return call(
+            functools.partial(near_kernel, tile, near_slots, units, len(sides)),
+            count, pixels, [near_ints], [*beside, *sides, *factors],
+            scratch + [pltpu.SemaphoreType.DMA((2,))] * bring,
+            left=2 * bring,
+            more=[jax.ShapeDtypeStruct(x.shape, x.dtype) for x in factors] * bring,
+        )
+
+    near_inner, *brought = near_part(inner_units, [], [near_factor, near_other], 1)
+    (near_outer,) = near_part(outer_units, halos, brought, 0)
 
     inner = rows > 4
     for step in range(1, rows - 3):
         if inner:
             even.append([exchange(x, "rows", 0) for x in odd[step - 1]])
         odd.append([exchange(x, "rows", 1) for x in even[step - 1]])
-    source = after(even[rows - 4], near_ints, far_ints, *halos, odd[0][1])
+    source = after(even[rows - 4], near_inner, far_ints, *halos, odd[0][1])
     def cut(pieces, c):
         spots = slice(starts[c] * tile.unit, (starts[c] + parts[c]) * tile.unit)
         return jnp.concatenate([x[spots] for x in pieces], axis=0)
@@ -376,14 +389,14 @@
     partner = ([far_slots + k for k in slots], (0, 0))
     mine = (slots, (0, -1))
     ready = []
-    sent = near_own
+    sent = near_outer
     for c in range(len(parts)):
         (sent,) = far_chunk(c, [partner], sent)
         ready.append(exchange(sent, "rows", 0))
     far_own = [far_chunk(c, [mine], sent)[0] for c in range(len(parts))]
     mixed, awaited = call(
-        functools.partial(mix_kernel, tile, parts),
-        size, pixels, [block_level], [near_own, *far_own], [], 2,
+        functools.partial(mix_kernel, tile, parts, inner_units, outer_units),
+        size, pixels, [block_level], [near_inner, near_outer, *far_own], [], 2,
     )
     (result,) = call(
         functools.partial(final_kernel, tile, parts),

time: 41 us -> 39.3 us (0.959)
  waiting for transfers between devices: 12.9 us -> 7.89 us
  Pallas kernels: 6.11 us -> 8.22 us
  starting transfers between devices: 19.4 us -> 20.6 us
    ppermute x12, waiting for transfers between devices: 12.3 us -> 7.28 us  [exchange(): return lax.ppermute(array, (axis, 'sub'), pairs)]
    pallas_call x10 -> x11, Pallas kernels: 6.11 us -> 8.22 us  [call(): pl.pallas_call(kernel, out_shape=[shape] * outputs + list(more), in_specs...]
    ppermute x12, starting transfers between devices: 18.8 us -> 20 us  [exchange(): return lax.ppermute(array, (axis, 'sub'), pairs)]
  transfers between devices with their start and end apart: 15 -> 15, of which waited for: 6 -> 5; matrix products, arithmetic and copies ran while one was open for 3% -> 4% of each run, Pallas kernels for 13% -> 19%
where the time goes in v5:
time: 39.3 us; the launch traced here: 39.1 us
  starting transfers between devices  20.6 us (52%)
  Pallas kernels  8.22 us (21%)
  waiting for transfers between devices  7.89 us (20%)
  local copies, waits for them, and re-layouts  1.96 us (5%)
    ppermute x12, starting transfers between devices, exchange(): return lax.ppermute(array, (axis, 'sub'), pairs)  20 us
    pallas_call x11, Pallas kernels, call(): pl.pallas_call(kernel, out_shape=[shape] * outputs + list(more), in_specs...  8.22 us
    ppermute x12, waiting for transfers between devices, exchange(): return lax.ppermute(array, (axis, 'sub'), pairs)  7.28 us
    dynamic_slice x1, local copies, waits for them, and re-layouts, on_device(): lax.dynamic_slice(convergence, (start, 0, sub * half, 0), (tile.split, ti...  1.06 us
  transfers between devices with their start and end apart: 15, of which 5 were waited for; matrix products, arithmetic and copies ran while one was open for 4% of the time, Pallas kernels for 19%

profile of v5, /device:TPU:0, one launch (start us, length us, event | category | flops | bytes accessed | tf_op | source)
XLA Modules:
  0.0 39.1 jit_solution(13063967769127393621)
XLA Ops:
  0.0 0.0 copy-start.2
  0.0 0.0 copy-start.3
  0.0 0.5 %collective-permute-start.4 = (bf16[512,2048]{1,0:T(8,128)(2,1)}, bf16[512,2048]{1,0:T(8,128)(2,1)}, u32[]{:S(2)}, u32[]{:S(2)}) collective-permute-start(bf16[512,2048]{1,0:T(8,128)(2,1)} %refs_0_.1), channel_id=1, source_target_pairs={{0,1},{1,0},{2,3},{3,2},{4,5},{5,4},{6,7},{7,6},{8,9},{9,8},{10,11... | collective-permute-start | bytes 6291464 | tf_op jit(solution)/shard_map/ppermute | solution.py:31
  0.5 0.1 collective-permute-start.6
  0.5 3.0 %collective-permute-start = (s32[4,2,16]{2,1,0:T(2,128)}, s32[4,2,16]{2,1,0:T(2,128)S(1)}, u32[]{:S(2)}, u32[]{:S(2)}) collective-permute-start(s32[4,2,16]{2,1,0:T(2,128)} %bitcast.55), channel_id=1, source_target_pairs={{0,4},{1,5},{4,0},{5,1},{8,12},{9,13},{12,8},{13,9},{2,6},{3,7},{6... | collective-permute-start | bytes 1544 | tf_op jit(solution)/shard_map/ppermute | solution.py:26
  3.5 1.1 %constant_dynamic-slice_fusion = (bf16[2,16,8,512]{3,2,1,0:T(8,128)(2,1)S(1)}, bf16[2,16,8,512]{3,2,1,0:T(8,128)(2,1)S(1)}) fusion(bf16[4,16,16,512]{3,2,1,0:T(8,128)(2,1)} %param.6, s32[]{:T(128)S(6)} %select_n.31, s32[]{:T(128)S(6)} %select_n.30, s32[]{:T(128)S(6)} %select_n.29), kind=kLoop, calls=%fused_computation.17 | loop fusion | bytes 1048588 | tf_op jit(solution)/shard_map/dynamic_slice | solution.py:295
  4.6 0.1 collective-permute-start.2
  4.7 0.1 collective-permute-start.3
  4.8 0.0 copy-done.3
  4.8 0.1 fusion.4
  4.9 0.4 %collective-permute-done = s32[4,2,16]{2,1,0:T(2,128)S(1)} collective-permute-done((s32[4,2,16]{2,1,0:T(2,128)}, s32[4,2,16]{2,1,0:T(2,128)S(1)}, u32[]{:S(2)}, u32[]{:S(2)}) %collective-permute-start) | collective-permute-done | bytes 544 | tf_op jit(solution)/shard_map/ppermute | solution.py:26
  5.3 0.0 copy-done.2
  5.4 0.1 collective-permute-start.1
  5.5 0.4 %collective-permute-done.6.refs_8_ = bf16[512,1024]{1,0:T(8,128)(2,1)S(1)} collective-permute-done((bf16[512,1024]{1,0:T(8,128)(2,1)}, bf16[512,1024]{1,0:T(8,128)(2,1)S(1)}, u32[]{:S(2)}, u32[]{:S(2)}) %collective-permute-start.6) | collective-permute-done | bytes 1048608 | tf_op jit(solution)/shard_map/ppermute | solution.py:31
  5.9 0.2 collective-permute-done.4.refs_1_
  6.1 2.9 %collective-permute-start.7 = (bf16[256,512]{1,0:T(8,128)(2,1)S(1)}, bf16[256,512]{1,0:T(8,128)(2,1)S(1)}, u32[]{:S(2)}, u32[]{:S(2)}) collective-permute-start(bf16[256,512]{1,0:T(8,128)(2,1)S(1)} %bitcast.43), channel_id=1, source_target_pairs={{0,4},{1,5},{4,0},{5,1},{8,12},{9,13},{12,8},{13,9},{2,6},{3,7},{6... | collective-permute-start | bytes 786440 | tf_op jit(solution)/shard_map/ppermute | solution.py:26
  9.0 0.0 collective-permute-start.8
  9.0 0.0 collective-permute-done.1
  9.0 4.9 %collective-permute-done.2.even.refs_2_ = bf16[256,512]{1,0:T(8,128)(2,1)S(1)} collective-permute-done((bf16[256,512]{1,0:T(8,128)(2,1)S(1)}, bf16[256,512]{1,0:T(8,128)(2,1)S(1)}, u32[]{:S(2)}, u32[]{:S(2)}) %collective-permute-start.2) | collective-permute-done | bytes 262176 | tf_op jit(solution)/shard_map/ppermute | solution.py:26
  13.9 0.0 collective-permute-done.3.odd.refs_4_
  13.9 0.1 shard_map.65
  14.0 1.6 %collective-permute-start.5 = (bf16[128,512]{1,0:T(8,128)(2,1)S(1)}, bf16[128,512]{1,0:T(8,128)(2,1)S(1)}, u32[]{:S(2)}, u32[]{:S(2)}) collective-permute-start(bf16[128,512]{1,0:T(8,128)(2,1)S(1)} %shard_map.65), channel_id=1, source_target_pairs={{0,2},{1,3},{2,0},{3,1},{4,6},{5,7},{6,4},{7,5},{8,10},{9,11},{10,... | collective-permute-start | bytes 393224 | tf_op jit(solution)/shard_map/ppermute | solution.py:26
  15.6 0.1 reshape.26.ints_in
  15.7 0.1 reshape.31.ints_in
  15.7 4.1 %shard_map.64 = (bf16[384,512]{1,0:T(8,128)(2,1)S(1)}, bf16[512,2048]{1,0:T(8,128)(2,1)S(1)}, bf16[512,2048]{1,0:T(8,128)(2,1)S(1)}) custom-call(s32[4,128]{1,0:T(4,128)S(1)} %reshape.26.ints_in, bf16[256,512]{1,0:T(8,128)(2,1)S(1)} %bitcast.34, bf16[256,512]{1,0:T(8,128)(2,1)S(1)} %bitcast.45, bf16[256,512]{1,0:T(8,128)(2,1)S(1)} %collective-permute-done.2.even.refs_2_, ...), custom_call_target="tpu_custom_call" | custom-call | tf_op jit(solution)/shard_map/pallas_call | solution.py:41
  19.8 0.0 collective-permute-done.5.refs_0_
  19.8 0.0 collective-permute-done.7.refs_3_
  19.8 0.0 collective-permute-done.8.refs_5_
  19.9 0.1 collective-permute-start.9
  20.0 0.6 %collective-permute-start.10 = (bf16[192,512]{1,0:T(8,128)(2,1)S(1)}, bf16[192,512]{1,0:T(8,128)(2,1)S(1)}, u32[]{:S(2)}, u32[]{:S(2)}) collective-permute-start(bf16[192,512]{1,0:T(8,128)(2,1)S(1)} %pad_maximum_fusion.1), channel_id=1, source_target_pairs={{0,1},{1,0},{4,8},{5,9},{8,4},{9,5},{12,13},{13,12},{2,3},{3,2},{6... | collective-permute-start | bytes 589832 | tf_op jit(solution)/shard_map/ppermute | solution.py:26
  20.6 0.1 collective-permute-start.11
  20.7 0.0 copy-start
  20.7 2.2 %shard_map.66.near_out = bf16[128,512]{1,0:T(8,128)(2,1)S(1)} custom-call(s32[4,128]{1,0:T(4,128)S(1)} %reshape.26.ints_in, bf16[256,512]{1,0:T(8,128)(2,1)S(1)} %bitcast.35, bf16[256,512]{1,0:T(8,128)(2,1)S(1)} %bitcast.46, bf16[256,512]{1,0:T(8,128)(2,1)S(1)} %collective-permute-done.2.even.refs_2_, ...), custom_call_target="tpu_custom_call" | custom-call | tf_op jit(solution)/shard_map/pallas_call | solution.py:41
  22.9 0.0 collective-permute-done.9.refs_6_
  22.9 0.0 copy-done
  23.0 7.9 %collective-permute-start.12 = (bf16[192,512]{1,0:T(8,128)(2,1)S(1)}, bf16[192,512]{1,0:T(8,128)(2,1)S(1)}, u32[]{:S(2)}, u32[]{:S(2)}) collective-permute-start(bf16[192,512]{1,0:T(8,128)(2,1)S(1)} %shard_map.67), channel_id=1, source_target_pairs={{0,4},{1,5},{4,0},{5,1},{8,12},{9,13},{12,8},{13,9},{2,6},{3,7},{6... | collective-permute-start | bytes 589832 | tf_op jit(solution)/shard_map/ppermute | solution.py:26
  30.9 0.0 collective-permute-done.10.refs_6_
  30.9 2.1 %collective-permute-start.13 = (bf16[192,512]{1,0:T(8,128)(2,1)S(1)}, bf16[192,512]{1,0:T(8,128)(2,1)S(1)}, u32[]{:S(2)}, u32[]{:S(2)}) collective-permute-start(bf16[192,512]{1,0:T(8,128)(2,1)S(1)} %shard_map.68), channel_id=1, source_target_pairs={{0,4},{1,5},{4,0},{5,1},{8,12},{9,13},{12,8},{13,9},{2,6},{3,7},{6... | collective-permute-start | bytes 589832 | tf_op jit(solution)/shard_map/ppermute | solution.py:26
  33.0 0.0 collective-permute-done.11.refs_6_
  33.0 1.6 %collective-permute-start.14 = (bf16[128,512]{1,0:T(8,128)(2,1)S(1)}, bf16[128,512]{1,0:T(8,128)(2,1)S(1)}, u32[]{:S(2)}, u32[]{:S(2)}) collective-permute-start(bf16[128,512]{1,0:T(8,128)(2,1)S(1)} %shard_map.69), channel_id=1, source_target_pairs={{0,4},{1,5},{4,0},{5,1},{8,12},{9,13},{12,8},{13,9},{2,6},{3,7},{6... | collective-permute-start | bytes 393224 | tf_op jit(solution)/shard_map/ppermute | solution.py:26
  34.7 0.0 copy-start.1
  34.7 0.6 %copy-done.1 = s32[4,16]{1,0:T(4,128)S(1)} copy-done((s32[4,16]{1,0:T(4,128)S(1)}, s32[4,16]{1,0:T(4,128)}, u32[]{:S(2)}) %copy-start.1) | copy-done | bytes 280
  35.4 0.7 %shard_map.73 = (bf16[512,512]{1,0:T(8,128)(2,1)S(1)}, bf16[512,512]{1,0:T(8,128)(2,1)S(1)}) custom-call(s32[4,16]{1,0:T(4,128)S(1)} %copy-done.1, bf16[384,512]{1,0:T(8,128)(2,1)S(1)} %get-tuple-element.18.near_in, bf16[128,512]{1,0:T(8,128)(2,1)S(1)} %shard_map.66.near_out, bf16[192,512]{1,0:T(8,128)(2,1)S(1)} %shard_map.70.refs_0_, ...), custom_call_target="tpu_custom_call" | custom-call | tf_op jit(solution)/shard_map/pallas_call | solution.py:41
  36.1 2.0 %collective-permute-done.14.refs_2_ = bf16[128,512]{1,0:T(8,128)(2,1)S(1)} collective-permute-done((bf16[128,512]{1,0:T(8,128)(2,1)S(1)}, bf16[128,512]{1,0:T(8,128)(2,1)S(1)}, u32[]{:S(2)}, u32[]{:S(2)}) %collective-permute-start.14) | collective-permute-done | bytes 131104 | tf_op jit(solution)/shard_map/ppermute | solution.py:26
  38.1 0.0 collective-permute-done.12.refs_0_
  38.1 0.0 collective-permute-done.13.refs_1_
  38.1 1.0 %shard_map.74 = bf16[512,512]{1,0:T(8,128)(2,1)} custom-call(bf16[512,512]{1,0:T(8,128)(2,1)S(1)} %get-tuple-element.29.mixed, bf16[512,512]{1,0:T(8,128)(2,1)S(1)} %get-tuple-element.30.awaited, bf16[192,512]{1,0:T(8,128)(2,1)S(1)} %collective-permute-done.12.refs_0_, bf16[192,512]{1,0:T(8,128)(2,1)S(1)} %collective-permute-done.13.refs_1_, ...), custom_call_target="tpu_custom_call" | custom-call | tf_op jit(solution)/shard_map/pallas_call | solution.py:41
  (19 shorter events, 0.3 us)
Async XLA Ops:
  0.0 5.3 %copy-start.2 = (s32[4,16,2]{1,2,0:T(2,128)S(1)}, s32[4,16,2]{1,2,0:T(2,128)}, u32[]{:S(2)}) copy-start(s32[4,16,2]{1,2,0:T(2,128)} %param.9) | copy-start | bytes 1540
  0.0 4.8 %copy-start.3 = (s32[4,16,4]{1,2,0:T(4,128)S(1)}, s32[4,16,4]{1,2,0:T(4,128)}, u32[]{:S(2)}) copy-start(s32[4,16,4]{1,2,0:T(4,128)} %param.8) | copy-start | bytes 3076
  0.0 6.1 %collective-permute-start.4 = (bf16[512,2048]{1,0:T(8,128)(2,1)}, bf16[512,2048]{1,0:T(8,128)(2,1)}, u32[]{:S(2)}, u32[]{:S(2)}) collective-permute-start(bf16[512,2048]{1,0:T(8,128)(2,1)} %refs_0_.1), channel_id=1, source_target_pairs={{0,1},{1,0},{2,3},{3,2},{4,5},{5,4},{6,7},{7,6},{8,9},{9,8},{10,11... | collective-permute-start | bytes 6291464 | tf_op jit(solution)/shard_map/ppermute | solution.py:31
  0.5 5.4 %collective-permute-start.6 = (bf16[512,1024]{1,0:T(8,128)(2,1)}, bf16[512,1024]{1,0:T(8,128)(2,1)S(1)}, u32[]{:S(2)}, u32[]{:S(2)}) collective-permute-start(bf16[512,1024]{1,0:T(8,128)(2,1)} %refs_7_.11), channel_id=1, source_target_pairs={{0,1},{1,0},{2,3},{3,2},{4,5},{5,4},{6,7},{7,6},{8,9},{9,8},{10,11... | collective-permute-start | bytes 3145736 | tf_op jit(solution)/shard_map/ppermute | solution.py:31
  0.5 4.8 %collective-permute-start = (s32[4,2,16]{2,1,0:T(2,128)}, s32[4,2,16]{2,1,0:T(2,128)S(1)}, u32[]{:S(2)}, u32[]{:S(2)}) collective-permute-start(s32[4,2,16]{2,1,0:T(2,128)} %bitcast.55), channel_id=1, source_target_pairs={{0,4},{1,5},{4,0},{5,1},{8,12},{9,13},{12,8},{13,9},{2,6},{3,7},{6... | collective-permute-start | bytes 1544 | tf_op jit(solution)/shard_map/ppermute | solution.py:26
  4.6 9.3 %collective-permute-start.2 = (bf16[256,512]{1,0:T(8,128)(2,1)S(1)}, bf16[256,512]{1,0:T(8,128)(2,1)S(1)}, u32[]{:S(2)}, u32[]{:S(2)}) collective-permute-start(bf16[256,512]{1,0:T(8,128)(2,1)S(1)} %bitcast.31), channel_id=1, source_target_pairs={{0,4},{1,5},{4,0},{5,1},{8,12},{9,13},{12,8},{13,9},{2,6},{3,7},{6... | collective-permute-start | bytes 786440 | tf_op jit(solution)/shard_map/ppermute | solution.py:26
  4.7 9.2 %collective-permute-start.3 = (bf16[256,512]{1,0:T(8,128)(2,1)S(1)}, bf16[256,512]{1,0:T(8,128)(2,1)S(1)}, u32[]{:S(2)}, u32[]{:S(2)}) collective-permute-start(bf16[256,512]{1,0:T(8,128)(2,1)S(1)} %bitcast.42), channel_id=1, source_target_pairs={{0,1},{1,0},{4,8},{5,9},{8,4},{9,5},{12,13},{13,12},{2,3},{3,2},{6... | collective-permute-start | bytes 786440 | tf_op jit(solution)/shard_map/ppermute | solution.py:26
  5.4 3.7 %collective-permute-start.1 = (s32[4,8,16]{2,1,0:T(8,128)S(1)}, s32[4,8,16]{2,1,0:T(8,128)S(1)}, u32[]{:S(2)}, u32[]{:S(2)}) collective-permute-start(s32[4,8,16]{2,1,0:T(8,128)S(1)} %fusion), channel_id=1, source_target_pairs={{0,1},{1,0},{2,3},{3,2},{4,5},{5,4},{6,7},{7,6},{8,9},{9,8},{10,11... | collective-permute-start | bytes 6152 | tf_op jit(solution)/shard_map/ppermute | solution.py:31
  6.1 13.7 %collective-permute-start.7 = (bf16[256,512]{1,0:T(8,128)(2,1)S(1)}, bf16[256,512]{1,0:T(8,128)(2,1)S(1)}, u32[]{:S(2)}, u32[]{:S(2)}) collective-permute-start(bf16[256,512]{1,0:T(8,128)(2,1)S(1)} %bitcast.43), channel_id=1, source_target_pairs={{0,4},{1,5},{4,0},{5,1},{8,12},{9,13},{12,8},{13,9},{2,6},{3,7},{6... | collective-permute-start | bytes 786440 | tf_op jit(solution)/shard_map/ppermute | solution.py:26
  9.0 10.8 %collective-permute-start.8 = (bf16[256,512]{1,0:T(8,128)(2,1)S(1)}, bf16[256,512]{1,0:T(8,128)(2,1)S(1)}, u32[]{:S(2)}, u32[]{:S(2)}) collective-permute-start(bf16[256,512]{1,0:T(8,128)(2,1)S(1)} %bitcast.32), channel_id=1, source_target_pairs={{0,1},{1,0},{4,8},{5,9},{8,4},{9,5},{12,13},{13,12},{2,3},{3,2},{6... | collective-permute-start | bytes 786440 | tf_op jit(solution)/shard_map/ppermute | solution.py:26
  14.0 5.8 %collective-permute-start.5 = (bf16[128,512]{1,0:T(8,128)(2,1)S(1)}, bf16[128,512]{1,0:T(8,128)(2,1)S(1)}, u32[]{:S(2)}, u32[]{:S(2)}) collective-permute-start(bf16[128,512]{1,0:T(8,128)(2,1)S(1)} %shard_map.65), channel_id=1, source_target_pairs={{0,2},{1,3},{2,0},{3,1},{4,6},{5,7},{6,4},{7,5},{8,10},{9,11},{10,... | collective-permute-start | bytes 393224 | tf_op jit(solution)/shard_map/ppermute | solution.py:26
  19.9 3.0 %collective-permute-start.9 = (bf16[192,512]{1,0:T(8,128)(2,1)S(1)}, bf16[192,512]{1,0:T(8,128)(2,1)S(1)}, u32[]{:S(2)}, u32[]{:S(2)}) collective-permute-start(bf16[192,512]{1,0:T(8,128)(2,1)S(1)} %pad_maximum_fusion), channel_id=1, source_target_pairs={{0,1},{1,0},{4,8},{5,9},{8,4},{9,5},{12,13},{13,12},{2,3},{3,2},{6... | collective-permute-start | bytes 589832 | tf_op jit(solution)/shard_map/ppermute | solution.py:26
  20.0 10.9 %collective-permute-start.10 = (bf16[192,512]{1,0:T(8,128)(2,1)S(1)}, bf16[192,512]{1,0:T(8,128)(2,1)S(1)}, u32[]{:S(2)}, u32[]{:S(2)}) collective-permute-start(bf16[192,512]{1,0:T(8,128)(2,1)S(1)} %pad_maximum_fusion.1), channel_id=1, source_target_pairs={{0,1},{1,0},{4,8},{5,9},{8,4},{9,5},{12,13},{13,12},{2,3},{3,2},{6... | collective-permute-start | bytes 589832 | tf_op jit(solution)/shard_map/ppermute | solution.py:26
  20.6 12.4 %collective-permute-start.11 = (bf16[128,512]{1,0:T(8,128)(2,1)S(1)}, bf16[128,512]{1,0:T(8,128)(2,1)S(1)}, u32[]{:S(2)}, u32[]{:S(2)}) collective-permute-start(bf16[128,512]{1,0:T(8,128)(2,1)S(1)} %pad_maximum_fusion.2), channel_id=1, source_target_pairs={{0,1},{1,0},{4,8},{5,9},{8,4},{9,5},{12,13},{13,12},{2,3},{3,2},{6... | collective-permute-start | bytes 393224 | tf_op jit(solution)/shard_map/ppermute | solution.py:26
  20.7 2.2 %copy-start = (bf16[512,1024]{1,0:T(8,128)(2,1)S(1)}, bf16[512,1024]{1,0:T(8,128)(2,1)}, u32[]{:S(2)}) copy-start(bf16[512,1024]{1,0:T(8,128)(2,1)} %refs_7_.11) | copy-start | bytes 3145732
  23.0 15.1 %collective-permute-start.12 = (bf16[192,512]{1,0:T(8,128)(2,1)S(1)}, bf16[192,512]{1,0:T(8,128)(2,1)S(1)}, u32[]{:S(2)}, u32[]{:S(2)}) collective-permute-start(bf16[192,512]{1,0:T(8,128)(2,1)S(1)} %shard_map.67), channel_id=1, source_target_pairs={{0,4},{1,5},{4,0},{5,1},{8,12},{9,13},{12,8},{13,9},{2,6},{3,7},{6... | collective-permute-start | bytes 589832 | tf_op jit(solution)/shard_map/ppermute | solution.py:26
  30.9 7.2 %collective-permute-start.13 = (bf16[192,512]{1,0:T(8,128)(2,1)S(1)}, bf16[192,512]{1,0:T(8,128)(2,1)S(1)}, u32[]{:S(2)}, u32[]{:S(2)}) collective-permute-start(bf16[192,512]{1,0:T(8,128)(2,1)S(1)} %shard_map.68), channel_id=1, source_target_pairs={{0,4},{1,5},{4,0},{5,1},{8,12},{9,13},{12,8},{13,9},{2,6},{3,7},{6... | collective-permute-start | bytes 589832 | tf_op jit(solution)/shard_map/ppermute | solution.py:26
  33.0 5.1 %collective-permute-start.14 = (bf16[128,512]{1,0:T(8,128)(2,1)S(1)}, bf16[128,512]{1,0:T(8,128)(2,1)S(1)}, u32[]{:S(2)}, u32[]{:S(2)}) collective-permute-start(bf16[128,512]{1,0:T(8,128)(2,1)S(1)} %shard_map.69), channel_id=1, source_target_pairs={{0,4},{1,5},{4,0},{5,1},{8,12},{9,13},{12,8},{13,9},{2,6},{3,7},{6... | collective-permute-start | bytes 393224 | tf_op jit(solution)/shard_map/ppermute | solution.py:26
  34.7 0.7 %copy-start.1 = (s32[4,16]{1,0:T(4,128)S(1)}, s32[4,16]{1,0:T(4,128)}, u32[]{:S(2)}) copy-start(s32[4,16]{1,0:T(4,128)} %level_in.1) | copy-start | bytes 772

commit v6 on v5

--- a/solution.py
+++ b/solution.py
@@ -237,7 +237,7 @@
     copy = pltpu.make_async_copy(level_in, level, arrived)
     copy.start()
     copy.wait()
-    own, out, awaited = refs[: len(parts)], refs[-2], refs[-1]
+    own, (out, awaited, whole, stored) = refs[: len(parts)], refs[len(parts) :]
     row = lax.axis_index("rows")
     at_end = (row == 0) | (row == tile.rows - 1)
     lower = lax.broadcasted_iota(jnp.int32, (tile.group, tile.pixels), 0) // tile.half
@@ -261,22 +261,37 @@
                 wait = jnp.where((levels != 1) & at_end, 1.0, 0.0)
                 awaited[at : at + tile.group, :] = wait.astype(jnp.bfloat16)
         first += units
-
-
-def final_kernel(tile, parts, mixed, awaited, *refs):
-    out = refs[-1]
-    first = 0
-    for c, units in enumerate(parts):
-        for unit in range(units):
-            for g in range(tile.tile_rows):
-                at = (unit * tile.tile_rows + g) * tile.group
-                at_out = (g * tile.units + first + unit) * tile.group
-                spot = slice(at_out, at_out + tile.group)
-                far = refs[c][at : at + tile.group, :].astype(jnp.float32)
-                value = mixed[spot, :].astype(jnp.float32)
-                value = jnp.where(awaited[spot, :].astype(jnp.float32) > 0.5, far, value)
-                out[spot, :] = value.astype(jnp.bfloat16)
-        first += units
+    store = pltpu.make_async_copy(out, whole, stored)
+    store.start()
+    store.wait()
+
+
+def final_kernel(tile, parts, first, mixed, awaited, *refs):
+    ready, (_, out, chosen, done) = refs[: len(parts)], refs[len(parts) :]
+    row = lax.axis_index("rows")
+
+    @pl.when((row == 0) | (row == tile.rows - 1))
+    def _():
+        span = sum(parts) * tile.group
+        copies = []
+        for g in range(tile.tile_rows):
+            begin = (g * tile.units + first) * tile.group
+            shift = 0
+            for c, units in enumerate(parts):
+                for unit in range(units):
+                    at = (unit * tile.tile_rows + g) * tile.group
+                    spot = slice(begin + shift, begin + shift + tile.group)
+                    far = ready[c][at : at + tile.group, :].astype(jnp.float32)
+                    value = mixed[spot, :].astype(jnp.float32)
+                    value = jnp.where(awaited[spot, :].astype(jnp.float32) > 0.5, far, value)
+                    at = g * span + shift
+                    chosen[at : at + tile.group, :] = value.astype(jnp.bfloat16)
+                    shift += tile.group
+            part = chosen.at[pl.ds(g * span, span), :]
+            copies.append(pltpu.make_async_copy(part, out.at[pl.ds(begin, span), :], done.at[g]))
+            copies[g].start()
+        for copy in copies:
+            copy.wait()
 
 
 def on_device(convergence, block_level, near_codes, far_rows, near_factor, far_factor):
@@ -394,14 +409,35 @@
         (sent,) = far_chunk(c, [partner], sent)
         ready.append(exchange(sent, "rows", 0))
     far_own = [far_chunk(c, [mine], sent)[0] for c in range(len(parts))]
-    mixed, awaited = call(
+    vmem, hbm = (pl.BlockSpec(memory_space=space) for space in (pltpu.VMEM, pltpu.HBM))
+    params = pltpu.CompilerParams(vmem_limit_bytes=VMEM_BYTES)
+    shape = jax.ShapeDtypeStruct((size, pixels), jnp.bfloat16)
+    mixed, awaited, result = pl.pallas_call(
         functools.partial(mix_kernel, tile, parts, inner_units, outer_units),
-        size, pixels, [block_level], [near_inner, near_outer, *far_own], [], 2,
-    )
-    (result,) = call(
-        functools.partial(final_kernel, tile, parts),
-        size, pixels, [], [mixed, awaited, *ready], [],
-    )
+        out_shape=[shape] * 3,
+        in_specs=[vmem] * (3 + len(parts)),
+        out_specs=[vmem, vmem, hbm],
+        scratch_shapes=[
+            pltpu.SemaphoreType.DMA,
+            pltpu.SMEM(block_level.shape, block_level.dtype),
+            pltpu.SemaphoreType.DMA,
+        ],
+        compiler_params=params,
+    )(block_level, near_inner, near_outer, *far_own)
+    for some in (range(len(parts) - 1), range(len(parts) - 1, len(parts))):
+        units = [parts[c] for c in some]
+        result = pl.pallas_call(
+            functools.partial(final_kernel, tile, units, starts[some[0]]),
+            out_shape=shape,
+            in_specs=[vmem] * (2 + len(units)) + [hbm],
+            out_specs=hbm,
+            scratch_shapes=[
+                pltpu.VMEM((tile_rows * sum(units) * tile.group, pixels), jnp.bfloat16),
+                pltpu.SemaphoreType.DMA((tile_rows,)),
+            ],
+            input_output_aliases={2 + len(units): 0},
+            compiler_params=params,
+        )(mixed, awaited, *(ready[c] for c in some), result)
     return result.reshape(tile_rows, tile_cols, half, pixels)
 
 

time: 39.3 us -> 39 us (level)
  waiting for transfers between devices: 7.89 us -> 6.24 us
  Pallas kernels: 8.22 us -> 9.55 us
    pallas_call x0 -> x3, Pallas kernels: none -> 3.06 us  [the longest x1 1.53 us: on_device(): pl.pallas_call(functools.partial(mix_kernel, tile, parts, inner_units, ou...]
    pallas_call x11 -> x9, Pallas kernels: 8.22 us -> 6.49 us  [call(): pl.pallas_call(kernel, out_shape=[shape] * outputs + list(more), in_specs...]
    ppermute x12, waiting for transfers between devices: 7.28 us -> 5.64 us  [exchange(): return lax.ppermute(array, (axis, 'sub'), pairs)]
  transfers between devices with their start and end apart: 15 -> 15, of which waited for: 5 -> 5; matrix products, arithmetic and copies ran while one was open for 4% -> 4% of each run, Pallas kernels for 19% -> 23%
where the time goes in v6:
time: 39 us; the launch traced here: 38.8 us
  starting transfers between devices  20.6 us (53%)
  Pallas kernels  9.55 us (24%)
  waiting for transfers between devices  6.24 us (16%)
  local copies, waits for them, and re-layouts  1.96 us (5%)
    ppermute x12, starting transfers between devices, exchange(): return lax.ppermute(array, (axis, 'sub'), pairs)  20 us
    pallas_call x9, Pallas kernels, call(): pl.pallas_call(kernel, out_shape=[shape] * outputs + list(more), in_specs...  6.49 us
    ppermute x12, waiting for transfers between devices, exchange(): return lax.ppermute(array, (axis, 'sub'), pairs)  5.64 us
    pallas_call x1, Pallas kernels, on_device(): pl.pallas_call(functools.partial(mix_kernel, tile, parts, inner_units, ou...  1.53 us
    pallas_call x2, Pallas kernels, on_device(): pl.pallas_call(functools.partial(final_kernel, tile, units, starts[some[0...  1.53 us
    dynamic_slice x1, local copies, waits for them, and re-layouts, on_device(): lax.dynamic_slice(convergence, (start, 0, sub * half, 0), (tile.split, ti...  1.06 us
  transfers between devices with their start and end apart: 15, of which 5 were waited for; matrix products, arithmetic and copies ran while one was open for 4% of the time, Pallas kernels for 23%

profile of v6, /device:TPU:0, one launch (start us, length us, event | category | flops | bytes accessed | tf_op | source)
XLA Modules:
  0.0 38.8 jit_solution(5109026951959816041)
XLA Ops:
  0.0 0.0 copy-start.2
  0.0 0.0 copy-start.3
  0.0 0.5 %collective-permute-start.4 = (bf16[512,2048]{1,0:T(8,128)(2,1)}, bf16[512,2048]{1,0:T(8,128)(2,1)}, u32[]{:S(2)}, u32[]{:S(2)}) collective-permute-start(bf16[512,2048]{1,0:T(8,128)(2,1)} %refs_0_.1), channel_id=1, source_target_pairs={{0,1},{1,0},{2,3},{3,2},{4,5},{5,4},{6,7},{7,6},{8,9},{9,8},{10,11... | collective-permute-start | bytes 6291464 | tf_op jit(solution)/shard_map/ppermute | solution.py:31
  0.5 0.1 collective-permute-start.6
  0.5 3.0 %collective-permute-start = (s32[4,2,16]{2,1,0:T(2,128)}, s32[4,2,16]{2,1,0:T(2,128)S(1)}, u32[]{:S(2)}, u32[]{:S(2)}) collective-permute-start(s32[4,2,16]{2,1,0:T(2,128)} %bitcast.55), channel_id=1, source_target_pairs={{0,4},{1,5},{4,0},{5,1},{8,12},{9,13},{12,8},{13,9},{2,6},{3,7},{6... | collective-permute-start | bytes 1544 | tf_op jit(solution)/shard_map/ppermute | solution.py:26
  3.5 1.1 %constant_dynamic-slice_fusion = (bf16[2,16,8,512]{3,2,1,0:T(8,128)(2,1)S(1)}, bf16[2,16,8,512]{3,2,1,0:T(8,128)(2,1)S(1)}) fusion(bf16[4,16,16,512]{3,2,1,0:T(8,128)(2,1)} %param.6, s32[]{:T(128)S(6)} %select_n.31, s32[]{:T(128)S(6)} %select_n.30, s32[]{:T(128)S(6)} %select_n.29), kind=kLoop, calls=%fused_computation.17 | loop fusion | bytes 1048588 | tf_op jit(solution)/shard_map/dynamic_slice | solution.py:310
  4.6 0.1 collective-permute-start.2
  4.7 0.1 collective-permute-start.3
  4.8 0.0 copy-done.3
  4.8 0.1 fusion.4
  4.9 0.4 %collective-permute-done = s32[4,2,16]{2,1,0:T(2,128)S(1)} collective-permute-done((s32[4,2,16]{2,1,0:T(2,128)}, s32[4,2,16]{2,1,0:T(2,128)S(1)}, u32[]{:S(2)}, u32[]{:S(2)}) %collective-permute-start) | collective-permute-done | bytes 544 | tf_op jit(solution)/shard_map/ppermute | solution.py:26
  5.3 0.0 copy-done.2
  5.4 0.1 collective-permute-start.1
  5.5 0.4 %collective-permute-done.6.refs_8_ = bf16[512,1024]{1,0:T(8,128)(2,1)S(1)} collective-permute-done((bf16[512,1024]{1,0:T(8,128)(2,1)}, bf16[512,1024]{1,0:T(8,128)(2,1)S(1)}, u32[]{:S(2)}, u32[]{:S(2)}) %collective-permute-start.6) | collective-permute-done | bytes 1048608 | tf_op jit(solution)/shard_map/ppermute | solution.py:31
  5.9 0.2 collective-permute-done.4.refs_1_
  6.1 2.9 %collective-permute-start.7 = (bf16[256,512]{1,0:T(8,128)(2,1)S(1)}, bf16[256,512]{1,0:T(8,128)(2,1)S(1)}, u32[]{:S(2)}, u32[]{:S(2)}) collective-permute-start(bf16[256,512]{1,0:T(8,128)(2,1)S(1)} %bitcast.43), channel_id=1, source_target_pairs={{0,4},{1,5},{4,0},{5,1},{8,12},{9,13},{12,8},{13,9},{2,6},{3,7},{6... | collective-permute-start | bytes 786440 | tf_op jit(solution)/shard_map/ppermute | solution.py:26
  9.0 0.0 collective-permute-start.8
  9.0 0.0 collective-permute-done.1
  9.0 4.9 %collective-permute-done.2.even.refs_2_ = bf16[256,512]{1,0:T(8,128)(2,1)S(1)} collective-permute-done((bf16[256,512]{1,0:T(8,128)(2,1)S(1)}, bf16[256,512]{1,0:T(8,128)(2,1)S(1)}, u32[]{:S(2)}, u32[]{:S(2)}) %collective-permute-start.2) | collective-permute-done | bytes 262176 | tf_op jit(solution)/shard_map/ppermute | solution.py:26
  13.9 0.0 collective-permute-done.3.odd.refs_4_
  13.9 0.1 shard_map.65
  14.0 1.6 %collective-permute-start.5 = (bf16[128,512]{1,0:T(8,128)(2,1)S(1)}, bf16[128,512]{1,0:T(8,128)(2,1)S(1)}, u32[]{:S(2)}, u32[]{:S(2)}) collective-permute-start(bf16[128,512]{1,0:T(8,128)(2,1)S(1)} %shard_map.65), channel_id=1, source_target_pairs={{0,2},{1,3},{2,0},{3,1},{4,6},{5,7},{6,4},{7,5},{8,10},{9,11},{10,... | collective-permute-start | bytes 393224 | tf_op jit(solution)/shard_map/ppermute | solution.py:26
  15.6 0.1 reshape.26.ints_in
  15.7 0.1 reshape.31.ints_in
  15.7 4.1 %shard_map.64 = (bf16[384,512]{1,0:T(8,128)(2,1)S(1)}, bf16[512,2048]{1,0:T(8,128)(2,1)S(1)}, bf16[512,2048]{1,0:T(8,128)(2,1)S(1)}) custom-call(s32[4,128]{1,0:T(4,128)S(1)} %reshape.26.ints_in, bf16[256,512]{1,0:T(8,128)(2,1)S(1)} %bitcast.34, bf16[256,512]{1,0:T(8,128)(2,1)S(1)} %bitcast.45, bf16[256,512]{1,0:T(8,128)(2,1)S(1)} %collective-permute-done.2.even.refs_2_, ...), custom_call_target="tpu_custom_call" | custom-call | tf_op jit(solution)/shard_map/pallas_call | solution.py:41
  19.8 0.0 collective-permute-done.5.refs_0_
  19.8 0.0 collective-permute-done.7.refs_3_
  19.8 0.0 collective-permute-done.8.refs_5_
  19.9 0.1 collective-permute-start.9
  20.0 0.6 %collective-permute-start.10 = (bf16[192,512]{1,0:T(8,128)(2,1)S(1)}, bf16[192,512]{1,0:T(8,128)(2,1)S(1)}, u32[]{:S(2)}, u32[]{:S(2)}) collective-permute-start(bf16[192,512]{1,0:T(8,128)(2,1)S(1)} %pad_maximum_fusion.1), channel_id=1, source_target_pairs={{0,1},{1,0},{4,8},{5,9},{8,4},{9,5},{12,13},{13,12},{2,3},{3,2},{6... | collective-permute-start | bytes 589832 | tf_op jit(solution)/shard_map/ppermute | solution.py:26
  20.6 0.1 collective-permute-start.11
  20.7 0.0 copy-start
  20.7 2.2 %shard_map.66.near_out = bf16[128,512]{1,0:T(8,128)(2,1)S(1)} custom-call(s32[4,128]{1,0:T(4,128)S(1)} %reshape.26.ints_in, bf16[256,512]{1,0:T(8,128)(2,1)S(1)} %bitcast.35, bf16[256,512]{1,0:T(8,128)(2,1)S(1)} %bitcast.46, bf16[256,512]{1,0:T(8,128)(2,1)S(1)} %collective-permute-done.2.even.refs_2_, ...), custom_call_target="tpu_custom_call" | custom-call | tf_op jit(solution)/shard_map/pallas_call | solution.py:41
  22.9 0.0 collective-permute-done.9.refs_6_
  22.9 0.0 copy-done
  23.0 7.9 %collective-permute-start.13 = (bf16[192,512]{1,0:T(8,128)(2,1)S(1)}, bf16[192,512]{1,0:T(8,128)(2,1)S(1)}, u32[]{:S(2)}, u32[]{:S(2)}) collective-permute-start(bf16[192,512]{1,0:T(8,128)(2,1)S(1)} %shard_map.67), channel_id=1, source_target_pairs={{0,4},{1,5},{4,0},{5,1},{8,12},{9,13},{12,8},{13,9},{2,6},{3,7},{6... | collective-permute-start | bytes 589832 | tf_op jit(solution)/shard_map/ppermute | solution.py:26
  30.9 0.0 collective-permute-done.10.refs_6_
  30.9 2.1 %collective-permute-start.14 = (bf16[192,512]{1,0:T(8,128)(2,1)S(1)}, bf16[192,512]{1,0:T(8,128)(2,1)S(1)}, u32[]{:S(2)}, u32[]{:S(2)}) collective-permute-start(bf16[192,512]{1,0:T(8,128)(2,1)S(1)} %shard_map.68), channel_id=1, source_target_pairs={{0,4},{1,5},{4,0},{5,1},{8,12},{9,13},{12,8},{13,9},{2,6},{3,7},{6... | collective-permute-start | bytes 589832 | tf_op jit(solution)/shard_map/ppermute | solution.py:26
  33.0 0.0 collective-permute-done.11.refs_6_
  33.0 1.6 %collective-permute-start.12 = (bf16[128,512]{1,0:T(8,128)(2,1)S(1)}, bf16[128,512]{1,0:T(8,128)(2,1)S(1)}, u32[]{:S(2)}, u32[]{:S(2)}) collective-permute-start(bf16[128,512]{1,0:T(8,128)(2,1)S(1)} %shard_map.69), channel_id=1, source_target_pairs={{0,4},{1,5},{4,0},{5,1},{8,12},{9,13},{12,8},{13,9},{2,6},{3,7},{6... | collective-permute-start | bytes 393224 | tf_op jit(solution)/shard_map/ppermute | solution.py:26
  34.7 0.0 copy-start.1
  34.7 0.6 %copy-done.1 = s32[4,16]{1,0:T(4,128)S(1)} copy-done((s32[4,16]{1,0:T(4,128)S(1)}, s32[4,16]{1,0:T(4,128)}, u32[]{:S(2)}) %copy-start.1) | copy-done | bytes 280
  35.4 1.5 %shard_map.73 = (bf16[512,512]{1,0:T(8,128)(2,1)S(1)}, bf16[512,512]{1,0:T(8,128)(2,1)S(1)}, bf16[512,512]{1,0:T(8,128)(2,1)}) custom-call(s32[4,16]{1,0:T(4,128)S(1)} %copy-done.1, bf16[384,512]{1,0:T(8,128)(2,1)S(1)} %get-tuple-element.19.near_in, bf16[128,512]{1,0:T(8,128)(2,1)S(1)} %shard_map.66.near_out, bf16[192,512]{1,0:T(8,128)(2,1)S(1)} %shard_map.70.refs_0_, ...), custom_call_target="tpu_custom_call" | custom-call | tf_op jit(solution)/shard_map/pallas_call | solution.py:415
  36.9 0.0 collective-permute-done.13.refs_0_
  36.9 0.0 collective-permute-done.14.refs_1_
  36.9 0.8 %shard_map.74.refs_1_ = bf16[512,512]{1,0:T(8,128)(2,1)} custom-call(bf16[512,512]{1,0:T(8,128)(2,1)S(1)} %get-tuple-element.30.mixed, bf16[512,512]{1,0:T(8,128)(2,1)S(1)} %get-tuple-element.31.awaited, bf16[192,512]{1,0:T(8,128)(2,1)S(1)} %collective-permute-done.13.refs_0_, ...), custom_call_target="tpu_custom_call", output_to_operand_aliasing={{}: (4, {})} | custom-call | tf_op jit(solution)/shard_map/pallas_call | solution.py:429
  37.8 0.3 collective-permute-done.12.refs_0_
  38.1 0.7 %shard_map.75 = bf16[512,512]{1,0:T(8,128)(2,1)} custom-call(bf16[512,512]{1,0:T(8,128)(2,1)S(1)} %get-tuple-element.30.mixed, bf16[512,512]{1,0:T(8,128)(2,1)S(1)} %get-tuple-element.31.awaited, bf16[128,512]{1,0:T(8,128)(2,1)S(1)} %collective-permute-done.12.refs_0_, bf16[512,512]{1,0:T(8,128)(2,1)} %shard_map.74.refs_1_), custom_call_target="tpu_custom_call", output_to_operand_aliasing={{}: (3, {})} | custom-call | tf_op jit(solution)/shard_map/pallas_call | solution.py:429
  (19 shorter events, 0.3 us)
Async XLA Ops:
  0.0 5.3 %copy-start.2 = (s32[4,16,2]{1,2,0:T(2,128)S(1)}, s32[4,16,2]{1,2,0:T(2,128)}, u32[]{:S(2)}) copy-start(s32[4,16,2]{1,2,0:T(2,128)} %param.9) | copy-start | bytes 1540
  0.0 4.8 %copy-start.3 = (s32[4,16,4]{1,2,0:T(4,128)S(1)}, s32[4,16,4]{1,2,0:T(4,128)}, u32[]{:S(2)}) copy-start(s32[4,16,4]{1,2,0:T(4,128)} %param.8) | copy-start | bytes 3076
  0.0 6.1 %collective-permute-start.4 = (bf16[512,2048]{1,0:T(8,128)(2,1)}, bf16[512,2048]{1,0:T(8,128)(2,1)}, u32[]{:S(2)}, u32[]{:S(2)}) collective-permute-start(bf16[512,2048]{1,0:T(8,128)(2,1)} %refs_0_.1), channel_id=1, source_target_pairs={{0,1},{1,0},{2,3},{3,2},{4,5},{5,4},{6,7},{7,6},{8,9},{9,8},{10,11... | collective-permute-start | bytes 6291464 | tf_op jit(solution)/shard_map/ppermute | solution.py:31
  0.5 5.4 %collective-permute-start.6 = (bf16[512,1024]{1,0:T(8,128)(2,1)}, bf16[512,1024]{1,0:T(8,128)(2,1)S(1)}, u32[]{:S(2)}, u32[]{:S(2)}) collective-permute-start(bf16[512,1024]{1,0:T(8,128)(2,1)} %refs_7_.11), channel_id=1, source_target_pairs={{0,1},{1,0},{2,3},{3,2},{4,5},{5,4},{6,7},{7,6},{8,9},{9,8},{10,11... | collective-permute-start | bytes 3145736 | tf_op jit(solution)/shard_map/ppermute | solution.py:31
  0.5 4.8 %collective-permute-start = (s32[4,2,16]{2,1,0:T(2,128)}, s32[4,2,16]{2,1,0:T(2,128)S(1)}, u32[]{:S(2)}, u32[]{:S(2)}) collective-permute-start(s32[4,2,16]{2,1,0:T(2,128)} %bitcast.55), channel_id=1, source_target_pairs={{0,4},{1,5},{4,0},{5,1},{8,12},{9,13},{12,8},{13,9},{2,6},{3,7},{6... | collective-permute-start | bytes 1544 | tf_op jit(solution)/shard_map/ppermute | solution.py:26
  4.6 9.3 %collective-permute-start.2 = (bf16[256,512]{1,0:T(8,128)(2,1)S(1)}, bf16[256,512]{1,0:T(8,128)(2,1)S(1)}, u32[]{:S(2)}, u32[]{:S(2)}) collective-permute-start(bf16[256,512]{1,0:T(8,128)(2,1)S(1)} %bitcast.31), channel_id=1, source_target_pairs={{0,4},{1,5},{4,0},{5,1},{8,12},{9,13},{12,8},{13,9},{2,6},{3,7},{6... | collective-permute-start | bytes 786440 | tf_op jit(solution)/shard_map/ppermute | solution.py:26
  4.7 9.2 %collective-permute-start.3 = (bf16[256,512]{1,0:T(8,128)(2,1)S(1)}, bf16[256,512]{1,0:T(8,128)(2,1)S(1)}, u32[]{:S(2)}, u32[]{:S(2)}) collective-permute-start(bf16[256,512]{1,0:T(8,128)(2,1)S(1)} %bitcast.42), channel_id=1, source_target_pairs={{0,1},{1,0},{4,8},{5,9},{8,4},{9,5},{12,13},{13,12},{2,3},{3,2},{6... | collective-permute-start | bytes 786440 | tf_op jit(solution)/shard_map/ppermute | solution.py:26
  5.4 3.7 %collective-permute-start.1 = (s32[4,8,16]{2,1,0:T(8,128)S(1)}, s32[4,8,16]{2,1,0:T(8,128)S(1)}, u32[]{:S(2)}, u32[]{:S(2)}) collective-permute-start(s32[4,8,16]{2,1,0:T(8,128)S(1)} %fusion), channel_id=1, source_target_pairs={{0,1},{1,0},{2,3},{3,2},{4,5},{5,4},{6,7},{7,6},{8,9},{9,8},{10,11... | collective-permute-start | bytes 6152 | tf_op jit(solution)/shard_map/ppermute | solution.py:31
  6.1 13.7 %collective-permute-start.7 = (bf16[256,512]{1,0:T(8,128)(2,1)S(1)}, bf16[256,512]{1,0:T(8,128)(2,1)S(1)}, u32[]{:S(2)}, u32[]{:S(2)}) collective-permute-start(bf16[256,512]{1,0:T(8,128)(2,1)S(1)} %bitcast.43), channel_id=1, source_target_pairs={{0,4},{1,5},{4,0},{5,1},{8,12},{9,13},{12,8},{13,9},{2,6},{3,7},{6... | collective-permute-start | bytes 786440 | tf_op jit(solution)/shard_map/ppermute | solution.py:26
  9.0 10.8 %collective-permute-start.8 = (bf16[256,512]{1,0:T(8,128)(2,1)S(1)}, bf16[256,512]{1,0:T(8,128)(2,1)S(1)}, u32[]{:S(2)}, u32[]{:S(2)}) collective-permute-start(bf16[256,512]{1,0:T(8,128)(2,1)S(1)} %bitcast.32), channel_id=1, source_target_pairs={{0,1},{1,0},{4,8},{5,9},{8,4},{9,5},{12,13},{13,12},{2,3},{3,2},{6... | collective-permute-start | bytes 786440 | tf_op jit(solution)/shard_map/ppermute | solution.py:26
  14.0 5.8 %collective-permute-start.5 = (bf16[128,512]{1,0:T(8,128)(2,1)S(1)}, bf16[128,512]{1,0:T(8,128)(2,1)S(1)}, u32[]{:S(2)}, u32[]{:S(2)}) collective-permute-start(bf16[128,512]{1,0:T(8,128)(2,1)S(1)} %shard_map.65), channel_id=1, source_target_pairs={{0,2},{1,3},{2,0},{3,1},{4,6},{5,7},{6,4},{7,5},{8,10},{9,11},{10,... | collective-permute-start | bytes 393224 | tf_op jit(solution)/shard_map/ppermute | solution.py:26
  19.9 3.0 %collective-permute-start.9 = (bf16[192,512]{1,0:T(8,128)(2,1)S(1)}, bf16[192,512]{1,0:T(8,128)(2,1)S(1)}, u32[]{:S(2)}, u32[]{:S(2)}) collective-permute-start(bf16[192,512]{1,0:T(8,128)(2,1)S(1)} %pad_maximum_fusion), channel_id=1, source_target_pairs={{0,1},{1,0},{4,8},{5,9},{8,4},{9,5},{12,13},{13,12},{2,3},{3,2},{6... | collective-permute-start | bytes 589832 | tf_op jit(solution)/shard_map/ppermute | solution.py:26
  20.0 10.9 %collective-permute-start.10 = (bf16[192,512]{1,0:T(8,128)(2,1)S(1)}, bf16[192,512]{1,0:T(8,128)(2,1)S(1)}, u32[]{:S(2)}, u32[]{:S(2)}) collective-permute-start(bf16[192,512]{1,0:T(8,128)(2,1)S(1)} %pad_maximum_fusion.1), channel_id=1, source_target_pairs={{0,1},{1,0},{4,8},{5,9},{8,4},{9,5},{12,13},{13,12},{2,3},{3,2},{6... | collective-permute-start | bytes 589832 | tf_op jit(solution)/shard_map/ppermute | solution.py:26
  20.6 12.4 %collective-permute-start.11 = (bf16[128,512]{1,0:T(8,128)(2,1)S(1)}, bf16[128,512]{1,0:T(8,128)(2,1)S(1)}, u32[]{:S(2)}, u32[]{:S(2)}) collective-permute-start(bf16[128,512]{1,0:T(8,128)(2,1)S(1)} %pad_maximum_fusion.2), channel_id=1, source_target_pairs={{0,1},{1,0},{4,8},{5,9},{8,4},{9,5},{12,13},{13,12},{2,3},{3,2},{6... | collective-permute-start | bytes 393224 | tf_op jit(solution)/shard_map/ppermute | solution.py:26
  20.7 2.2 %copy-start = (bf16[512,1024]{1,0:T(8,128)(2,1)S(1)}, bf16[512,1024]{1,0:T(8,128)(2,1)}, u32[]{:S(2)}) copy-start(bf16[512,1024]{1,0:T(8,128)(2,1)} %refs_7_.11) | copy-start | bytes 3145732
  23.0 13.9 %collective-permute-start.13 = (bf16[192,512]{1,0:T(8,128)(2,1)S(1)}, bf16[192,512]{1,0:T(8,128)(2,1)S(1)}, u32[]{:S(2)}, u32[]{:S(2)}) collective-permute-start(bf16[192,512]{1,0:T(8,128)(2,1)S(1)} %shard_map.67), channel_id=1, source_target_pairs={{0,4},{1,5},{4,0},{5,1},{8,12},{9,13},{12,8},{13,9},{2,6},{3,7},{6... | collective-permute-start | bytes 589832 | tf_op jit(solution)/shard_map/ppermute | solution.py:26
  30.9 6.0 %collective-permute-start.14 = (bf16[192,512]{1,0:T(8,128)(2,1)S(1)}, bf16[192,512]{1,0:T(8,128)(2,1)S(1)}, u32[]{:S(2)}, u32[]{:S(2)}) collective-permute-start(bf16[192,512]{1,0:T(8,128)(2,1)S(1)} %shard_map.68), channel_id=1, source_target_pairs={{0,4},{1,5},{4,0},{5,1},{8,12},{9,13},{12,8},{13,9},{2,6},{3,7},{6... | collective-permute-start | bytes 589832 | tf_op jit(solution)/shard_map/ppermute | solution.py:26
  33.0 5.1 %collective-permute-start.12 = (bf16[128,512]{1,0:T(8,128)(2,1)S(1)}, bf16[128,512]{1,0:T(8,128)(2,1)S(1)}, u32[]{:S(2)}, u32[]{:S(2)}) collective-permute-start(bf16[128,512]{1,0:T(8,128)(2,1)S(1)} %shard_map.69), channel_id=1, source_target_pairs={{0,4},{1,5},{4,0},{5,1},{8,12},{9,13},{12,8},{13,9},{2,6},{3,7},{6... | collective-permute-start | bytes 393224 | tf_op jit(solution)/shard_map/ppermute | solution.py:26
  34.7 0.7 %copy-start.1 = (s32[4,16]{1,0:T(4,128)S(1)}, s32[4,16]{1,0:T(4,128)}, u32[]{:S(2)}) copy-start(s32[4,16]{1,0:T(4,128)} %level_in.1) | copy-start | bytes 772
